TPU v7x, 128 devices: a whole 4x4x4 slice. The times are simulated.
128 devices in a mesh: depth: 2 (over core), tile: 64 (over z, y, x).
Axes of the slice: x: 4, y: 4, z: 4, core: 2. Of those that a mesh axis runs over, the one named last changes fastest.
Arguments:
- transmission: bfloat16 [2, 2, 2048, 16384], P('depth', None, None, 'tile')
- chirp_taps: float32 [5], replicated, may hold values from -0.06 to 0.06
- probe_field: float32 [2, 256, 256], replicated, may hold values from -6 to 6
- records: bfloat16 [64, 2, 256, 256], P('tile'), may hold values from 0 to 2
- pos_row: int32 [64, 2], P('tile'), may hold values from 0 to 1792
- pos_col: int32 [64, 2], P('tile'), may hold values from 0 to 255
- counts: int32 [64], P('tile'), may hold values from 1 to 2, as said below
Outputs:
- gradient: bfloat16 [2, 2, 2048, 16384], P('depth', None, None, 'tile')
Inputs may be any that keep to these rules, and one draw needn't show every extreme that they name: Slots 0 to counts[t] - 1 of tile t are live; some tile has 2.
All inputs are finite; a program needn't handle non-finite values.
Results may differ from a plain program's by a relative error of at most 0.011.
Values may be sent and summed in bfloat16 or wider, within the bound.
No kernel may reach another device: no remote copies, remote signals or barrier semaphores. Data moves between devices by JAX's collectives and lax.ppermute only.
A program may use at most 64 MiB of HBM per device.

v0:
```python
import math

import jax
import jax.numpy as jnp
from jax import lax
from jax.sharding import PartitionSpec as P


def from_behind(block, axis, distance):
    devices = range(lax.axis_size(axis))
    route = [((i - distance) % len(devices), i) for i in devices]
    return lax.ppermute(block, axis, route)


def passed_along(shard, axis, by):
    devices = lax.axis_size(axis)
    pairs = [(i, i + by) for i in range(devices) if 0 <= i + by < devices]
    return lax.ppermute(shard, axis, pairs)


def spread_taps(values, chirp_taps, axis_pos):
    reach = chirp_taps.shape[0] - 1
    length = values.shape[axis_pos]
    widths = [(0, 0)] * values.ndim
    widths[axis_pos] = (reach, reach)
    padded = jnp.pad(values, widths)
    total = chirp_taps[0] * values
    for offset in range(1, reach + 1):
        upper = lax.slice_in_dim(padded, reach + offset, reach + offset + length, axis=axis_pos)
        lower = lax.slice_in_dim(padded, reach - offset, reach - offset + length, axis=axis_pos)
        total = total + chirp_taps[offset] * (upper + lower)
    return total


def propagate(wavefield, chirp_taps, sign_value):
    for axis_neg in (-1, -2):
        real_part = wavefield[..., 0, :, :]
        imag_part = wavefield[..., 1, :, :]
        axis_pos = real_part.ndim + axis_neg
        new_real = real_part - sign_value * spread_taps(imag_part, chirp_taps, axis_pos)
        new_imag = imag_part + sign_value * spread_taps(real_part, chirp_taps, axis_pos)
        wavefield = jnp.stack([new_real, new_imag], axis=-3)
    return wavefield


def complex_mul(first, second):
    ar, ai = (first[..., 0, :, :], first[..., 1, :, :])
    br, bi = (second[..., 0, :, :], second[..., 1, :, :])
    return jnp.stack([ar * br - ai * bi, ar * bi + ai * br], axis=-3)


def conj_mul(first, second):
    ar, ai = (first[..., 0, :, :], first[..., 1, :, :])
    br, bi = (second[..., 0, :, :], second[..., 1, :, :])
    return jnp.stack([ar * br + ai * bi, ar * bi - ai * br], axis=-3)


def group_forward(wavefield, windows, chirp_taps):
    incoming = [wavefield]
    wavefield = propagate(complex_mul(windows[:, 0], wavefield), chirp_taps, 1.0)
    return (wavefield, jnp.stack(incoming, axis=1))


def group_adjoint(adjoint, windows, incoming, chirp_taps):
    terms = [None] * windows.shape[1]
    for number in reversed(range(windows.shape[1])):
        pulled = propagate(adjoint, chirp_taps, -1.0)
        terms[number] = conj_mul(incoming[:, number], pulled)
        adjoint = conj_mul(windows[:, number], pulled)
    return (adjoint, jnp.stack(terms, axis=1))


def dft_tables(length):
    indices = jnp.arange(length, dtype=jnp.int32)
    product = indices[:, None] * indices[None, :] % length
    angle = product.astype(jnp.float32) * (2.0 * math.pi / length)
    factor = 1.0 / math.sqrt(length)
    return (
        (jnp.cos(angle) * factor).astype(jnp.bfloat16),
        (jnp.sin(angle) * factor).astype(jnp.bfloat16),
    )


def left_mul(matrix, values):
    return jnp.einsum("jk,bkl->bjl", matrix, values, preferred_element_type=jnp.float32)


def right_mul(values, matrix):
    return jnp.einsum("bjk,kl->bjl", values, matrix, preferred_element_type=jnp.float32)


def far_field(exit_wave, intensity, live_mask):
    cos_table, sin_table = dft_tables(exit_wave.shape[-1])
    exit_real = exit_wave[:, 0].astype(jnp.bfloat16)
    exit_imag = exit_wave[:, 1].astype(jnp.bfloat16)
    half_real = (left_mul(cos_table, exit_real) + left_mul(sin_table, exit_imag)).astype(
        jnp.bfloat16
    )
    half_imag = (left_mul(cos_table, exit_imag) - left_mul(sin_table, exit_real)).astype(
        jnp.bfloat16
    )
    far_real = right_mul(half_real, cos_table) + right_mul(half_imag, sin_table)
    far_imag = right_mul(half_imag, cos_table) - right_mul(half_real, sin_table)
    misfit = (
        far_real * far_real + far_imag * far_imag - intensity.astype(jnp.float32)
    ) * live_mask[:, None, None]
    grad_real = (misfit * far_real).astype(jnp.bfloat16)
    grad_imag = (misfit * far_imag).astype(jnp.bfloat16)
    back_real = (left_mul(cos_table, grad_real) - left_mul(sin_table, grad_imag)).astype(
        jnp.bfloat16
    )
    back_imag = (left_mul(cos_table, grad_imag) + left_mul(sin_table, grad_real)).astype(
        jnp.bfloat16
    )
    adj_real = right_mul(back_real, cos_table) - right_mul(back_imag, sin_table)
    adj_imag = right_mul(back_imag, cos_table) + right_mul(back_real, sin_table)
    return jnp.stack([adj_real, adj_imag], axis=1)


def on_device(transmission, chirp_taps, probe_field, records, pos_row, pos_col, counts):
    slices_here = transmission.shape[0]
    tile_cols = transmission.shape[3]
    side = probe_field.shape[-1]
    slots = pos_row.shape[1]
    zero_index = jnp.int32(0)
    neighbor = from_behind(transmission, "tile", -1)
    extended = jnp.concatenate([transmission, neighbor], axis=3)

    def window_at(row_start, col_start):
        return lax.dynamic_slice(
            extended, (zero_index, zero_index, row_start, col_start), (slices_here, 2, side, side)
        )

    windows = jax.vmap(window_at)(pos_row[0], pos_col[0]).astype(jnp.float32)
    live_mask = (jnp.arange(slots, dtype=jnp.int32) < counts[0]).astype(jnp.float32)
    depth_count = lax.axis_size("depth")
    my_depth = lax.axis_index("depth")
    num_blocks = slots // slots
    total_steps = depth_count + num_blocks - 1
    probe_batch = jnp.broadcast_to(probe_field, (slots, 2, side, side))
    empty_wire = jnp.zeros((slots, 2, side, side), jnp.bfloat16)
    stored_start = jnp.zeros((slots, slices_here, 2, side, side), jnp.float32)

    def remember(stored, incoming, start_row):
        return lax.dynamic_update_slice_in_dim(stored, incoming, start_row, 0)

    def advance(counter, carried):
        received, inputs, stored, exits = carried
        block_id = counter - my_depth
        active = (block_id >= 0) & (block_id < num_blocks)
        start_row = jnp.clip(block_id, 0, num_blocks - 1) * slots
        entry = jnp.where(my_depth == 0, probe_batch, received.astype(jnp.float32))

        def advance_run_group(operand):
            leaving, incoming = group_forward(entry, windows, chirp_taps)
            new_stored = remember(stored, incoming, start_row)
            return (leaving.astype(jnp.bfloat16), entry, new_stored, leaving)

        def advance_skip_group(operand):
            return (empty_wire, inputs, stored, exits)

        return lax.cond(active, advance_run_group, advance_skip_group, 0)

    def forward_step(counter, carried):
        outgoing, inputs, stored, exits = advance(counter, carried)
        received = passed_along(outgoing, "depth", 1)
        return (received, inputs, stored, exits)

    wave_zeros = jnp.zeros((slots, 2, side, side), jnp.float32)
    carried = lax.fori_loop(
        0, total_steps - 1, forward_step, (empty_wire, wave_zeros, stored_start, wave_zeros)
    )
    unused, inputs, stored, exits = advance(total_steps - 1, carried)

    def bottom_work(operand):
        return far_field(exits, records[0], live_mask)

    def bottom_skip(operand):
        return wave_zeros

    bottom = lax.cond(my_depth == depth_count - 1, bottom_work, bottom_skip, 0)

    def retreat(counter, carried):
        received, grads = carried
        block_id = counter - (depth_count - 1 - my_depth)
        active = (block_id >= 0) & (block_id < num_blocks)
        start_row = jnp.clip(block_id, 0, num_blocks - 1) * slots
        entry = jnp.where(my_depth == depth_count - 1, bottom, received.astype(jnp.float32))

        def retreat_run_group(operand):
            leaving, terms = group_adjoint(entry, windows, stored, chirp_taps)
            return (
                leaving.astype(jnp.bfloat16),
                lax.dynamic_update_slice_in_dim(grads, terms, start_row, 0),
            )

        def retreat_skip_group(operand):
            return (empty_wire, grads)

        return lax.cond(active, retreat_run_group, retreat_skip_group, 0)

    def backward_step(counter, carried):
        outgoing, grads = retreat(counter, carried)
        received = passed_along(outgoing, "depth", -1)
        return (received, grads)

    grads_start = jnp.zeros((slots, slices_here, 2, side, side), jnp.float32)
    carried = lax.fori_loop(0, total_steps - 1, backward_step, (empty_wire, grads_start))
    unused, grads = retreat(total_steps - 1, carried)
    accum = jnp.zeros((slices_here, 2, transmission.shape[2], 2 * tile_cols), jnp.float32)
    for slot in range(slots):
        corner = (zero_index, zero_index, pos_row[0, slot], pos_col[0, slot])
        current = lax.dynamic_slice(accum, corner, (slices_here, 2, side, side))
        accum = lax.dynamic_update_slice(accum, current + grads[slot], corner)
    from_left = from_behind(accum[..., tile_cols:].astype(jnp.bfloat16), "tile", 1).astype(
        jnp.float32
    )
    return (accum[..., :tile_cols] + from_left).astype(jnp.bfloat16)


def solution(mesh):
    in_specs = (
        P("depth", None, None, "tile"),
        P(),
        P(),
        P("tile", None, None, None),
        P("tile", None),
        P("tile", None),
        P("tile"),
    )
    out_specs = P("depth", None, None, "tile")
    return jax.shard_map(
        on_device, mesh=mesh, in_specs=in_specs, out_specs=out_specs, check_vma=False
    )
```

profile of v0, /device:TPU:0, one launch (start us, length us, event | category | flops | bytes accessed | tf_op | source)
XLA Modules:
  0.0 231.2 jit_solution(1249420047535563483)
XLA Ops:
  0.0 8.8 %collective-permute-start = (bf16[1,2,2048,256]{3,2,1,0:T(8,128)(2,1)}, bf16[1,2,2048,256]{3,2,1,0:T(8,128)(2,1)}, u32[]{:S(2)}, u32[]{:S(2)}) collective-permute-start(bf16[1,2,2048,256]{3,2,1,0:T(8,128)(2,1)} %param.17), channel_id=1, source_target_pairs={{1,0},{2,1},{3,2},{4,3},{5,4},{6,5},{7,6},{8,7},{9,8},{10,9},{11,1... | collective-permute-start | bytes 6291464 | tf_op jit(solution)/shard_map/ppermute | solution.py:12
  8.8 0.7 compare_select_fusion.1
  9.5 0.7 compare_select_fusion
  10.5 43.4 %collective-permute-done = bf16[1,2,2048,256]{3,2,1,0:T(8,128)(2,1)} collective-permute-done((bf16[1,2,2048,256]{3,2,1,0:T(8,128)(2,1)}, bf16[1,2,2048,256]{3,2,1,0:T(8,128)(2,1)}, u32[]{:S(2)}, u32[]{:S(2)}) %collective-permute-start) | collective-permute-done | bytes 2097184 | tf_op jit(solution)/shard_map/ppermute | solution.py:12
  54.0 4.5 %pad_maximum_fusion.5 = bf16[1,2,2048,512]{3,2,1,0:T(8,128)(2,1)} fusion(bf16[1,2,2048,256]{3,2,1,0:T(8,128)(2,1)} %collective-permute-done, bf16[1,2,2048,256]{3,2,1,0:T(8,128)(2,1)} %param.17), kind=kLoop, calls=%fused_computation.361 | loop fusion | flops 8388608 | bytes 8388608 | tf_op jit(solution)/shard_map/concatenate | solution.py:127
  58.5 6.2 %while.4 = (s32[]{:T(128)}, bf16[1,2,2048,512]{3,2,1,0:T(8,128)(2,1)}, s32[2,4]{1,0:T(2,128)S(1)}, bf16[2,1,2,256,256]{4,3,2,1,0:T(8,128)(2,1)S(1)}, s32[]{:T(128)}) while((s32[]{:T(128)}, bf16[1,2,2048,512]{3,2,1,0:T(8,128)(2,1)}, s32[2,4]{1,0:T(2,128)S(1)}, bf16[2,1,2,256,256]{4,3,2,1,0:T(8,128)(2,1)S(1)}, s32[]{:T(128)}) %tuple.131), condition=%wide.while_cond, body=%wide.while_body.sunk | while | flops 2 | bytes 524421 | solution.py:130
  58.5 0.6 fusion.264
  59.1 2.4 %bitcast_dynamic-update-slice_fusion.2 = bf16[2,1,2,256,256]{4,3,2,1,0:T(8,128)(2,1)S(1)} fusion(bf16[2,1,2,256,256]{4,3,2,1,0:T(8,128)(2,1)S(1)} %get-tuple-element.381, s32[]{:T(128)S(6)} %copy.79, bf16[1,2,2048,512]{3,2,1,0:T(8,128)(2,1)} %get-tuple-element.384, s32[]{:T(128)} %bitcast.256, s32[]{:T(128)} %bitcast.257), kind=kLoop, calls=%fused_computation.356.clone.1 | loop fusion | bytes 524300 | tf_op jit(solution)/shard_map/vmap()/gather
  61.6 0.6 fusion.264
  62.2 2.4 %bitcast_dynamic-update-slice_fusion.2 = bf16[2,1,2,256,256]{4,3,2,1,0:T(8,128)(2,1)S(1)} fusion(bf16[2,1,2,256,256]{4,3,2,1,0:T(8,128)(2,1)S(1)} %get-tuple-element.381, s32[]{:T(128)S(6)} %copy.79, bf16[1,2,2048,512]{3,2,1,0:T(8,128)(2,1)} %get-tuple-element.384, s32[]{:T(128)} %bitcast.256, s32[]{:T(128)} %bitcast.257), kind=kLoop, calls=%fused_computation.356.clone.1 | loop fusion | bytes 524300 | tf_op jit(solution)/shard_map/vmap()/gather
  64.7 0.8 copy-done.1
  65.5 1.1 convert_element_type.186
  66.6 15.9 %conditional.5 = (bf16[2,2,256,256]{3,2,0,1:T(8,128)(2,1)S(1)}, f32[2,1,2,256,256]{4,3,2,1,0:T(8,128)}, f32[2,2,256,256]{3,2,0,1:T(8,128)}) conditional(s32[]{:T(128)} %convert_element_type.189, (f32[2,1,2,256,256]{4,3,0,2,1:T(8,128)S(1)}, f32[2,2,256,256]{3,2,0,1:T(8,128)S(1)}) %tuple.62, (f32[2,1,2,256,256]{4,3,2,1,0:T(8,128)S(1)}, pred[]{:T(512)}, ...), branch_computations={%region_0.1_spmd, %region_1.2_spmd} | conditional | flops 9175040 | bytes 18874492 | solution.py:162
  66.7 0.7 fusion.243
  67.4 1.1 broadcast_select_fusion
  68.6 1.1 stack.72
  69.7 4.1 %fusion.19 = (f32[2,256,256]{2,1,0:T(8,128)S(1)}, f32[2,256,256]{2,1,0:T(8,128)S(1)}) fusion(f32[2,256,256]{2,1,0:T(8,128)S(1)} %multiply_subtract_fusion, f32[]{:T(128)} %bitcast.9, f32[]{:T(128)} %bitcast.8, f32[]{:T(128)} %bitcast.7, f32[]{:T(128)} %bitcast.6, f32[]{:T(128)} %bitcast.5, f32[256,256]{1,0:T(8,128)S(1)} %get-tuple-element.303, ...), kind=kLoop, calls=%fused_computation.37 | loop fusion | flops 2228224 | bytes 3145748 | tf_op jit(solution)/shard_map/while/body/eval_jaxpr/cond/branch_1_fun/add | solution.py:41
  73.8 4.1 %subtract_bitcast_fusion = (f32[2,1,256,256]{3,2,0,1:T(8,128)S(1)}, f32[2,256,256]{2,1,0:T(8,128)S(1)}) fusion(f32[2,256,256]{2,1,0:T(8,128)S(1)} %get-tuple-element.285, f32[]{:T(128)} %bitcast.9, f32[]{:T(128)} %bitcast.8, f32[]{:T(128)} %bitcast.7, f32[]{:T(128)} %bitcast.6, f32[]{:T(128)} %bitcast.5, f32[2,256,256]{2,1,0:T(8,128)S(1)} %get-tuple-element.286, ...), kind=kLoop, calls=%fused_computation.47 | loop fusion | flops 4063232 | bytes 3670036 | tf_op jit(solution)/shard_map/while/body/eval_jaxpr/cond/branch_1_fun/stack | solution.py:42
  77.9 3.5 %add_bitcast_fusion = f32[2,1,256,256]{3,2,0,1:T(8,128)S(1)} fusion(f32[2,256,256]{2,1,0:T(8,128)S(1)} %get-tuple-element.285, f32[2,256,256]{2,1,0:T(8,128)S(1)} %get-tuple-element.284, f32[]{:T(128)} %bitcast.9, f32[]{:T(128)} %bitcast.8, f32[]{:T(128)} %bitcast.7, f32[]{:T(128)} %bitcast.6, f32[]{:T(128)} %bitcast.5), kind=kLoop, calls=%fused_computation.46 | loop fusion | flops 1835008 | bytes 1572884 | tf_op jit(solution)/shard_map/while/body/eval_jaxpr/cond/branch_1_fun/stack | solution.py:42
  81.4 1.2 fusion.238
  82.6 0.8 copy.50
  83.4 2.1 collective-permute-start.1
  86.1 0.4 collective-permute-done.1
  86.5 1.1 convert_element_type.190
  87.7 0.9 copy-done.5
  88.6 1.1 conditional.7
  88.6 1.1 broadcast_in_dim.31
  89.7 0.8 conditional.8
  89.7 0.8 broadcast_in_dim.32
  90.5 1.3 collective-permute-start.2
  91.8 0.6 fusion.248
  95.0 0.6 fusion.247
  100.6 42.8 %collective-permute-done.2 = bf16[2,2,256,256]{3,2,0,1:T(8,128)(2,1)S(1)} collective-permute-done((bf16[2,2,256,256]{3,2,0,1:T(8,128)(2,1)}, bf16[2,2,256,256]{3,2,0,1:T(8,128)(2,1)S(1)}, u32[]{:S(2)}, u32[]{:S(2)}) %collective-permute-start.2) | collective-permute-done | bytes 524320 | tf_op jit(solution)/shard_map/while/body/eval_jaxpr/ppermute | solution.py:18
  143.6 13.0 %conditional.9 = (f32[1,2,256,256]{3,2,0,1:T(8,128)}, f32[1,2,256,256]{3,2,0,1:T(8,128)}) conditional(s32[]{:T(128)} %convert_element_type.184, f32[2,1,2,256,256]{4,3,0,2,1:T(8,128)S(1)} %get-tuple-element.219, (f32[2,1,2,256,256]{4,3,2,0,1:T(8,128)}, pred[]{:T(512)}, f32[2,2,256,256]{3,2,0,1:T(8,128)}, f32[2,2,256,256]{3,2,0,1:T(8,128)S(1)}, ...), branch_computations={%region_8.9_spmd, %region_9.10_spmd} | conditional | flops 9175040 | bytes 18874464 | solution.py:200
  143.6 0.7 fusion.246
  144.2 0.1 broadcast_select_fusion.3
  144.4 1.3 copy_bitcast_fusion.4
  145.8 5.4 %fusion.230 = (f32[2,256,256]{2,1,0:T(8,128)S(1)}, f32[2,256,256]{2,1,0:T(8,128)S(1)}) fusion(f32[2,256,256]{2,1,0:T(8,128)S(1)} %get-tuple-element.333, f32[]{:T(128)} %bitcast.67, f32[]{:T(128)} %bitcast.66, f32[]{:T(128)} %bitcast.65, f32[]{:T(128)} %bitcast.64, f32[]{:T(128)} %bitcast.62, f32[2,2,256,256]{3,2,0,1:T(8,128)S(1)} %broadcast_select_fusion.3, ...), kind=kLoop, calls=%fused_computation.339 | loop fusion | flops 3932160 | bytes 3145748 | tf_op jit(solution)/shard_map/cond/branch_1_fun/add | solution.py:41
  151.1 4.2 %subtract_bitcast_fusion.3 = (f32[2,1,256,256]{3,2,0,1:T(8,128)S(1)}, f32[2,256,256]{2,1,0:T(8,128)S(1)}, f32[2,256,256]{2,1,0:T(8,128)S(1)}) fusion(f32[2,2,256,256]{3,2,0,1:T(8,128)S(1)} %copy_bitcast_fusion.4, f32[2,256,256]{2,1,0:T(8,128)S(1)} %get-tuple-element.332, f32[]{:T(128)} %bitcast.67, f32[]{:T(128)} %bitcast.66, f32[]{:T(128)} %bitcast.65, ...), kind=kLoop, calls=%fused_computation.351 | loop fusion | flops 4325376 | bytes 3670036 | tf_op jit(solution)/shard_map/cond/branch_1_fun/stack | solution.py:55
  155.3 0.1 add_bitcast_fusion.3
  155.5 1.1 pad_maximum_fusion.4
  156.5 4.4 %broadcast_in_dim.35 = f32[1,2,2048,512]{3,2,1,0:T(8,128)} broadcast(f32[]{:T(128)} %constant.86.clone.1), dimensions={} | broadcast | bytes 8388612 | tf_op jit(solution)/shard_map/broadcast_in_dim | solution.py:210
  160.9 6.0 %dynamic_update_slice.8 = f32[1,2,2048,512]{3,2,1,0:T(8,128)} dynamic-update-slice(f32[1,2,2048,512]{3,2,1,0:T(8,128)} %broadcast_in_dim.35, f32[1,2,256,256]{3,2,1,0:T(8,128)} %bitcast.74, s32[]{:T(128)} %constant.89.clone.1, s32[]{:T(128)} %constant.89.clone.1, s32[]{:T(128)S(6)} %select_n.117, s32[]{:T(128)S(6)} %select_n.118) | dynamic-update-slice | bytes 1048580 | tf_op jit(solution)/shard_map/dynamic_update_slice | solution.py:214
  166.9 1.5 bitcast_add_fusion.1
  168.4 6.5 %dynamic_update_slice.9 = f32[1,2,2048,512]{3,2,1,0:T(8,128)} dynamic-update-slice(f32[1,2,2048,512]{3,2,1,0:T(8,128)} %dynamic_update_slice.8, f32[1,2,256,256]{3,2,1,0:T(8,128)S(1)} %bitcast_add_fusion.1, s32[]{:T(128)} %constant.89.clone.1, s32[]{:T(128)} %constant.89.clone.1, s32[]{:T(128)S(6)} %select_n.119, s32[]{:T(128)S(6)} %select_n.120) | dynamic-update-slice | bytes 1048580 | tf_op jit(solution)/shard_map/dynamic_update_slice | solution.py:214
  174.9 2.4 %slice.1412 = bf16[1,2,2048,256]{3,2,1,0:T(8,128)(2,1)S(1)} slice(f32[1,2,2048,512]{3,2,1,0:T(8,128)} %dynamic_update_slice.9), slice={[0:1], [0:2], [0:2048], [256:512]} | slice | bytes 4194304 | tf_op jit(solution)/shard_map/slice | solution.py:215
  177.4 49.7 %collective-permute-done.3 = bf16[1,2,2048,256]{3,2,1,0:T(8,128)(2,1)S(1)} collective-permute-done((bf16[1,2,2048,256]{3,2,1,0:T(8,128)(2,1)S(1)}, bf16[1,2,2048,256]{3,2,1,0:T(8,128)(2,1)S(1)}, u32[]{:S(2)}, u32[]{:S(2)}) %collective-permute-start.3) | collective-permute-done | bytes 2097184 | tf_op jit(solution)/shard_map/ppermute | solution.py:12
  227.1 4.1 %fusion.237 = bf16[1,2,2048,256]{3,2,1,0:T(8,128)(2,1)} fusion(f32[1,2,2048,512]{3,2,1,0:T(8,128)} %dynamic_update_slice.9, bf16[1,2,2048,256]{3,2,1,0:T(8,128)(2,1)S(1)} %collective-permute-done.3), kind=kLoop, calls=%fused_computation.360 | loop fusion | flops 3145728 | bytes 8388608 | tf_op jit(solution)/shard_map/convert_element_type | solution.py:218
  (26 shorter events, 0.9 us)
Async XLA Ops:
  0.0 54.0 %collective-permute-start = (bf16[1,2,2048,256]{3,2,1,0:T(8,128)(2,1)}, bf16[1,2,2048,256]{3,2,1,0:T(8,128)(2,1)}, u32[]{:S(2)}, u32[]{:S(2)}) collective-permute-start(bf16[1,2,2048,256]{3,2,1,0:T(8,128)(2,1)} %param.17), channel_id=1, source_target_pairs={{1,0},{2,1},{3,2},{4,3},{5,4},{6,5},{7,6},{8,7},{9,8},{10,9},{11,1... | collective-permute-start | bytes 6291464 | tf_op jit(solution)/shard_map/ppermute | solution.py:12
  58.5 8.2 %copy-start.2 = (f32[5]{0:T(128)S(1)}, f32[5]{0:T(128)}, u32[]{:S(2)}) copy-start(f32[5]{0:T(128)} %param.18) | copy-start | bytes 64
  64.7 0.8 copy-start.1
  83.4 3.1 %collective-permute-start.1 = (bf16[2,2,256,256]{3,2,1,0:T(8,128)(2,1)}, bf16[2,2,256,256]{3,2,1,0:T(8,128)(2,1)}, u32[]{:S(2)}, u32[]{:S(2)}) collective-permute-start(bf16[2,2,256,256]{3,2,1,0:T(8,128)(2,1)} %copy.50), channel_id=1, source_target_pairs={{0,64},{1,65},{2,66},{3,67},{4,68},{5,69},{6,70},{7,71},{8,72},{9,... | collective-permute-start | bytes 1572872 | tf_op jit(solution)/shard_map/while/body/eval_jaxpr/ppermute | solution.py:18
  87.7 1.0 copy-start.5
  89.7 2.1 copy-start.3
  89.7 5.3 %copy-start.4 = (s32[1,2]{1,0:T(1,128)S(1)}, s32[1,2]{1,0:T(1,128)}, u32[]{:S(2)}) copy-start(s32[1,2]{1,0:T(1,128)} %param.22) | copy-start | bytes 28
  90.5 52.9 %collective-permute-start.2 = (bf16[2,2,256,256]{3,2,0,1:T(8,128)(2,1)}, bf16[2,2,256,256]{3,2,0,1:T(8,128)(2,1)S(1)}, u32[]{:S(2)}, u32[]{:S(2)}) collective-permute-start(bf16[2,2,256,256]{3,2,0,1:T(8,128)(2,1)} %get-tuple-element.220), channel_id=1, source_target_pairs={{64,0},{65,1},{66,2},{67,3},{68,4},{69,5},{70,6},{71,7},{72,8},{73... | collective-permute-start | bytes 1572872 | tf_op jit(solution)/shard_map/while/body/eval_jaxpr/ppermute | solution.py:18
  177.3 49.8 %collective-permute-start.3 = (bf16[1,2,2048,256]{3,2,1,0:T(8,128)(2,1)S(1)}, bf16[1,2,2048,256]{3,2,1,0:T(8,128)(2,1)S(1)}, u32[]{:S(2)}, u32[]{:S(2)}) collective-permute-start(bf16[1,2,2048,256]{3,2,1,0:T(8,128)(2,1)S(1)} %slice.1412), channel_id=1, source_target_pairs={{63,0},{0,1},{1,2},{2,3},{3,4},{4,5},{5,6},{6,7},{7,8},{8,9},{9,10... | collective-permute-start | bytes 6291464 | tf_op jit(solution)/shard_map/ppermute | solution.py:12
where the time goes:
time: 235 us; the launch traced here: 231 us
  waiting for transfers between devices  136 us (58%)
  other arithmetic  38.8 us (17%)
  local copies, waits for them, and re-layouts  35.4 us (15%)
  starting transfers between devices  12.2 us (5%)
  between operations  8.33 us (4%)
    ppermute x2, waiting for transfers between devices, from_behind(): return lax.ppermute(block, axis, route)  93.1 us
    ppermute x2, waiting for transfers between devices, passed_along(): return lax.ppermute(shard, axis, pairs)  43.2 us
    dynamic_update_slice x2, local copies, waits for them, and re-layouts, on_device(): accum = lax.dynamic_update_slice(accum, current + grads[slot], corner)  12.5 us
    add x2, other arithmetic, propagate(): imag_part + sign_value * spread_taps(real_part, chirp_taps, axis_pos)  9.48 us
    ppermute x2, starting transfers between devices, from_behind(): return lax.ppermute(block, axis, route)  8.84 us
    another operation x2, other arithmetic, propagate(): wavefield = jnp.stack([new_real, new_imag], axis=-3)  7.59 us
    gather x6, local copies, waits for them, and re-layouts  6.19 us
    another operation x3, other arithmetic, conj_mul(): return jnp.stack([ar * br + ai * bi, ar * bi - ai * br], axis=-3)  5.38 us
  transfers between devices with their start and end apart: 4, of which 4 were waited for; matrix products, arithmetic and copies ran while one was open for 1% of the time, Pallas kernels for 0%

commit v1 on v0

v1 whole, which is shorter than its diff:
```python
import math

import jax
import jax.numpy as jnp
import numpy as np
from jax import lax
from jax.experimental import pallas as pl
from jax.experimental.pallas import tpu as pltpu
from jax.sharding import PartitionSpec as P

W = 256
STEP = 16
SPAN = W + STEP
LS = 16
RS = 8
EDGE = W - 8
BF = jnp.bfloat16
F32 = jnp.float32
ROW, COL, CNT, DEP = 0, 2, 4, 5


def dot(a, b):
    return jnp.dot(a, b, preferred_element_type=F32)


def iota(shape, dim):
    return lax.broadcasted_iota(jnp.int32, shape, dim)


def dft_tables():
    indices = np.arange(W)
    angle = (indices[:, None] * indices[None, :] % W).astype(np.float64) * (2.0 * math.pi / W)
    factor = 1.0 / math.sqrt(W)
    cos = (np.cos(angle) * factor).astype(np.float32)
    sin = (np.sin(angle) * factor).astype(np.float32)
    return np.concatenate([cos, sin], axis=0), np.concatenate([cos, sin], axis=1)


def place(meta, slot, height):
    row = meta[ROW + slot]
    base = jnp.minimum(row // STEP * STEP, height - SPAN)
    return base, row - base, meta[COL + slot]


def fold(buf, offset):
    lane = buf.shape[-1]
    top = jnp.where(iota((STEP, lane), 0) < offset, buf[W:SPAN].astype(F32), buf[0:STEP].astype(F32))
    return jnp.concatenate([top.astype(BF), buf[STEP:W]], axis=0)


def taps_table(taps, shift):
    a = (iota((W, W), 0) - shift) & (W - 1)
    b = (iota((W, W), 1) - shift) & (W - 1)
    k = jnp.abs(a - b)
    out = jnp.zeros((W, W), F32)
    for distance in range(5):
        out = jnp.where(k == distance, taps[distance], out)
    return out.astype(BF)


def propagate(re, im, t_row, t_col, sign):
    y = dot(jnp.concatenate([re.astype(BF), im.astype(BF)], axis=0), t_col)
    re, im = re - sign * y[W:], im + sign * y[:W]
    z = dot(t_row, jnp.concatenate([re.astype(BF), im.astype(BF)], axis=1))
    return re - sign * z[:, W:], im + sign * z[:, :W]


def one_hot(shift, transposed):
    m, a = (iota((W, W), 1), iota((W, W), 0)) if transposed else (iota((W, W), 0), iota((W, W), 1))
    return jnp.where(a == ((m - shift) & (W - 1)), 1.0, 0.0).astype(BF)


def rotate_probe(probe, row_shift, col_shift):
    re, im = probe[0], probe[1]
    hr, hi = re.astype(BF), im.astype(BF)
    lr, li = (re - hr.astype(F32)).astype(BF), (im - hi.astype(F32)).astype(BF)
    x = dot(one_hot(row_shift, False), jnp.concatenate([hr, hi, lr, li], axis=1)).astype(BF)
    y = jnp.concatenate([x[:, i * W : (i + 1) * W] for i in range(4)], axis=0)
    z = dot(y, one_hot(col_shift, True))
    return z[0:W] + z[2 * W : 3 * W], z[W : 2 * W] + z[3 * W :]


def forward(w0, w1, psi0, t_row, t_col):
    p1 = propagate(w0[0] * psi0[0] - w0[1] * psi0[1], w0[0] * psi0[1] + w0[1] * psi0[0], t_row, t_col, 1.0)
    p1b = (p1[0].astype(BF), p1[1].astype(BF))
    q = (p1b[0].astype(F32), p1b[1].astype(F32))
    p2 = propagate(w1[0] * q[0] - w1[1] * q[1], w1[0] * q[1] + w1[1] * q[0], t_row, t_col, 1.0)
    return p1b, (p2[0].astype(BF), p2[1].astype(BF))


def pack(parts, first, width):
    blocks = 128 // (width * len(parts))
    rows = W // blocks
    left = jnp.concatenate(
        [part[b * rows : (b + 1) * rows] for b in range(blocks) for part in parts], axis=1
    )
    q = iota((left.shape[1], 128), 0)
    lane = iota((left.shape[1], 128), 1)
    col = (q & 127) - first
    hit = (col >= 0) & (col < width) & (lane == (q // 128) * width + col)
    return dot(left, jnp.where(hit, 1.0, 0.0).astype(BF)).astype(BF)


def unpack(packed, count, first, width):
    blocks = 128 // (width * count)
    n = blocks * count * 128
    q = iota((128, n), 1)
    lane = iota((128, n), 0)
    col = (q & 127) - first
    hit = (col >= 0) & (col < width) & (lane == (q // 128) * width + col)
    out = dot(packed, jnp.where(hit, 1.0, 0.0).astype(BF)).astype(BF)
    return [
        jnp.concatenate(
            [out[:, (b * count + i) * 128 : (b * count + i + 1) * 128] for b in range(blocks)], axis=0
        )
        for i in range(count)
    ]


def span_copy(tile, base, buf, sem):
    return pltpu.make_async_copy(tile.at[0, :, pl.ds(base, SPAN), :], buf, sem)


def left_windows(meta, tile, keep, send, strip_keep, strip_send, buf, sems):
    height = tile.shape[2]
    mine = meta[DEP]
    copies = []
    for k, slot in enumerate((mine, 1 - mine)):
        base, _, _ = place(meta, slot, height)
        copy = span_copy(tile, pl.multiple_of(base, STEP), buf.at[k], sems.at[k])
        copy.start()
        copies.append(copy)
    for k, (slot, out, strip) in enumerate(((1 - mine, send, strip_send), (mine, keep, strip_keep))):
        copies[1 - k].wait()
        _, offset, _ = place(meta, slot, height)
        parts = []
        for i in range(2):
            window = fold(buf[1 - k, i], offset)
            out[i] = window
            parts.append(window[:, W - 128 :])
        strip[...] = pack(parts, 128 - LS, LS)


def pair(own, other, mine):
    first = jnp.where(mine == 0, own, other)
    second = jnp.where(mine == 0, other, own)
    return first, second


def left_forward(meta, taps, keep, recv, probe, exit_ref, psi0_ref, t_row_ref, t_col_ref):
    mine = meta[DEP]
    _, offset, col0 = place(meta, mine, meta[DEP + 1])
    t_row, t_col = taps_table(taps, offset), taps_table(taps, col0)
    t_row_ref[...], t_col_ref[...] = t_row, t_col
    psi0 = rotate_probe(probe, offset, col0)
    psi0_ref[0], psi0_ref[1] = psi0
    inside = iota((W, W), 1) >= col0
    own = [jnp.where(inside, keep[i].astype(F32), 0.0) for i in range(2)]
    other = [jnp.where(inside, recv[i].astype(F32), 0.0) for i in range(2)]
    re, im = pair(own[0], other[0], mine), pair(own[1], other[1], mine)
    _, psi2 = forward((re[0], im[0]), (re[1], im[1]), psi0, t_row, t_col)
    exit_ref[0], exit_ref[1] = psi2


def right_forward(
    meta, taps, tile, tile_other, strip_a, strip_b, probe,
    exit_ref, strip_out, w_ref, psi0_ref, psi1_ref, t_row_ref, t_col_ref, buf, sems,
):
    mine = meta[DEP]
    base, offset, col0 = place(meta, mine, tile.shape[2])
    base = pl.multiple_of(base, STEP)
    copies = [
        span_copy(tile, base, buf.at[mine], sems.at[0]),
        span_copy(tile_other, base, buf.at[1 - mine], sems.at[1]),
    ]
    for copy in copies:
        copy.start()
    t_row, t_col = taps_table(taps, offset), taps_table(taps, col0)
    t_row_ref[...], t_col_ref[...] = t_row, t_col
    psi0 = rotate_probe(probe, offset, col0)
    psi0_ref[0], psi0_ref[1] = psi0
    lane = iota((W, 128), 1)
    strips = pair(strip_a[...].astype(F32), strip_b[...].astype(F32), mine)
    for copy in copies:
        copy.wait()
    windows, heads = [], []
    for s in range(2):
        left = unpack(strips[s].astype(BF), 2, 128 - LS, LS)
        for i in range(2):
            window = fold(buf[s, i], offset)
            heads.append(window[:, :128])
            w_ref[s, i, :, :128] = jnp.where(lane < col0, window[:, :128].astype(F32), 0.0).astype(BF)
            w_ref[s, i, :, 128:] = jnp.where(
                lane + 128 < col0, window[:, 128:].astype(F32), left[i].astype(F32)
            ).astype(BF)
            windows.append(w_ref[s, i].astype(F32))
    strip_out[...] = pack(heads, 0, RS)
    psi1, psi2 = forward(windows[0:2], windows[2:4], psi0, t_row, t_col)
    psi1_ref[0], psi1_ref[1] = psi1
    exit_ref[0], exit_ref[1] = psi2


def left_merge(meta, keep, recv, strip, psi0, t_row, t_col, w_ref, psi1_ref):
    mine = meta[DEP]
    _, _, col0 = place(meta, mine, meta[DEP + 1])
    heads = unpack(strip[...], 4, 0, RS)
    lane = iota((W, 128), 1)
    for i in range(2):
        parts = pair(keep[i].astype(F32), recv[i].astype(F32), mine)
        for s in range(2):
            w_ref[s, i, :, :128] = jnp.where(lane >= col0, parts[s][:, :128], heads[s * 2 + i].astype(F32)).astype(BF)
            w_ref[s, i, :, 128:] = jnp.where(lane + 128 >= col0, parts[s][:, 128:], 0.0).astype(BF)
    w = (w_ref[0, 0].astype(F32), w_ref[0, 1].astype(F32))
    p1 = propagate(
        w[0] * psi0[0] - w[1] * psi0[1], w[0] * psi0[1] + w[1] * psi0[0], t_row[...], t_col[...], 1.0
    )
    psi1_ref[0], psi1_ref[1] = p1[0].astype(BF), p1[1].astype(BF)


def rotated_tables(meta, tall, wide, f_row, f_col_t, f_row_t, f_col):
    _, offset, col0 = place(meta, meta[DEP], meta[DEP + 1])
    f_row[...] = dot(one_hot(offset, False), wide[...]).astype(BF)
    x = dot(tall[...], one_hot(offset, True)).astype(BF)
    f_row_t[:, :W], f_row_t[:, W:] = x[:W], x[W:]
    f_col_t[...] = dot(tall[...], one_hot(col0, True)).astype(BF)
    y = dot(one_hot(col0, False), wide[...]).astype(BF)
    f_col[:W], f_col[W:] = y[:, :W], y[:, W:]


def far_field(side, meta, exit_l, exit_r, record, f_row, f_col_t, f_row_t, f_col, w, psi0, psi1, t_row, t_col, keep, send):
    mine = meta[DEP]
    _, _, col0 = place(meta, mine, meta[DEP + 1])
    live = jnp.where(mine < meta[CNT], 1.0, 0.0)
    column = iota((W, W), 1)
    left = (column >= col0) & (column < EDGE)
    er = jnp.where(left, exit_l[0].astype(F32), exit_r[0].astype(F32))
    ei = jnp.where(left, exit_l[1].astype(F32), exit_r[1].astype(F32))
    rhs = jnp.concatenate(
        [jnp.concatenate([er, ei], axis=1), jnp.concatenate([ei, -er], axis=1)], axis=0
    ).astype(BF)
    a = dot(f_row_t[...], rhs)
    ar, ai = a[:, :W], a[:, W:]
    lhs = jnp.concatenate(
        [jnp.concatenate([ar, ai], axis=1), jnp.concatenate([ai, -ar], axis=1)], axis=0
    ).astype(BF)
    far = dot(lhs, f_col[...])
    fr, fi = far[:W], far[W:]
    misfit = (fr * fr + fi * fi - record[...].astype(F32)) * live
    gr, gi = misfit * fr, misfit * fi
    rhs = jnp.concatenate(
        [jnp.concatenate([gr, gi], axis=1), jnp.concatenate([-gi, gr], axis=1)], axis=0
    ).astype(BF)
    b = dot(f_row[...], rhs)
    br, bi = b[:, :W], b[:, W:]
    lhs = jnp.concatenate(
        [jnp.concatenate([br, -bi], axis=1), jnp.concatenate([bi, br], axis=1)], axis=0
    ).astype(BF)
    chi = dot(lhs, f_col_t[...])
    q1 = propagate(chi[:W], chi[W:], t_row[...], t_col[...], -1.0)
    region = (column >= col0) if side == 0 else (column < col0)

    def term(psi_r, psi_i, q):
        return (
            jnp.where(region, psi_r * q[0] + psi_i * q[1], 0.0),
            jnp.where(region, psi_r * q[1] - psi_i * q[0], 0.0),
        )

    term1 = term(psi1[0].astype(F32), psi1[1].astype(F32), q1)
    wr, wi = w[1, 0].astype(F32), w[1, 1].astype(F32)
    cr = (wr * q1[0] + wi * q1[1]).astype(BF).astype(F32)
    ci = (wr * q1[1] - wi * q1[0]).astype(BF).astype(F32)
    q0 = propagate(cr, ci, t_row[...], t_col[...], -1.0)
    term0 = term(psi0[0], psi0[1], q0)
    for i in range(2):
        first, second = pair(term0[i], term1[i], mine)
        keep[i], send[i] = first.astype(BF), second.astype(BF)


def assemble(meta, meta_left, l_keep, l_recv, r_keep, r_recv, out):
    height = out.shape[2]
    out[...] = jnp.zeros(out.shape, BF)
    mine = meta[DEP]
    for where, slot, term in (
        (meta_left, mine, r_keep),
        (meta_left, 1 - mine, r_recv),
        (meta, mine, l_keep),
        (meta, 1 - mine, l_recv),
    ):
        base, offset, _ = place(where, slot, height)
        base = pl.multiple_of(base, STEP)
        mask = iota((STEP, W), 0) >= offset
        for i in range(2):
            top = term[i, 0:STEP].astype(F32)
            rows = pl.ds(base, STEP)
            out[0, i, rows, :] = (out[0, i, rows, :].astype(F32) + jnp.where(mask, top, 0.0)).astype(BF)
            rows = pl.ds(pl.multiple_of(base + STEP, STEP), W - STEP)
            out[0, i, rows, :] = (out[0, i, rows, :].astype(F32) + term[i, STEP:W].astype(F32)).astype(BF)
            rows = pl.ds(pl.multiple_of(base + W, STEP), STEP)
            out[0, i, rows, :] = (out[0, i, rows, :].astype(F32) + jnp.where(mask, 0.0, top)).astype(BF)


SMEM = pl.BlockSpec(memory_space=pltpu.SMEM)
VMEM = pl.BlockSpec(memory_space=pltpu.VMEM)
ANY = pl.BlockSpec(memory_space=pl.ANY)


def call(kernel, name, specs, outs, args, scratch=(), flops=0):
    outs = [jax.ShapeDtypeStruct(shape, kind) for shape, kind in outs]
    moved = sum(math.prod(o.shape) * o.dtype.itemsize for o in outs)
    moved += sum(math.prod(a.shape) * a.dtype.itemsize for a, s in zip(args, specs) if s is not ANY)
    return pl.pallas_call(
        kernel,
        name=name,
        out_shape=outs,
        in_specs=list(specs),
        out_specs=[VMEM] * len(outs),
        scratch_shapes=list(scratch),
        compiler_params=pltpu.CompilerParams(vmem_limit_bytes=40 * 1024 * 1024),
        cost_estimate=pl.CostEstimate(flops=flops, bytes_accessed=moved, transcendentals=0),
    )(*args)


def on_device(transmission, chirp_taps, probe_field, records, pos_row, pos_col, counts):
    height = transmission.shape[2]
    tiles = lax.axis_size("tile")
    my_depth = lax.axis_index("depth").astype(jnp.int32)

    def to_right(x):
        return lax.ppermute(x, "tile", [(i, (i + 1) % tiles) for i in range(tiles)])

    def to_left(x):
        return lax.ppermute(x, "tile", [(i, (i - 1) % tiles) for i in range(tiles)])

    def to_right_other(x):
        pairs = [(d * tiles + i, (1 - d) * tiles + (i + 1) % tiles) for d in range(2) for i in range(tiles)]
        return lax.ppermute(x, ("depth", "tile"), pairs)

    def to_other(x):
        return lax.ppermute(x, "depth", [(0, 1), (1, 0)])

    meta = jnp.concatenate(
        [pos_row[0], pos_col[0], counts, my_depth[None], jnp.full((1,), height, jnp.int32)]
    )
    meta_left = to_right(meta)
    field, strip, table = ((2, W, W), BF), ((W // 4, 128), BF), ((W, 2 * W), BF)
    tall_table, taps_shape, wave = ((2 * W, W), BF), ((W, W), BF), ((2, W, W), F32)
    windows = ((2, 2, W, W), BF)
    spans = [pltpu.VMEM((2, 2, SPAN, W), BF), pltpu.SemaphoreType.DMA((2,))]

    keep, send, strip_keep, strip_send = call(
        left_windows, "left_windows", [SMEM, ANY], [field, field, strip, strip], [meta, transmission], spans
    )
    strip_a = to_right(strip_keep)
    strip_b = to_right_other(strip_send)
    recv = to_other(send)
    record = lax.dynamic_index_in_dim(records[0], my_depth, 0, keepdims=False)
    record_left = to_right(record)
    other_tile = to_other(transmission)
    tall, wide = dft_tables()
    tall, wide = jnp.asarray(tall, BF), jnp.asarray(wide, BF)

    exit_l, psi0, t_row, t_col = call(
        left_forward, "left_forward", [SMEM, SMEM, VMEM, VMEM, VMEM],
        [field, wave, taps_shape, taps_shape], [meta, chirp_taps, keep, recv, probe_field], flops=10**9,
    )
    exit_l_left = to_right(exit_l)
    exit_r_left, strip_r_left, w_left, psi0_left, psi1_left, t_row_left, t_col_left = call(
        right_forward, "right_forward", [SMEM, SMEM, ANY, ANY, VMEM, VMEM, VMEM],
        [field, strip, windows, wave, field, taps_shape, taps_shape],
        [meta_left, chirp_taps, transmission, other_tile, strip_a, strip_b, probe_field], spans, flops=10**9,
    )
    strip_r = to_left(strip_r_left)
    exit_r = to_left(exit_r_left)
    tables = call(
        rotated_tables, "tables", [SMEM, VMEM, VMEM], [table, taps_shape_tall(), table, tall_table],
        [meta, tall, wide], flops=3 * 10**8,
    )
    tables_left = call(
        rotated_tables, "tables_left", [SMEM, VMEM, VMEM], [table, taps_shape_tall(), table, tall_table],
        [meta_left, tall, wide], flops=3 * 10**8,
    )
    w, psi1 = call(
        left_merge, "left_merge", [SMEM] + [VMEM] * 6, [windows, field],
        [meta, keep, recv, strip_r, psi0, t_row, t_col], flops=3 * 10**8,
    )

    def terms(side, *args):
        def kernel(*refs):
            far_field(side, *refs)

        return call(kernel, f"far_field_{side}", [SMEM] + [VMEM] * (len(args) - 1), [field, field], args, flops=10**9)

    r_keep, r_send = terms(
        1, meta_left, exit_l_left, exit_r_left, record_left, *tables_left,
        w_left, psi0_left, psi1_left, t_row_left, t_col_left,
    )
    r_recv = to_other(r_send)
    l_keep, l_send = terms(0, meta, exit_l, exit_r, record, *tables, w, psi0, psi1, t_row, t_col)
    l_recv = to_other(l_send)
    return call(
        assemble, "assemble", [SMEM, SMEM] + [VMEM] * 4, [(transmission.shape, BF)],
        [meta, meta_left, l_keep, l_recv, r_keep, r_recv],
    )[0]


def taps_shape_tall():
    return ((2 * W, W), BF)


def solution(mesh):
    in_specs = (
        P("depth", None, None, "tile"),
        P(),
        P(),
        P("tile", None, None, None),
        P("tile", None),
        P("tile", None),
        P("tile"),
    )
    out_specs = P("depth", None, None, "tile")
    return jax.shard_map(
        on_device, mesh=mesh, in_specs=in_specs, out_specs=out_specs, check_vma=False
    )
```

time: 235 us -> 45.9 us (0.20)
  the two profiles are of different devices: /device:TPU:0 before, /device:TPU:1 now
where the time goes in v1:
time: 45.9 us; the launch traced here: 45.7 us
  Pallas kernels  18.3 us (40%)
  starting transfers between devices  17.9 us (39%)
  waiting for transfers between devices  6.34 us (14%)
  local copies, waits for them, and re-layouts  2.38 us (5%)
  between operations  0.79 us (2%)
    pallas_call x9, Pallas kernels, call(): pl.pallas_call(kernel, name=name, out_shape=outs, in_specs=list(specs), o...  18.3 us
    ppermute x2, starting transfers between devices, to_left(): return lax.ppermute(x, 'tile', [(i, (i - 1) % tiles) for i in range(tiles)])  9.44 us
    ppermute x4, starting transfers between devices, to_right(): return lax.ppermute(x, 'tile', [(i, (i + 1) % tiles) for i in range(tiles)])  3.88 us
    ppermute x4, waiting for transfers between devices, to_right(): return lax.ppermute(x, 'tile', [(i, (i + 1) % tiles) for i in range(tiles)])  3.42 us
    ppermute x4, starting transfers between devices, to_other(): return lax.ppermute(x, 'depth', [(0, 1), (1, 0)])  2.78 us
    ppermute x1, starting transfers between devices, to_right_other(): return lax.ppermute(x, ('depth', 'tile'), pairs)  1.79 us
    unnamed x14, local copies, waits for them, and re-layouts  1.62 us
    ppermute x4, waiting for transfers between devices, to_other(): return lax.ppermute(x, 'depth', [(0, 1), (1, 0)])  1.51 us
  transfers between devices with their start and end apart: 11, of which 5 were waited for; matrix products, arithmetic and copies ran while one was open for 2% of the time, Pallas kernels for 35%

profile of v1, /device:TPU:1, one launch (start us, length us, event | category | flops | bytes accessed | tf_op | source)
XLA Modules:
  0.0 45.7 jit_solution(685824275119628848)
XLA Ops:
  0.0 0.0 copy-start
  0.0 0.0 copy-start.4
  0.0 1.4 %collective-permute-start.2 = (bf16[1,2,2048,256]{3,2,1,0:T(8,128)(2,1)}, bf16[1,2,2048,256]{3,2,1,0:T(8,128)(2,1)}, u32[]{:S(2)}, u32[]{:S(2)}) collective-permute-start(bf16[1,2,2048,256]{3,2,1,0:T(8,128)(2,1)} %tile.3), channel_id=1, source_target_pairs={{0,64},{64,0},{1,65},{65,1},{2,66},{66,2},{3,67},{67,3},{4,68},{68... | collective-permute-start | bytes 6291464 | tf_op jit(solution)/shard_map/ppermute | solution.py:339
  2.1 0.7 %concatenate.3.meta.refs_0_ = s32[7]{0:T(128)S(1)} concatenate(s32[2]{0:T(128)} %bitcast.5, s32[2]{0:T(128)} %bitcast.6, s32[1]{0:T(128)S(6)} %copy.10, s32[1]{0:T(128)} %bitcast.2, s32[1]{0:T(128)} %constant.16.clone.1), dimensions={0} | concatenate | bytes 56 | tf_op jit(solution)/shard_map/concatenate | solution.py:341
  2.8 0.0 copy-start.1
  2.8 1.6 %copy-done.1 = bf16[1,2,2048,256]{3,2,1,0:T(8,128)(2,1)S(1)} copy-done((bf16[1,2,2048,256]{3,2,1,0:T(8,128)(2,1)S(1)}, bf16[1,2,2048,256]{3,2,1,0:T(8,128)(2,1)}, u32[]{:S(2)}) %copy-start.1) | copy-done | bytes 2097176
  4.4 0.0 copy-start.3
  4.4 1.6 %left_windows.1 = (bf16[2,256,256]{2,1,0:T(8,128)(2,1)S(1)}, bf16[2,256,256]{2,1,0:T(8,128)(2,1)}, bf16[64,128]{1,0:T(8,128)(2,1)S(1)}, bf16[64,128]{1,0:T(8,128)(2,1)S(1)}) custom-call(s32[7]{0:T(128)S(1)} %concatenate.3.meta.refs_0_, bf16[1,2,2048,256]{3,2,1,0:T(8,128)(2,1)S(1)} %copy-done.1), custom_call_target="tpu_custom_call" | custom-call | bytes 557084 | tf_op jit(solution)/shard_map/left_windows/pallas_call | solution.py:311
  6.0 0.0 copy-start.2
  6.0 0.1 collective-permute-start.1
  6.1 1.3 %collective-permute-start = (s32[7]{0:T(128)S(1)}, s32[7]{0:T(128)S(1)}, u32[]{:S(2)}, u32[]{:S(2)}) collective-permute-start(s32[7]{0:T(128)S(1)} %concatenate.3.meta.refs_0_), channel_id=1, source_target_pairs={{0,1},{1,2},{2,3},{3,4},{4,5},{5,6},{6,7},{7,8},{8,9},{9,10},{10,1... | collective-permute-start | bytes 92 | tf_op jit(solution)/shard_map/ppermute | solution.py:329
  7.5 1.2 %collective-permute-start.3 = (bf16[64,128]{1,0:T(8,128)(2,1)S(1)}, bf16[64,128]{1,0:T(8,128)(2,1)S(1)}, u32[]{:S(2)}, u32[]{:S(2)}) collective-permute-start(bf16[64,128]{1,0:T(8,128)(2,1)S(1)} %get-tuple-element.37), channel_id=1, source_target_pairs={{0,1},{1,2},{2,3},{3,4},{4,5},{5,6},{6,7},{7,8},{8,9},{9,10},{10,1... | collective-permute-start | bytes 49160 | tf_op jit(solution)/shard_map/ppermute | solution.py:329
  8.7 1.8 %collective-permute-start.4 = (bf16[64,128]{1,0:T(8,128)(2,1)S(1)}, bf16[64,128]{1,0:T(8,128)(2,1)S(1)}, u32[]{:S(2)}, u32[]{:S(2)}) collective-permute-start(bf16[64,128]{1,0:T(8,128)(2,1)S(1)} %get-tuple-element.38), channel_id=1, source_target_pairs={{0,65},{1,66},{2,67},{3,68},{4,69},{5,70},{6,71},{7,72},{8,73},{9,... | collective-permute-start | bytes 49160 | tf_op jit(solution)/shard_map/ppermute | solution.py:336
  10.5 0.0 collective-permute-done.1.recv
  10.5 0.0 copy-done.4
  10.5 0.0 copy-done.3
  10.5 2.2 %left_forward.1 = (bf16[2,256,256]{2,1,0:T(8,128)(2,1)S(1)}, f32[2,256,256]{2,1,0:T(8,128)S(1)}, bf16[256,256]{1,0:T(8,128)(2,1)S(1)}, bf16[256,256]{1,0:T(8,128)(2,1)S(1)}) custom-call(s32[7]{0:T(128)S(1)} %concatenate.3.meta.refs_0_, f32[5]{0:T(128)S(1)} %copy-done.4, bf16[2,256,256]{2,1,0:T(8,128)(2,1)S(1)} %get-tuple-element.34.keep, ...), custom_call_target="tpu_custom_call" | custom-call | flops 1000000000 | bytes 2097200 | tf_op jit(solution)/shard_map/left_forward/pallas_call | solution.py:311
  12.7 0.0 copy-start.5
  12.7 0.0 copy-start.6
  12.7 1.3 %collective-permute-start.8 = (bf16[2,256,256]{2,1,0:T(8,128)(2,1)S(1)}, bf16[2,256,256]{2,1,0:T(8,128)(2,1)S(1)}, u32[]{:S(2)}, u32[]{:S(2)}) collective-permute-start(bf16[2,256,256]{2,1,0:T(8,128)(2,1)S(1)} %get-tuple-element.36.refs_1_), channel_id=1, source_target_pairs={{0,1},{1,2},{2,3},{3,4},{4,5},{5,6},{6,7},{7,8},{8,9},{9,10},{10,1... | collective-permute-start | bytes 786440 | tf_op jit(solution)/shard_map/ppermute | solution.py:329
  14.0 1.6 %collective-permute-done.meta.refs_0_.meta_left = s32[7]{0:T(128)S(1)} collective-permute-done((s32[7]{0:T(128)S(1)}, s32[7]{0:T(128)S(1)}, u32[]{:S(2)}, u32[]{:S(2)}) %collective-permute-start) | collective-permute-done | bytes 60 | tf_op jit(solution)/shard_map/ppermute | solution.py:329
  15.6 0.3 collective-permute-done.3.strip_a
  15.9 1.4 %collective-permute-done.4.strip_b = bf16[64,128]{1,0:T(8,128)(2,1)S(1)} collective-permute-done((bf16[64,128]{1,0:T(8,128)(2,1)S(1)}, bf16[64,128]{1,0:T(8,128)(2,1)S(1)}, u32[]{:S(2)}, u32[]{:S(2)}) %collective-permute-start.4) | collective-permute-done | bytes 16416 | tf_op jit(solution)/shard_map/ppermute | solution.py:336
  17.3 0.0 collective-permute-done.2.tile_other
  17.3 0.0 copy-done.2
  17.3 3.1 %right_forward.1 = (bf16[2,256,256]{2,1,0:T(8,128)(2,1)S(1)}, bf16[64,128]{1,0:T(8,128)(2,1)S(1)}, bf16[2,2,256,256]{3,2,1,0:T(8,128)(2,1)S(1)}, f32[2,256,256]{...) custom-call(s32[7]{0:T(128)S(1)} %collective-permute-done.meta.refs_, ...), custom_call_target="tpu_custom_call" | custom-call | flops 1000000000 | bytes 2408496 | tf_op jit(solution)/shard_map/right_forward/pallas_call | solution.py:311
  20.4 2.5 %collective-permute-start.5 = (bf16[2,256,256]{2,1,0:T(8,128)(2,1)S(1)}, bf16[2,256,256]{2,1,0:T(8,128)(2,1)S(1)}, u32[]{:S(2)}, u32[]{:S(2)}) collective-permute-start(bf16[2,256,256]{2,1,0:T(8,128)(2,1)S(1)} %get-tuple-element.39.refs_2_), channel_id=1, source_target_pairs={{0,63},{1,0},{2,1},{3,2},{4,3},{5,4},{6,5},{7,6},{8,7},{9,8},{10,9... | collective-permute-start | bytes 786440 | tf_op jit(solution)/shard_map/ppermute | solution.py:332
  22.9 0.0 copy-done
  22.9 0.1 collective-permute-start.9
  23.0 0.0 copy-done.5
  23.0 0.0 copy-done.6
  23.0 1.0 %tables.1 = (bf16[256,512]{1,0:T(8,128)(2,1)S(1)}, bf16[512,256]{1,0:T(8,128)(2,1)S(1)}, bf16[256,512]{1,0:T(8,128)(2,1)S(1)}, bf16[512,256]{1,0:T(8,128)(2,1)S(1)}) custom-call(s32[7]{0:T(128)S(1)} %concatenate.3.meta.refs_0_, bf16[512,256]{1,0:T(8,128)(2,1)S(1)} %copy-done.5, bf16[256,512]{1,0:T(8,128)(2,1)S(1)} %copy-done.6), custom_call_target="tpu_custom_call" | custom-call | flops 300000000 | bytes 1572892 | tf_op jit(solution)/shard_map/tables/pallas_call | solution.py:311
  24.0 1.0 %tables_left.1 = (bf16[256,512]{1,0:T(8,128)(2,1)S(1)}, bf16[512,256]{1,0:T(8,128)(2,1)S(1)}, bf16[256,512]{1,0:T(8,128)(2,1)S(1)}, bf16[512,256]{1,0:T(8,128)(2,1)S(1)}) custom-call(s32[7]{0:T(128)S(1)} %collective-permute-done.meta.refs_0_.meta_left, bf16[512,256]{1,0:T(8,128)(2,1)S(1)} %copy-done.5, bf16[256,512]{1,0:T(8,128)(2,1)S(1)} %copy-done.6), custom_call_target="tpu_custom_call" | custom-call | flops 300000000 | bytes 1572892 | tf_op jit(solution)/shard_map/tables_left/pallas_call | solution.py:311
  25.0 6.9 %collective-permute-start.6 = (bf16[64,128]{1,0:T(8,128)(2,1)S(1)}, bf16[64,128]{1,0:T(8,128)(2,1)S(1)}, u32[]{:S(2)}, u32[]{:S(2)}) collective-permute-start(bf16[64,128]{1,0:T(8,128)(2,1)S(1)} %get-tuple-element.44), channel_id=1, source_target_pairs={{0,63},{1,0},{2,1},{3,2},{4,3},{5,4},{6,5},{7,6},{8,7},{9,8},{10,9... | collective-permute-start | bytes 49160 | tf_op jit(solution)/shard_map/ppermute | solution.py:332
  31.9 1.5 %collective-permute-done.9.refs_3_ = bf16[256,256]{1,0:T(8,128)(2,1)S(1)} collective-permute-done((bf16[256,256]{1,0:T(8,128)(2,1)S(1)}, bf16[256,256]{1,0:T(8,128)(2,1)S(1)}, u32[]{:S(2)}, u32[]{:S(2)}) %collective-permute-start.9) | collective-permute-done | bytes 131104 | tf_op jit(solution)/shard_map/ppermute | solution.py:329
  33.5 0.0 collective-permute-done.8.refs_1_
  33.5 2.9 %far_field_1.1 = (bf16[2,256,256]{2,1,0:T(8,128)(2,1)S(1)}, bf16[2,256,256]{2,1,0:T(8,128)(2,1)S(1)}) custom-call(s32[7]{0:T(128)S(1)} %collective-permute-done.meta.refs_0_.meta_left, bf16[2,256,256]{2,1,0:T(8,128)(2,1)S(1)} %collective-permute-done.8.refs_1_, bf16[2,256,256]{2,1,0:T(8,128)(2,1)S(1)} %get-tuple-element.39.refs_2_, ...), custom_call_target="tpu_custom_call" | custom-call | flops 1000000000 | bytes 3801116 | tf_op jit(solution)/shard_map/far_field_1/pallas_call | solution.py:311
  36.4 1.1 %collective-permute-start.10 = (bf16[2,256,256]{2,1,0:T(8,128)(2,1)S(1)}, bf16[2,256,256]{2,1,0:T(8,128)(2,1)S(1)}, u32[]{:S(2)}, u32[]{:S(2)}) collective-permute-start(bf16[2,256,256]{2,1,0:T(8,128)(2,1)S(1)} %get-tuple-element.62), channel_id=1, source_target_pairs={{0,64},{64,0},{1,65},{65,1},{2,66},{66,2},{3,67},{67,3},{4,68},{68... | collective-permute-start | bytes 786440 | tf_op jit(solution)/shard_map/ppermute | solution.py:339
  37.5 0.0 collective-permute-done.6.strip
  37.5 1.3 %left_merge.1 = (bf16[2,2,256,256]{3,2,1,0:T(8,128)(2,1)S(1)}, bf16[2,256,256]{2,1,0:T(8,128)(2,1)S(1)}) custom-call(s32[7]{0:T(128)S(1)} %concatenate.3.meta.refs_0_, bf16[2,256,256]{2,1,0:T(8,128)(2,1)S(1)} %get-tuple-element.34.keep, bf16[2,256,256]{2,1,0:T(8,128)(2,1)S(1)} %collective-permute-done.1.recv, ...), custom_call_target="tpu_custom_call" | custom-call | flops 300000000 | bytes 2113564 | tf_op jit(solution)/shard_map/left_merge/pallas_call | solution.py:311
  38.8 0.0 collective-permute-done.5.refs_2_
  38.8 2.9 %far_field_0.1 = (bf16[2,256,256]{2,1,0:T(8,128)(2,1)S(1)}, bf16[2,256,256]{2,1,0:T(8,128)(2,1)S(1)}) custom-call(s32[7]{0:T(128)S(1)} %concatenate.3.meta.refs_0_, bf16[2,256,256]{2,1,0:T(8,128)(2,1)S(1)} %get-tuple-element.36.refs_1_, bf16[2,256,256]{2,1,0:T(8,128)(2,1)S(1)} %collective-permute-done.5.refs_2_, ...), custom_call_target="tpu_custom_call" | custom-call | flops 1000000000 | bytes 3801116 | tf_op jit(solution)/shard_map/far_field_0/pallas_call | solution.py:311
  41.7 0.1 collective-permute-start.7
  41.8 0.0 collective-permute-done.10.r_recv
  41.8 1.5 %collective-permute-done.7.l_recv = bf16[2,256,256]{2,1,0:T(8,128)(2,1)S(1)} collective-permute-done((bf16[2,256,256]{2,1,0:T(8,128)(2,1)S(1)}, bf16[2,256,256]{2,1,0:T(8,128)(2,1)S(1)}, u32[]{:S(2)}, u32[]{:S(2)}) %collective-permute-start.7) | collective-permute-done | bytes 262176 | tf_op jit(solution)/shard_map/ppermute | solution.py:339
  43.3 2.4 %assemble.1 = bf16[1,2,2048,256]{3,2,1,0:T(8,128)(2,1)} custom-call(s32[7]{0:T(128)S(1)} %concatenate.3.meta.refs_0_, s32[7]{0:T(128)S(1)} %collective-permute-done.meta.refs_0_.meta_left, bf16[2,256,256]{2,1,0:T(8,128)(2,1)S(1)} %get-tuple-element.50.l_keep, bf16[2,256,256]{2,1,0:T(8,128)(2,1)S(1)} %collective-permute-done.7.l_recv, ...), custom_call_target="tpu_custom_call" | custom-call | bytes 3145784 | tf_op jit(solution)/shard_map/assemble/pallas_call | solution.py:311
  (1 shorter events, 0.0 us)
Async XLA Ops:
  0.0 22.9 %copy-start = (bf16[1,2,256,256]{3,2,1,0:T(8,128)(2,1)S(1)}, bf16[1,2,256,256]{3,2,1,0:T(8,128)(2,1)}, u32[]{:S(2)}) copy-start(bf16[1,2,256,256]{3,2,1,0:T(8,128)(2,1)} %param.12) | copy-start | bytes 786436
  0.0 10.5 %copy-start.4 = (f32[5]{0:T(128)S(1)}, f32[5]{0:T(128)}, u32[]{:S(2)}) copy-start(f32[5]{0:T(128)} %taps.3) | copy-start | bytes 64
  0.0 17.3 %collective-permute-start.2 = (bf16[1,2,2048,256]{3,2,1,0:T(8,128)(2,1)}, bf16[1,2,2048,256]{3,2,1,0:T(8,128)(2,1)}, u32[]{:S(2)}, u32[]{:S(2)}) collective-permute-start(bf16[1,2,2048,256]{3,2,1,0:T(8,128)(2,1)} %tile.3), channel_id=1, source_target_pairs={{0,64},{64,0},{1,65},{65,1},{2,66},{66,2},{3,67},{67,3},{4,68},{68... | collective-permute-start | bytes 6291464 | tf_op jit(solution)/shard_map/ppermute | solution.py:339
  2.8 1.6 %copy-start.1 = (bf16[1,2,2048,256]{3,2,1,0:T(8,128)(2,1)S(1)}, bf16[1,2,2048,256]{3,2,1,0:T(8,128)(2,1)}, u32[]{:S(2)}) copy-start(bf16[1,2,2048,256]{3,2,1,0:T(8,128)(2,1)} %tile.3) | copy-start | bytes 6291460
  4.4 6.0 %copy-start.3 = (f32[2,256,256]{2,1,0:T(8,128)S(1)}, f32[2,256,256]{2,1,0:T(8,128)}, u32[]{:S(2)}) copy-start(f32[2,256,256]{2,1,0:T(8,128)} %probe.3) | copy-start | bytes 1572868
  6.0 11.3 %copy-start.2 = (bf16[1,2,2048,256]{3,2,1,0:T(8,128)(2,1)S(1)}, bf16[1,2,2048,256]{3,2,1,0:T(8,128)(2,1)}, u32[]{:S(2)}) copy-start(bf16[1,2,2048,256]{3,2,1,0:T(8,128)(2,1)} %tile.3) | copy-start | bytes 6291460
  6.0 4.5 %collective-permute-start.1 = (bf16[2,256,256]{2,1,0:T(8,128)(2,1)}, bf16[2,256,256]{2,1,0:T(8,128)(2,1)S(1)}, u32[]{:S(2)}, u32[]{:S(2)}) collective-permute-start(bf16[2,256,256]{2,1,0:T(8,128)(2,1)} %get-tuple-element.35), channel_id=1, source_target_pairs={{0,64},{64,0},{1,65},{65,1},{2,66},{66,2},{3,67},{67,3},{4,68},{68... | collective-permute-start | bytes 786440 | tf_op jit(solution)/shard_map/ppermute | solution.py:339
  6.1 9.4 %collective-permute-start = (s32[7]{0:T(128)S(1)}, s32[7]{0:T(128)S(1)}, u32[]{:S(2)}, u32[]{:S(2)}) collective-permute-start(s32[7]{0:T(128)S(1)} %concatenate.3.meta.refs_0_), channel_id=1, source_target_pairs={{0,1},{1,2},{2,3},{3,4},{4,5},{5,6},{6,7},{7,8},{8,9},{9,10},{10,1... | collective-permute-start | bytes 92 | tf_op jit(solution)/shard_map/ppermute | solution.py:329
  7.5 8.4 %collective-permute-start.3 = (bf16[64,128]{1,0:T(8,128)(2,1)S(1)}, bf16[64,128]{1,0:T(8,128)(2,1)S(1)}, u32[]{:S(2)}, u32[]{:S(2)}) collective-permute-start(bf16[64,128]{1,0:T(8,128)(2,1)S(1)} %get-tuple-element.37), channel_id=1, source_target_pairs={{0,1},{1,2},{2,3},{3,4},{4,5},{5,6},{6,7},{7,8},{8,9},{9,10},{10,1... | collective-permute-start | bytes 49160 | tf_op jit(solution)/shard_map/ppermute | solution.py:329
  8.7 8.6 %collective-permute-start.4 = (bf16[64,128]{1,0:T(8,128)(2,1)S(1)}, bf16[64,128]{1,0:T(8,128)(2,1)S(1)}, u32[]{:S(2)}, u32[]{:S(2)}) collective-permute-start(bf16[64,128]{1,0:T(8,128)(2,1)S(1)} %get-tuple-element.38), channel_id=1, source_target_pairs={{0,65},{1,66},{2,67},{3,68},{4,69},{5,70},{6,71},{7,72},{8,73},{9,... | collective-permute-start | bytes 49160 | tf_op jit(solution)/shard_map/ppermute | solution.py:336
  12.7 10.3 %copy-start.5 = (bf16[512,256]{1,0:T(8,128)(2,1)S(1)}, bf16[512,256]{1,0:T(8,128)(2,1)}, u32[]{:S(2)}) copy-start(bf16[512,256]{1,0:T(8,128)(2,1)} %constant.19.clone.tall) | copy-start | bytes 786436
  12.7 10.3 %copy-start.6 = (bf16[256,512]{1,0:T(8,128)(2,1)S(1)}, bf16[256,512]{1,0:T(8,128)(2,1)}, u32[]{:S(2)}) copy-start(bf16[256,512]{1,0:T(8,128)(2,1)} %constant.20.clone.wide) | copy-start | bytes 786436
  12.7 20.8 %collective-permute-start.8 = (bf16[2,256,256]{2,1,0:T(8,128)(2,1)S(1)}, bf16[2,256,256]{2,1,0:T(8,128)(2,1)S(1)}, u32[]{:S(2)}, u32[]{:S(2)}) collective-permute-start(bf16[2,256,256]{2,1,0:T(8,128)(2,1)S(1)} %get-tuple-element.36.refs_1_), channel_id=1, source_target_pairs={{0,1},{1,2},{2,3},{3,4},{4,5},{5,6},{6,7},{7,8},{8,9},{9,10},{10,1... | collective-permute-start | bytes 786440 | tf_op jit(solution)/shard_map/ppermute | solution.py:329
  20.4 18.4 %collective-permute-start.5 = (bf16[2,256,256]{2,1,0:T(8,128)(2,1)S(1)}, bf16[2,256,256]{2,1,0:T(8,128)(2,1)S(1)}, u32[]{:S(2)}, u32[]{:S(2)}) collective-permute-start(bf16[2,256,256]{2,1,0:T(8,128)(2,1)S(1)} %get-tuple-element.39.refs_2_), channel_id=1, source_target_pairs={{0,63},{1,0},{2,1},{3,2},{4,3},{5,4},{6,5},{7,6},{8,7},{9,8},{10,9... | collective-permute-start | bytes 786440 | tf_op jit(solution)/shard_map/ppermute | solution.py:332
  22.9 10.6 %collective-permute-start.9 = (bf16[256,256]{1,0:T(8,128)(2,1)S(1)}, bf16[256,256]{1,0:T(8,128)(2,1)S(1)}, u32[]{:S(2)}, u32[]{:S(2)}) collective-permute-start(bf16[256,256]{1,0:T(8,128)(2,1)S(1)} %dynamic-slice_bitcast_fusion.refs_3_), channel_id=1, source_target_pairs={{0,1},{1,2},{2,3},{3,4},{4,5},{5,6},{6,7},{7,8},{8,9},{9,10},{10,1... | collective-permute-start | bytes 393224 | tf_op jit(solution)/shard_map/ppermute | solution.py:329
  25.0 12.5 %collective-permute-start.6 = (bf16[64,128]{1,0:T(8,128)(2,1)S(1)}, bf16[64,128]{1,0:T(8,128)(2,1)S(1)}, u32[]{:S(2)}, u32[]{:S(2)}) collective-permute-start(bf16[64,128]{1,0:T(8,128)(2,1)S(1)} %get-tuple-element.44), channel_id=1, source_target_pairs={{0,63},{1,0},{2,1},{3,2},{4,3},{5,4},{6,5},{7,6},{8,7},{9,8},{10,9... | collective-permute-start | bytes 49160 | tf_op jit(solution)/shard_map/ppermute | solution.py:332
  36.4 5.4 %collective-permute-start.10 = (bf16[2,256,256]{2,1,0:T(8,128)(2,1)S(1)}, bf16[2,256,256]{2,1,0:T(8,128)(2,1)S(1)}, u32[]{:S(2)}, u32[]{:S(2)}) collective-permute-start(bf16[2,256,256]{2,1,0:T(8,128)(2,1)S(1)} %get-tuple-element.62), channel_id=1, source_target_pairs={{0,64},{64,0},{1,65},{65,1},{2,66},{66,2},{3,67},{67,3},{4,68},{68... | collective-permute-start | bytes 786440 | tf_op jit(solution)/shard_map/ppermute | solution.py:339
  41.7 1.6 %collective-permute-start.7 = (bf16[2,256,256]{2,1,0:T(8,128)(2,1)S(1)}, bf16[2,256,256]{2,1,0:T(8,128)(2,1)S(1)}, u32[]{:S(2)}, u32[]{:S(2)}) collective-permute-start(bf16[2,256,256]{2,1,0:T(8,128)(2,1)S(1)} %get-tuple-element.51), channel_id=1, source_target_pairs={{0,64},{64,0},{1,65},{65,1},{2,66},{66,2},{3,67},{67,3},{4,68},{68... | collective-permute-start | bytes 786440 | tf_op jit(solution)/shard_map/ppermute | solution.py:339

commit v2 on v1

v2 whole, which is shorter than its diff:
```python
import math

import jax
import jax.numpy as jnp
import numpy as np
from jax import lax
from jax.experimental import pallas as pl
from jax.experimental.pallas import tpu as pltpu
from jax.sharding import PartitionSpec as P

W = 256
STEP = 16
SPAN = W + STEP
LS = 16
RS = 4
EDGE = W - 8
BF = jnp.bfloat16
F32 = jnp.float32


def dot(a, b):
    return jnp.dot(a, b, preferred_element_type=F32)


def iota(shape, dim):
    return lax.broadcasted_iota(jnp.int32, shape, dim)


def dft_tables():
    indices = np.arange(W)
    angle = (indices[:, None] * indices[None, :] % W).astype(np.float64) * (2.0 * math.pi / W)
    factor = 1.0 / math.sqrt(W)
    cos = (np.cos(angle) * factor).astype(np.float32)
    sin = (np.sin(angle) * factor).astype(np.float32)
    return np.concatenate([cos, sin], axis=0)


def place(slots, slot):
    if len(slots) == 2:
        return slots[0][0, slot], slots[1][0, slot]
    value = slots[0][slot]
    return value & 2047, value >> 11


def span(row, height):
    base = jnp.minimum(row & ~(STEP - 1), height - SPAN)
    return pl.multiple_of(base, STEP), row - base


def fold(buf, offset):
    lane = buf.shape[-1]
    top = jnp.where(iota((STEP, lane), 0) < offset, buf[W:SPAN].astype(F32), buf[0:STEP].astype(F32))
    return jnp.concatenate([top, buf[STEP:W].astype(F32)], axis=0)


def taps_table(taps, shift):
    a = (iota((W, 1), 0) - shift) & (W - 1)
    b = (iota((1, W), 1) - shift) & (W - 1)
    k = jnp.abs(a - b)
    out = jnp.where(k == 0, taps[0], 0.0)
    for distance in range(1, 5):
        out = jnp.where(k == distance, taps[distance], out)
    return out.astype(BF)


def column_pass(re, im, t_col, sign):
    y = dot(jnp.concatenate([re.astype(BF), im.astype(BF)], axis=0), t_col)
    return re - sign * y[W:], im + sign * y[:W]


def propagate(re, im, t_row, t_col, sign):
    re, im = column_pass(re, im, t_col, sign)
    z = dot(t_row, jnp.concatenate([re.astype(BF), im.astype(BF)], axis=1))
    return re - sign * z[:, W:], im + sign * z[:, :W]


def one_hot(shift, transposed):
    if transposed:
        hit = iota((W, 1), 0) == ((iota((1, W), 1) - shift) & (W - 1))
    else:
        hit = iota((1, W), 1) == ((iota((W, 1), 0) - shift) & (W - 1))
    return jnp.where(hit, 1.0, 0.0).astype(BF)


def rotate_probe(probe, from_row, to_col):
    re, im = probe[0], probe[1]
    hr, hi = re.astype(BF), im.astype(BF)
    lr, li = (re - hr.astype(F32)).astype(BF), (im - hi.astype(F32)).astype(BF)
    x = dot(from_row, jnp.concatenate([hr, hi, lr, li], axis=1)).astype(BF)
    y = jnp.concatenate([x[:, i * W : (i + 1) * W] for i in range(4)], axis=0)
    z = dot(y, to_col)
    return z[0:W] + z[2 * W : 3 * W], z[W : 2 * W] + z[3 * W :]


def forward(w0, w1, psi0, t_row, t_col):
    p1 = propagate(w0[0] * psi0[0] - w0[1] * psi0[1], w0[0] * psi0[1] + w0[1] * psi0[0], t_row, t_col, 1.0)
    p1b = (p1[0].astype(BF), p1[1].astype(BF))
    q = (p1b[0].astype(F32), p1b[1].astype(F32))
    p2 = column_pass(w1[0] * q[0] - w1[1] * q[1], w1[0] * q[1] + w1[1] * q[0], t_col, 1.0)
    return p1b, (p2[0].astype(BF), p2[1].astype(BF))


def pack(parts, firsts, width):
    total = width * len(parts)
    blocks = 128 // total
    rows = W // blocks
    lane = iota((W, 128), 1)
    row = parts[0] if firsts[0] == 0 else pltpu.roll(parts[0], 128 - firsts[0], 1)
    for i in range(1, len(parts)):
        row = jnp.where(lane < i * width, row, pltpu.roll(parts[i], (i * width - firsts[i]) % 128, 1))
    out = row[:rows]
    for b in range(1, blocks):
        moved = pltpu.roll(row[b * rows : (b + 1) * rows], b * total, 1)
        out = jnp.where(lane[:rows] < b * total, out, moved)
    return out.astype(BF)


def unpack(packed, firsts, width):
    total = width * len(firsts)
    blocks = 128 // total
    values = packed.astype(F32)
    row = jnp.concatenate(
        [values] + [pltpu.roll(values, 128 - b * total, 1) for b in range(1, blocks)], axis=0
    )
    shifts = [(first - i * width) % 128 for i, first in enumerate(firsts)]
    return [pltpu.roll(row, shift, 1) if shift else row for shift in shifts]


def pair(own, other, mine):
    return jnp.where(mine == 0, own, other), jnp.where(mine == 0, other, own)


def windows_of(tile, other, mine, base, offset):
    rows = pl.ds(base, SPAN)
    out = []
    for i in range(2):
        for s, part in enumerate(pair(fold(tile[0, i, rows, :], offset), fold(other[0, i, rows, :], offset), mine)):
            out.append((s, i, part))
    return {(s, i): part for s, i, part in out}


def edges(pos_row, pos_col, tile, records, strip_keep, strip_send, keep, buf, buf_send, sems):
    mine = lax.axis_index("depth")
    work = []
    for k, (slot, target, width) in enumerate(((mine, buf, W), (1 - mine, buf_send, 128))):
        base, offset = span(pos_row[0, slot], tile.shape[2])
        source = tile.at[0, :, pl.ds(base, SPAN), pl.ds(W - width, width)]
        copy = pltpu.make_async_copy(source, target, sems.at[k])
        copy.start()
        work.append((copy, offset))
    record_copies = []
    for half in range(2):
        source = records.at[0, 1 - mine, :, pl.ds(half * 128, 128)]
        target = strip_send.at[pl.ds(W // 4 + half * W, W), :]
        record_copies.append(pltpu.make_async_copy(source, target, sems.at[2 + half]))
        record_copies[-1].start()
    lane = iota((STEP, 128), 1)
    numbers = jnp.zeros((STEP, 128), jnp.int32)
    for slot in range(2):
        row, col = pos_row[0, slot], pos_col[0, slot]
        for k, part in enumerate((row & (W - 1), row >> 8, col)):
            numbers = jnp.where(lane == slot * 4 + k, part, numbers)
    strip_keep[W // 4 :] = numbers.astype(F32).astype(BF)
    (copy, offset), (copy_send, offset_send) = work
    copy.wait()
    window = [fold(buf[i], offset) for i in range(2)]
    keep[0], keep[1] = window[0].astype(BF), window[1].astype(BF)
    strip_keep[: W // 4] = pack([part[:, W - 128 :] for part in window], [128 - LS] * 2, LS)
    copy_send.wait()
    strip_send[: W // 4] = pack([fold(buf_send[i], offset_send) for i in range(2)], [128 - LS] * 2, LS)
    for copy in record_copies:
        copy.wait()


def receive(strip, slots):
    lane = iota((8, 128), 1)
    values = strip[W // 4 :].astype(F32)[:8]
    for slot in range(2):
        weight = jnp.zeros((8, 128), F32)
        for k, factor in enumerate((1, W, 2048)):
            weight = jnp.where(lane == slot * 4 + k, factor / 8.0, weight)
        slots[slot] = jnp.sum(values * weight).astype(jnp.int32)


def settle(height, slots, taps, probe, psi0, t_row, t_col):
    row, col0 = place(slots, lax.axis_index("depth"))
    _, offset = span(row, height)
    t_row[...], t_col[...] = taps_table(taps, offset), taps_table(taps, col0)
    psi0[0], psi0[1] = rotate_probe(probe, one_hot(offset, False), one_hot(col0, True))


def tables(height, slots, dft, t_row, t_col, f_to, f_right, f_back, f_last):
    row, col0 = place(slots, lax.axis_index("depth"))
    _, offset = span(row, height)
    tall = dft[...]
    wide = jnp.concatenate([tall[:W], tall[W:]], axis=1)
    x = dot(tall, one_hot(offset, True)).astype(BF)
    y = dot(x, t_row[...])
    cos, sin = (x[:W].astype(F32) + y[W:]).astype(BF), (x[W:].astype(F32) - y[:W]).astype(BF)
    f_to[:W, :W], f_to[:W, W:], f_to[W:, :W], f_to[W:, W:] = cos, sin, -sin, cos
    x = dot(one_hot(col0, False), wide).astype(BF)
    cos, sin = x[:, :W], x[:, W:]
    f_right[:W, :W], f_right[:W, W:], f_right[W:, :W], f_right[W:, W:] = cos, -sin, sin, cos
    x = dot(one_hot(offset, False), wide).astype(BF)
    y = dot(t_row[...], x)
    cos, sin = (x[:, :W].astype(F32) + y[:, W:]).astype(BF), (x[:, W:].astype(F32) - y[:, :W]).astype(BF)
    f_back[:W, :W], f_back[:W, W:], f_back[W:, :W], f_back[W:, W:] = cos, -sin, sin, cos
    x = dot(tall, one_hot(col0, True)).astype(BF)
    y = dot(x, t_col[...])
    cos, sin = (x[:W].astype(F32) + y[W:]).astype(BF), (x[W:].astype(F32) - y[:W]).astype(BF)
    f_last[:W, :W], f_last[:W, W:], f_last[W:, :W], f_last[W:, W:] = cos, sin, -sin, cos


def put_exit(exit_ref, psi2, inside):
    for i in range(2):
        part = jnp.where(inside, psi2[i], 0.0).astype(BF)
        for half in range(2):
            exit_ref[(2 * i + half) * W : (2 * i + half + 1) * W] = part[:, half * 128 : (half + 1) * 128]


def left_forward(slots, counts, keep, other, psi0, t_row, t_col, exit_ref, w_ref, psi1_ref):
    mine = lax.axis_index("depth")
    row, col0 = place(slots, mine)
    base, offset = span(row, other.shape[2])
    column = iota((1, W), 1)
    inside = column >= col0
    w = {}
    for i in range(2):
        far = fold(other[0, i, pl.ds(base, SPAN), :], offset)
        for s, part in enumerate(pair(keep[i].astype(F32), far, mine)):
            w[s, i] = jnp.where(inside, part, 0.0)
    w_ref[0], w_ref[1] = w[1, 0].astype(BF), w[1, 1].astype(BF)
    psi1, psi2 = forward((w[0, 0], w[0, 1]), (w[1, 0], w[1, 1]), psi0, t_row[...], t_col[...])
    psi1_ref[0], psi1_ref[1] = psi1
    put_exit(exit_ref, psi2, inside & (column < EDGE))
    number, lane = iota((STEP, 128), 0), iota((STEP, 128), 1)
    live = jnp.where(mine < counts[0], 1.0, 0.0)
    marks = jnp.where(lane + jnp.where(number == 2, 128, 0) >= col0, 1.0, 0.0)
    exit_ref[4 * W :] = jnp.where(number == 0, live, marks).astype(BF)


def right_forward(
    slots, tile, other, strip_a, strip_b, psi0, t_row, t_col, exit_ref, w_ref, psi1_ref
):
    mine = lax.axis_index("depth")
    row, col0 = place(slots, mine)
    base, offset = span(row, tile.shape[2])
    lane, column = iota((1, 128), 1), iota((1, W), 1)
    strips = pair(strip_a[: W // 4].astype(F32), strip_b[: W // 4].astype(F32), mine)
    w = windows_of(tile, other, mine, base, offset)
    for s in range(2):
        lefts = unpack(strips[s], [128 - LS] * 2, LS)
        for i in range(2):
            left = jnp.where(lane >= 128 - LS, lefts[i], 0.0)
            low = jnp.where(lane < col0, w[s, i][:, :128], 0.0)
            high = jnp.where(lane + 128 < col0, w[s, i][:, 128:], left)
            w[s, i] = jnp.concatenate([low, high], axis=1)
    w_ref[0], w_ref[1] = w[1, 0].astype(BF), w[1, 1].astype(BF)
    psi1, psi2 = forward((w[0, 0], w[0, 1]), (w[1, 0], w[1, 1]), psi0, t_row[...], t_col[...])
    psi1_ref[0], psi1_ref[1] = psi1
    put_exit(exit_ref, psi2, (column < col0) | (column >= EDGE))
    parts = [psi1[0][:, 128:].astype(F32), psi1[1][:, 128:].astype(F32), w[1, 0][:, :128], w[1, 1][:, :128]]
    exit_ref[4 * W :] = pack(parts, [128 - RS, 128 - RS, 0, 0], RS)


def far_field(
    side, exit_l, exit_r, record, psi0, t_row, t_col, f_to, f_right, f_back, f_last, psi1, w1, keep, send
):
    mine = lax.axis_index("depth")
    notes = exit_l[4 * W :].astype(F32)
    live = notes[0:1, 0:1]
    of_left = jnp.concatenate([notes[1:2], notes[2:3]], axis=1)
    region = of_left if side == 0 else 1.0 - of_left
    lane = iota((1, 128), 1)
    halves = [exit_l[k * W : (k + 1) * W] + exit_r[k * W : (k + 1) * W] for k in range(4)]
    wave = jnp.concatenate([jnp.concatenate(halves[:2], axis=1), jnp.concatenate(halves[2:], axis=1)], axis=0)
    x = dot(f_to[...], wave).astype(BF)
    x = dot(jnp.concatenate([x[:W], x[W:]], axis=1), f_right[...])
    fr, fi = x[:, :W], x[:, W:]
    if side == 1:
        record = jnp.concatenate([record[W // 4 : W // 4 + W], record[W // 4 + W :]], axis=1)
    misfit = (fr * fr + fi * fi - record[...].astype(F32)) * live
    x = dot(f_back[...], jnp.concatenate([(misfit * fr).astype(BF), (misfit * fi).astype(BF)], axis=0)).astype(BF)
    x = dot(jnp.concatenate([x[:W], x[W:]], axis=1), f_last[...])
    q1 = x[:, :W], x[:, W:]
    psi = [psi1[i].astype(F32) for i in range(2)]
    w = [w1[i].astype(F32) for i in range(2)]
    if side == 0:
        strips = unpack(exit_r[4 * W :], [128 - RS, 128 - RS, 0, 0], RS)
        for i in range(2):
            high = jnp.where(lane >= 128 - RS, strips[i], psi[i][:, 128:])
            psi[i] = jnp.concatenate([psi[i][:, :128], high], axis=1)
            low = jnp.where(lane < RS, w[i][:, :128] + strips[2 + i] * (1.0 - of_left[:, :128]), w[i][:, :128])
            w[i] = jnp.concatenate([low, w[i][:, 128:]], axis=1)

    def term(psi_r, psi_i, q):
        return (psi_r * q[0] + psi_i * q[1]) * region, (psi_r * q[1] - psi_i * q[0]) * region

    term1 = term(psi[0], psi[1], q1)
    cr = (w[0] * q1[0] + w[1] * q1[1]).astype(BF).astype(F32)
    ci = (w[0] * q1[1] - w[1] * q1[0]).astype(BF).astype(F32)
    q0 = propagate(cr, ci, t_row[...], t_col[...], -1.0)
    term0 = term(psi0[0], psi0[1], q0)
    for i in range(2):
        first, second = pair(term0[i], term1[i], mine)
        keep[i], send[i] = first.astype(BF), second.astype(BF)


def assemble(own, left, l_keep, l_recv, r_keep, r_recv, out, buf, sems):
    height = out.shape[2]
    mine = lax.axis_index("depth")
    work = []
    for where, slot, term in (
        (left, mine, r_keep),
        (left, 1 - mine, r_recv),
        (own, mine, l_keep),
        (own, 1 - mine, l_recv),
    ):
        row, _ = place(where, slot)
        base, offset = span(row, height)
        work.append((base, offset, term))
    copies = []
    for i in range(2):
        buf[i] = jnp.zeros((height, W), BF)
        for base, offset, term in work:
            mask = iota((STEP, 1), 0) >= offset
            top = term[i, 0:STEP].astype(F32)
            rows = pl.ds(base, STEP)
            buf[i, rows, :] = buf[i, rows, :] + jnp.where(mask, top, 0.0).astype(BF)
            rows = pl.ds(pl.multiple_of(base + STEP, STEP), W - STEP)
            buf[i, rows, :] = buf[i, rows, :] + term[i, STEP:W]
            rows = pl.ds(pl.multiple_of(base + W, STEP), STEP)
            buf[i, rows, :] = buf[i, rows, :] + jnp.where(mask, 0.0, top).astype(BF)
        for k in range(4):
            rows = pl.ds(k * (height // 4), height // 4)
            copy = pltpu.make_async_copy(buf.at[i, rows, :], out.at[0, i, rows, :], sems.at[i, k])
            copy.start()
            copies.append(copy)
    for copy in copies:
        copy.wait()


SMEM = pl.BlockSpec(memory_space=pltpu.SMEM)
VMEM = pl.BlockSpec(memory_space=pltpu.VMEM)
HBM = pl.BlockSpec(memory_space=pltpu.HBM)


def call(kernel, name, specs, outs, args, scratch=(), out_specs=None, vmem=40, after=(), token=False):
    count, extra, made = len(args), len(after), len(outs)

    def body(*refs):
        refs = list(refs)
        if token:
            refs.pop(count + extra + made)[...] = jnp.zeros((8, 128), F32)
        kernel(*refs[:count], *refs[count + extra :])

    outs, out_specs = list(outs), list(out_specs or [VMEM] * made)
    if token:
        outs, out_specs = outs + [((8, 128), F32)], out_specs + [VMEM]
    moved = sum(math.prod(shape) * jnp.dtype(kind).itemsize for shape, kind in outs)
    moved += sum(math.prod(a.shape) * a.dtype.itemsize for a, s in zip(args, specs) if s is not HBM)
    return pl.pallas_call(
        body,
        name=name,
        out_shape=[jax.ShapeDtypeStruct(shape, kind) for shape, kind in outs],
        in_specs=list(specs) + [VMEM] * extra,
        out_specs=out_specs,
        scratch_shapes=list(scratch),
        compiler_params=pltpu.CompilerParams(vmem_limit_bytes=vmem * 1024 * 1024),
        cost_estimate=pl.CostEstimate(flops=10**9, bytes_accessed=moved, transcendentals=0),
    )(*args, *after)


FIELD, WAVE = ((2, W, W), BF), ((2, W, W), F32)
BAND, QUAD = ((W, W), BF), ((2 * W, 2 * W), BF)
MARKED, LOADED, SLOTS = ((W // 4 + STEP, 128), BF), ((W // 4 + 2 * W, 128), BF), ((2,), jnp.int32)
EXIT_L, EXIT_R = ((4 * W + STEP, 128), BF), ((4 * W + W * 4 * RS // 128, 128), BF)


def on_device(transmission, chirp_taps, probe_field, records, pos_row, pos_col, counts):
    height = transmission.shape[2]
    tiles = lax.axis_size("tile")
    my_depth = lax.axis_index("depth")

    def to_right(x):
        return lax.ppermute(x, "tile", [(i, (i + 1) % tiles) for i in range(tiles)])

    def to_left(x):
        return lax.ppermute(x, "tile", [(i, (i - 1) % tiles) for i in range(tiles)])

    def to_right_other(x):
        pairs = [(d * tiles + i, (1 - d) * tiles + (i + 1) % tiles) for d in range(2) for i in range(tiles)]
        return lax.ppermute(x, ("depth", "tile"), pairs)

    def to_other(x):
        return lax.ppermute(x, "depth", [(0, 1), (1, 0)])

    def own(kernel):
        return lambda pos_row, pos_col, *refs: kernel((pos_row, pos_col), *refs)

    def left(kernel):
        return lambda slots, *refs: kernel((slots,), *refs)

    def table_kernel(*refs):
        tables(height, *refs)

    def settle_own(*refs):
        settle(height, *refs)

    def settle_left(strip, taps, probe, slots, *refs):
        receive(strip, slots)
        settle(height, (slots,), taps, probe, *refs)

    def terms(side, *args, after=(), token=False):
        def kernel(*refs):
            far_field(side, *refs)

        return call(
            kernel, f"far_field_{side}", [VMEM] * len(args), [FIELD, FIELD], args, after=after, token=token
        )

    dft = jnp.asarray(dft_tables(), BF)
    other_tile = to_other(transmission)
    record = lax.dynamic_index_in_dim(records[0], my_depth, 0, keepdims=False)
    strip_keep, strip_send, keep = call(
        edges, "edges", [SMEM, SMEM, HBM, HBM], [MARKED, LOADED, FIELD],
        [pos_row, pos_col, transmission, records],
        [pltpu.VMEM((2, SPAN, W), BF), pltpu.VMEM((2, SPAN, 128), BF), pltpu.SemaphoreType.DMA((4,))], vmem=56,
    )
    strip_a = to_right(strip_keep)
    strip_b = to_right_other(strip_send)
    settled = call(
        own(settle_own), "settle", [SMEM, SMEM, SMEM, VMEM], [WAVE, BAND, BAND],
        [pos_row, pos_col, chirp_taps, probe_field],
    )
    exit_l, w1, psi1, done = call(
        own(left_forward), "left_forward", [SMEM] * 3 + [VMEM] * 5, [EXIT_L, FIELD, FIELD],
        [pos_row, pos_col, counts, keep, other_tile, *settled], token=True,
    )
    exit_l_left = to_right(exit_l)
    slots_left, *settled_left = call(
        settle_left, "settle_left", [VMEM, SMEM, VMEM], [SLOTS, WAVE, BAND, BAND],
        [strip_a, chirp_taps, probe_field], out_specs=[SMEM] + [VMEM] * 3, after=[done],
    )
    exit_r_left, w_left, psi1_left, done = call(
        left(right_forward), "right_forward", [SMEM] + [VMEM] * 7, [EXIT_R, FIELD, FIELD],
        [slots_left, transmission, other_tile, strip_a, strip_b, *settled_left], token=True,
    )
    exit_r = to_left(exit_r_left)
    *left_tables, done = call(
        left(table_kernel), "tables_left", [SMEM] + [VMEM] * 3, [QUAD] * 4, [slots_left, dft, *settled_left[1:]],
        after=[done], token=True,
    )
    *own_tables, done = call(
        own(table_kernel), "tables", [SMEM] * 2 + [VMEM] * 3, [QUAD] * 4, [pos_row, pos_col, dft, *settled[1:]],
        after=[done], token=True,
    )
    r_keep, r_send, done = terms(
        1, exit_l_left, exit_r_left, strip_b, *settled_left, *left_tables, psi1_left, w_left, after=[done], token=True
    )
    r_recv = to_other(r_send)
    l_keep, l_send = terms(0, exit_l, exit_r, record, *settled, *own_tables, psi1, w1, after=[done])
    l_recv = to_other(l_send)

    def assemble_kernel(pos_row, pos_col, slots, *refs):
        assemble((pos_row, pos_col), (slots,), *refs)

    return call(
        assemble_kernel, "assemble", [SMEM] * 3 + [VMEM] * 4, [(transmission.shape, BF)],
        [pos_row, pos_col, slots_left, l_keep, l_recv, r_keep, r_recv],
        [pltpu.VMEM((2, height, W), BF), pltpu.SemaphoreType.DMA((2, 4))], out_specs=[HBM],
    )[0]


def solution(mesh):
    in_specs = (
        P("depth", None, None, "tile"),
        P(),
        P(),
        P("tile", None, None, None),
        P("tile", None),
        P("tile", None),
        P("tile"),
    )
    out_specs = P("depth", None, None, "tile")
    return jax.shard_map(
        on_device, mesh=mesh, in_specs=in_specs, out_specs=out_specs, check_vma=False
    )
```

time: 45.9 us -> 33.5 us (0.73)
  starting transfers between devices: 17.9 us -> 9.26 us
  local copies, waits for them, and re-layouts: 2.38 us -> 0.06 us
  Pallas kernels: 18.3 us -> 17 us
    ppermute x2 -> x1, starting transfers between devices: 9.44 us -> 1.75 us  [to_left(): return lax.ppermute(x, 'tile', [(i, (i - 1) % tiles) for i in range(tiles)])]
    unnamed x14 -> x16, local copies, waits for them, and re-layouts: 1.62 us -> 0.04 us
    ppermute x4 -> x2, starting transfers between devices: 3.88 us -> 2.37 us  [to_right(): return lax.ppermute(x, 'tile', [(i, (i + 1) % tiles) for i in range(tiles)])]
    pallas_call x9 -> x10, Pallas kernels: 18.3 us -> 17 us  [call(): pl.pallas_call(body, name=name, out_shape=[jax.ShapeDtypeStruct(shape, ki...]
    ppermute x4 -> x3, starting transfers between devices: 2.78 us -> 3.61 us  [to_other(): return lax.ppermute(x, 'depth', [(0, 1), (1, 0)])]
    concatenate x1 -> x0, local copies, waits for them, and re-layouts: 0.75 us -> none  [on_device(): jnp.concatenate([pos_row[0], pos_col[0], counts, my_depth[None], jnp.full...]
    ppermute x1, waiting for transfers between devices: 1.4 us -> 1.99 us  [to_right_other(): return lax.ppermute(x, ('depth', 'tile'), pairs)]
    ppermute x4 -> x2, waiting for transfers between devices: 3.42 us -> 3.03 us  [to_right(): return lax.ppermute(x, 'tile', [(i, (i + 1) % tiles) for i in range(tiles)])]
  transfers between devices with their start and end apart: 11 -> 7, of which waited for: 5 -> 4; matrix products, arithmetic and copies ran while one was open for 2% -> 0% of each run, Pallas kernels for 35% -> 45%
where the time goes in v2:
time: 33.5 us; the launch traced here: 33.4 us
  Pallas kernels  17 us (51%)
  starting transfers between devices  9.26 us (28%)
  waiting for transfers between devices  6.19 us (18%)
  between operations  0.82 us (2%)
    pallas_call x10, Pallas kernels, call(): pl.pallas_call(body, name=name, out_shape=[jax.ShapeDtypeStruct(shape, ki...  17 us
    ppermute x3, starting transfers between devices, to_other(): return lax.ppermute(x, 'depth', [(0, 1), (1, 0)])  3.61 us
    ppermute x2, waiting for transfers between devices, to_right(): return lax.ppermute(x, 'tile', [(i, (i + 1) % tiles) for i in range(tiles)])  3.03 us
    ppermute x2, starting transfers between devices, to_right(): return lax.ppermute(x, 'tile', [(i, (i + 1) % tiles) for i in range(tiles)])  2.37 us
    ppermute x1, waiting for transfers between devices, to_right_other(): return lax.ppermute(x, ('depth', 'tile'), pairs)  1.99 us
    ppermute x1, starting transfers between devices, to_left(): return lax.ppermute(x, 'tile', [(i, (i - 1) % tiles) for i in range(tiles)])  1.75 us
    ppermute x1, starting transfers between devices, to_right_other(): return lax.ppermute(x, ('depth', 'tile'), pairs)  1.54 us
    ppermute x3, waiting for transfers between devices, to_other(): return lax.ppermute(x, 'depth', [(0, 1), (1, 0)])  1.16 us
  transfers between devices with their start and end apart: 7, of which 4 were waited for; matrix products, arithmetic and copies ran while one was open for 0% of the time, Pallas kernels for 45%

profile of v2, /device:TPU:1, one launch (start us, length us, event | category | flops | bytes accessed | tf_op | source)
XLA Modules:
  0.0 33.4 jit_solution(18083242501645933416)
XLA Ops:
  0.0 0.0 copy-start.3
  0.0 0.0 copy-start.4
  0.0 0.0 copy-start.1
  0.0 0.0 copy-start.2
  0.0 1.5 %collective-permute-start.1 = (bf16[1,2,2048,256]{3,2,1,0:T(8,128)(2,1)}, bf16[1,2,2048,256]{3,2,1,0:T(8,128)(2,1)S(1)}, u32[]{:S(2)}, u32[]{:S(2)}) collective-permute-start(bf16[1,2,2048,256]{3,2,1,0:T(8,128)(2,1)} %refs_1_.12), channel_id=1, source_target_pairs={{0,64},{64,0},{1,65},{65,1},{2,66},{66,2},{3,67},{67,3},{4,68},{68... | collective-permute-start | bytes 6291464 | tf_op jit(solution)/shard_map/ppermute | solution.py:396
  1.5 2.8 %edges.1 = (bf16[80,128]{1,0:T(8,128)(2,1)}, bf16[576,128]{1,0:T(8,128)(2,1)}, bf16[2,256,256]{2,1,0:T(8,128)(2,1)}) custom-call(s32[1,2]{1,0:T(1,128)} %refs_0_.9, s32[1,2]{1,0:T(1,128)} %refs_1_.14, bf16[1,2,2048,256]{3,2,1,0:T(8,128)(2,1)} %refs_1_.12, bf16[1,2,256,256]{3,2,1,0:T(8,128)(2,1)} %refs_3_.2), custom_call_target="tpu_custom_call" | custom-call | flops 1000000000 | bytes 430096 | tf_op jit(solution)/shard_map/edges/pallas_call | solution.py:362
  4.3 0.0 copy-start.7
  4.3 0.0 copy-start.6
  4.3 1.4 %collective-permute-start = (bf16[80,128]{1,0:T(8,128)(2,1)}, bf16[80,128]{1,0:T(8,128)(2,1)S(1)}, u32[]{:S(2)}, u32[]{:S(2)}) collective-permute-start(bf16[80,128]{1,0:T(8,128)(2,1)} %get-tuple-element.38), channel_id=1, source_target_pairs={{0,1},{1,2},{2,3},{3,4},{4,5},{5,6},{6,7},{7,8},{8,9},{9,10},{10,1... | collective-permute-start | bytes 61448 | tf_op jit(solution)/shard_map/ppermute | solution.py:386
  5.7 1.5 %collective-permute-start.2 = (bf16[576,128]{1,0:T(8,128)(2,1)}, bf16[576,128]{1,0:T(8,128)(2,1)S(1)}, u32[]{:S(2)}, u32[]{:S(2)}) collective-permute-start(bf16[576,128]{1,0:T(8,128)(2,1)} %get-tuple-element.46), channel_id=1, source_target_pairs={{0,65},{1,66},{2,67},{3,68},{4,69},{5,70},{6,71},{7,72},{8,73},{9,... | collective-permute-start | bytes 442376 | tf_op jit(solution)/shard_map/ppermute | solution.py:393
  7.9 0.0 copy-done.3
  7.9 0.0 copy-done.4
  7.9 0.0 copy-done.1
  7.9 0.0 copy-done.2
  7.9 1.3 %settle.1 = (f32[2,256,256]{2,1,0:T(8,128)S(1)}, bf16[256,256]{1,0:T(8,128)(2,1)S(1)}, bf16[256,256]{1,0:T(8,128)(2,1)S(1)}) custom-call(s32[1,2]{1,0:T(1,128)S(1)} %copy-done.3, s32[1,2]{1,0:T(1,128)S(1)} %copy-done.4, f32[5]{0:T(128)S(1)} %copy-done.2, f32[2,256,256]{2,1,0:T(8,128)S(1)} %copy-done.1), custom_call_target="tpu_custom_call" | custom-call | flops 1000000000 | bytes 1310756 | tf_op jit(solution)/shard_map/settle/pallas_call | solution.py:362
  9.2 0.0 copy-done.7
  9.2 0.0 collective-permute-done.1.refs_4_.refs_2_
  9.2 0.0 copy-done.6
  9.3 1.3 %left_forward.1 = (bf16[1040,128]{1,0:T(8,128)(2,1)S(1)}, bf16[2,256,256]{2,1,0:T(8,128)(2,1)S(1)}, bf16[2,256,256]{2,1,0:T(8,128)(2,1)S(1)}, f32[8,128]{1,0:T(8,128)S(1)}) custom-call(s32[1,2]{1,0:T(1,128)S(1)} %copy-done.3, s32[1,2]{1,0:T(1,128)S(1)} %copy-done.4, s32[1]{0:T(128)S(6)} %copy.9.refs_2_, bf16[2,256,256]{2,1,0:T(8,128)(2,1)S(1)} %copy-done.6, ...), custom_call_target="tpu_custom_call" | custom-call | flops 1000000000 | bytes 3940372 | tf_op jit(solution)/shard_map/left_forward/pallas_call | solution.py:362
  10.6 0.0 copy-start
  10.6 1.0 %collective-permute-start.4 = (bf16[1040,128]{1,0:T(8,128)(2,1)S(1)}, bf16[1040,128]{1,0:T(8,128)(2,1)S(1)}, u32[]{:S(2)}, u32[]{:S(2)}) collective-permute-start(bf16[1040,128]{1,0:T(8,128)(2,1)S(1)} %get-tuple-element.45.refs_0_), channel_id=1, source_target_pairs={{0,1},{1,2},{2,3},{3,4},{4,5},{5,6},{6,7},{7,8},{8,9},{9,10},{10,1... | collective-permute-start | bytes 798728 | tf_op jit(solution)/shard_map/ppermute | solution.py:386
  11.6 2.7 %collective-permute-done.refs_0_.refs_3_ = bf16[80,128]{1,0:T(8,128)(2,1)S(1)} collective-permute-done((bf16[80,128]{1,0:T(8,128)(2,1)}, bf16[80,128]{1,0:T(8,128)(2,1)S(1)}, u32[]{:S(2)}, u32[]{:S(2)}) %collective-permute-start) | collective-permute-done | bytes 20512 | tf_op jit(solution)/shard_map/ppermute | solution.py:386
  14.3 1.4 %settle_left.1 = (s32[2]{0:T(128)S(1)}, f32[2,256,256]{2,1,0:T(8,128)S(1)}, bf16[256,256]{1,0:T(8,128)(2,1)S(1)}, bf16[256,256]{1,0:T(8,128)(2,1)S(1)}) custom-call(bf16[80,128]{1,0:T(8,128)(2,1)S(1)} %collective-permute-done.refs_0_.refs_3_, f32[5]{0:T(128)S(1)} %copy-done.2, f32[2,256,256]{2,1,0:T(8,128)S(1)} %copy-done.1, ...), custom_call_target="tpu_custom_call" | custom-call | flops 1000000000 | bytes 1331228 | tf_op jit(solution)/shard_map/settle_left/pallas_call | solution.py:362
  15.7 2.0 %collective-permute-done.2.refs_4_.refs_2_ = bf16[576,128]{1,0:T(8,128)(2,1)S(1)} collective-permute-done((bf16[576,128]{1,0:T(8,128)(2,1)}, bf16[576,128]{1,0:T(8,128)(2,1)S(1)}, u32[]{:S(2)}, u32[]{:S(2)}) %collective-permute-start.2) | collective-permute-done | bytes 147488 | tf_op jit(solution)/shard_map/ppermute | solution.py:393
  17.7 0.0 copy-done
  17.7 0.0 copy-start.5
  17.7 1.4 %right_forward.1 = (bf16[1056,128]{1,0:T(8,128)(2,1)S(1)}, bf16[2,256,256]{2,1,0:T(8,128)(2,1)S(1)}, bf16[2,256,256]{2,1,0:T(8,128)(2,1)S(1)}, f32[8,128]{1,0:T(8,128)S(1)}) custom-call(s32[2]{0:T(128)S(1)} %get-tuple-element.44.refs_0_.refs_2_, bf16[1,2,2048,256]{3,2,1,0:T(8,128)(2,1)S(1)} %copy-done, ...), custom_call_target="tpu_custom_call" | custom-call | flops 1000000000 | bytes 5947400 | tf_op jit(solution)/shard_map/right_forward/pallas_call | solution.py:362
  19.1 1.7 %collective-permute-start.3 = (bf16[1056,128]{1,0:T(8,128)(2,1)S(1)}, bf16[1056,128]{1,0:T(8,128)(2,1)S(1)}, u32[]{:S(2)}, u32[]{:S(2)}) collective-permute-start(bf16[1056,128]{1,0:T(8,128)(2,1)S(1)} %get-tuple-element.50.refs_1_), channel_id=1, source_target_pairs={{0,63},{1,0},{2,1},{3,2},{4,3},{5,4},{6,5},{7,6},{8,7},{9,8},{10,9... | collective-permute-start | bytes 811016 | tf_op jit(solution)/shard_map/ppermute | solution.py:389
  20.8 0.0 copy-done.5
  20.8 1.4 %tables_left.1 = (bf16[512,512]{1,0:T(8,128)(2,1)S(1)}, bf16[512,512]{1,0:T(8,128)(2,1)S(1)}, bf16[512,512]{1,0:T(8,128)(2,1)S(1)}, bf16[512,512]{1,0:T(8,128)(2,1)S(1)}, f32[8,128]{1,0:T(8,128)S(1)}) custom-call(s32[2]{0:T(128)S(1)} %get-tuple-element.44.refs_0_.refs_2_, bf16[512,256]{1,0:T(8,128)(2,1)S(1)} %copy-done.5, ...), custom_call_target="tpu_custom_call" | custom-call | flops 1000000000 | bytes 2625544 | tf_op jit(solution)/shard_map/tables_left/pallas_call | solution.py:362
  22.3 1.4 %tables.1 = (bf16[512,512]{1,0:T(8,128)(2,1)S(1)}, bf16[512,512]{1,0:T(8,128)(2,1)S(1)}, bf16[512,512]{1,0:T(8,128)(2,1)S(1)}, bf16[512,512]{1,0:T(8,128)(2,1)S(1)}, f32[8,128]{1,0:T(8,128)S(1)}) custom-call(s32[1,2]{1,0:T(1,128)S(1)} %copy-done.3, s32[1,2]{1,0:T(1,128)S(1)} %copy-done.4, bf16[512,256]{1,0:T(8,128)(2,1)S(1)} %copy-done.5, ...), custom_call_target="tpu_custom_call" | custom-call | flops 1000000000 | bytes 2625552 | tf_op jit(solution)/shard_map/tables/pallas_call | solution.py:362
  23.7 0.3 collective-permute-done.4.refs_0_
  24.0 2.0 %far_field_1.1 = (bf16[2,256,256]{2,1,0:T(8,128)(2,1)S(1)}, bf16[2,256,256]{2,1,0:T(8,128)(2,1)S(1)}, f32[8,128]{1,0:T(8,128)S(1)}) custom-call(bf16[1040,128]{1,0:T(8,128)(2,1)S(1)} %collective-permute-done.4.refs_0_, bf16[1056,128]{1,0:T(8,128)(2,1)S(1)} %get-tuple-element.50.refs_1_, bf16[576,128]{1,0:T(8,128)(2,1)S(1)} %collective-permute-done.2.refs_4_.refs_2_, ...), custom_call_target="tpu_custom_call" | custom-call | flops 1000000000 | bytes 4620288 | tf_op jit(solution)/shard_map/far_field_1/pallas_call | solution.py:362
  26.0 0.9 %collective-permute-start.6 = (bf16[2,256,256]{2,1,0:T(8,128)(2,1)S(1)}, bf16[2,256,256]{2,1,0:T(8,128)(2,1)S(1)}, u32[]{:S(2)}, u32[]{:S(2)}) collective-permute-start(bf16[2,256,256]{2,1,0:T(8,128)(2,1)S(1)} %get-tuple-element.70), channel_id=1, source_target_pairs={{0,64},{64,0},{1,65},{65,1},{2,66},{66,2},{3,67},{67,3},{4,68},{68... | collective-permute-start | bytes 786440 | tf_op jit(solution)/shard_map/ppermute | solution.py:396
  26.9 0.0 collective-permute-done.3.refs_1_
  27.0 2.0 %far_field_0.1 = (bf16[2,256,256]{2,1,0:T(8,128)(2,1)S(1)}, bf16[2,256,256]{2,1,0:T(8,128)(2,1)S(1)}) custom-call(bf16[1040,128]{1,0:T(8,128)(2,1)S(1)} %get-tuple-element.45.refs_0_, bf16[1056,128]{1,0:T(8,128)(2,1)S(1)} %collective-permute-done.3.refs_1_, bf16[256,256]{1,0:T(8,128)(2,1)S(1)} %dynamic-slice_bitcast_fusion.refs_2_, ...), custom_call_target="tpu_custom_call" | custom-call | flops 1000000000 | bytes 4599808 | tf_op jit(solution)/shard_map/far_field_0/pallas_call | solution.py:362
  29.0 1.2 %collective-permute-start.5 = (bf16[2,256,256]{2,1,0:T(8,128)(2,1)S(1)}, bf16[2,256,256]{2,1,0:T(8,128)(2,1)S(1)}, u32[]{:S(2)}, u32[]{:S(2)}) collective-permute-start(bf16[2,256,256]{2,1,0:T(8,128)(2,1)S(1)} %get-tuple-element.68), channel_id=1, source_target_pairs={{0,64},{64,0},{1,65},{65,1},{2,66},{66,2},{3,67},{67,3},{4,68},{68... | collective-permute-start | bytes 786440 | tf_op jit(solution)/shard_map/ppermute | solution.py:396
  30.1 0.0 collective-permute-done.6.refs_6_
  30.1 1.2 %collective-permute-done.5.refs_4_ = bf16[2,256,256]{2,1,0:T(8,128)(2,1)S(1)} collective-permute-done((bf16[2,256,256]{2,1,0:T(8,128)(2,1)S(1)}, bf16[2,256,256]{2,1,0:T(8,128)(2,1)S(1)}, u32[]{:S(2)}, u32[]{:S(2)}) %collective-permute-start.5) | collective-permute-done | bytes 262176 | tf_op jit(solution)/shard_map/ppermute | solution.py:396
  31.3 2.1 %assemble.1 = bf16[1,2,2048,256]{3,2,1,0:T(8,128)(2,1)} custom-call(s32[1,2]{1,0:T(1,128)S(1)} %copy-done.3, s32[1,2]{1,0:T(1,128)S(1)} %copy-done.4, s32[2]{0:T(128)S(1)} %get-tuple-element.44.refs_0_.refs_2_, bf16[2,256,256]{2,1,0:T(8,128)(2,1)S(1)} %get-tuple-element.67.refs_3_, bf16[2,256,256]{2,1,0:T(8,128)(2,1)S(1)} %collective-permute-done.5.refs_4_, ...), custom_call_target="tpu_custom_call" | custom-call | flops 1000000000 | bytes 3145752 | tf_op jit(solution)/shard_map/assemble/pallas_call | solution.py:362
  (1 shorter events, 0.0 us)
Async XLA Ops:
  0.0 7.9 %copy-start.3 = (s32[1,2]{1,0:T(1,128)S(1)}, s32[1,2]{1,0:T(1,128)}, u32[]{:S(2)}) copy-start(s32[1,2]{1,0:T(1,128)} %refs_0_.9) | copy-start | bytes 28
  0.0 7.9 %copy-start.4 = (s32[1,2]{1,0:T(1,128)S(1)}, s32[1,2]{1,0:T(1,128)}, u32[]{:S(2)}) copy-start(s32[1,2]{1,0:T(1,128)} %refs_1_.14) | copy-start | bytes 28
  0.0 7.9 %copy-start.1 = (f32[2,256,256]{2,1,0:T(8,128)S(1)}, f32[2,256,256]{2,1,0:T(8,128)}, u32[]{:S(2)}) copy-start(f32[2,256,256]{2,1,0:T(8,128)} %refs_2_.7) | copy-start | bytes 1572868
  0.0 7.9 %copy-start.2 = (f32[5]{0:T(128)S(1)}, f32[5]{0:T(128)}, u32[]{:S(2)}) copy-start(f32[5]{0:T(128)} %refs_1_.11) | copy-start | bytes 64
  0.0 9.2 %collective-permute-start.1 = (bf16[1,2,2048,256]{3,2,1,0:T(8,128)(2,1)}, bf16[1,2,2048,256]{3,2,1,0:T(8,128)(2,1)S(1)}, u32[]{:S(2)}, u32[]{:S(2)}) collective-permute-start(bf16[1,2,2048,256]{3,2,1,0:T(8,128)(2,1)} %refs_1_.12), channel_id=1, source_target_pairs={{0,64},{64,0},{1,65},{65,1},{2,66},{66,2},{3,67},{67,3},{4,68},{68... | collective-permute-start | bytes 6291464 | tf_op jit(solution)/shard_map/ppermute | solution.py:396
  4.3 4.9 %copy-start.7 = (bf16[1,2,256,256]{3,2,1,0:T(8,128)(2,1)S(1)}, bf16[1,2,256,256]{3,2,1,0:T(8,128)(2,1)}, u32[]{:S(2)}) copy-start(bf16[1,2,256,256]{3,2,1,0:T(8,128)(2,1)} %refs_3_.2) | copy-start | bytes 786436
  4.3 4.9 %copy-start.6 = (bf16[2,256,256]{2,1,0:T(8,128)(2,1)S(1)}, bf16[2,256,256]{2,1,0:T(8,128)(2,1)}, u32[]{:S(2)}) copy-start(bf16[2,256,256]{2,1,0:T(8,128)(2,1)} %get-tuple-element.39.refs_3_) | copy-start | bytes 786436
  4.3 10.0 %collective-permute-start = (bf16[80,128]{1,0:T(8,128)(2,1)}, bf16[80,128]{1,0:T(8,128)(2,1)S(1)}, u32[]{:S(2)}, u32[]{:S(2)}) collective-permute-start(bf16[80,128]{1,0:T(8,128)(2,1)} %get-tuple-element.38), channel_id=1, source_target_pairs={{0,1},{1,2},{2,3},{3,4},{4,5},{5,6},{6,7},{7,8},{8,9},{9,10},{10,1... | collective-permute-start | bytes 61448 | tf_op jit(solution)/shard_map/ppermute | solution.py:386
  5.7 12.0 %collective-permute-start.2 = (bf16[576,128]{1,0:T(8,128)(2,1)}, bf16[576,128]{1,0:T(8,128)(2,1)S(1)}, u32[]{:S(2)}, u32[]{:S(2)}) collective-permute-start(bf16[576,128]{1,0:T(8,128)(2,1)} %get-tuple-element.46), channel_id=1, source_target_pairs={{0,65},{1,66},{2,67},{3,68},{4,69},{5,70},{6,71},{7,72},{8,73},{9,... | collective-permute-start | bytes 442376 | tf_op jit(solution)/shard_map/ppermute | solution.py:393
  10.6 7.1 %copy-start = (bf16[1,2,2048,256]{3,2,1,0:T(8,128)(2,1)S(1)}, bf16[1,2,2048,256]{3,2,1,0:T(8,128)(2,1)}, u32[]{:S(2)}) copy-start(bf16[1,2,2048,256]{3,2,1,0:T(8,128)(2,1)} %refs_1_.12) | copy-start | bytes 6291460
  10.6 13.4 %collective-permute-start.4 = (bf16[1040,128]{1,0:T(8,128)(2,1)S(1)}, bf16[1040,128]{1,0:T(8,128)(2,1)S(1)}, u32[]{:S(2)}, u32[]{:S(2)}) collective-permute-start(bf16[1040,128]{1,0:T(8,128)(2,1)S(1)} %get-tuple-element.45.refs_0_), channel_id=1, source_target_pairs={{0,1},{1,2},{2,3},{3,4},{4,5},{5,6},{6,7},{7,8},{8,9},{9,10},{10,1... | collective-permute-start | bytes 798728 | tf_op jit(solution)/shard_map/ppermute | solution.py:386
  17.7 3.2 %copy-start.5 = (bf16[512,256]{1,0:T(8,128)(2,1)S(1)}, bf16[512,256]{1,0:T(8,128)(2,1)}, u32[]{:S(2)}) copy-start(bf16[512,256]{1,0:T(8,128)(2,1)} %constant.15.clone.refs_1_.refs_2_) | copy-start | bytes 786436
  19.1 7.9 %collective-permute-start.3 = (bf16[1056,128]{1,0:T(8,128)(2,1)S(1)}, bf16[1056,128]{1,0:T(8,128)(2,1)S(1)}, u32[]{:S(2)}, u32[]{:S(2)}) collective-permute-start(bf16[1056,128]{1,0:T(8,128)(2,1)S(1)} %get-tuple-element.50.refs_1_), channel_id=1, source_target_pairs={{0,63},{1,0},{2,1},{3,2},{4,3},{5,4},{6,5},{7,6},{8,7},{9,8},{10,9... | collective-permute-start | bytes 811016 | tf_op jit(solution)/shard_map/ppermute | solution.py:389
  26.0 4.1 %collective-permute-start.6 = (bf16[2,256,256]{2,1,0:T(8,128)(2,1)S(1)}, bf16[2,256,256]{2,1,0:T(8,128)(2,1)S(1)}, u32[]{:S(2)}, u32[]{:S(2)}) collective-permute-start(bf16[2,256,256]{2,1,0:T(8,128)(2,1)S(1)} %get-tuple-element.70), channel_id=1, source_target_pairs={{0,64},{64,0},{1,65},{65,1},{2,66},{66,2},{3,67},{67,3},{4,68},{68... | collective-permute-start | bytes 786440 | tf_op jit(solution)/shard_map/ppermute | solution.py:396
  29.0 2.3 %collective-permute-start.5 = (bf16[2,256,256]{2,1,0:T(8,128)(2,1)S(1)}, bf16[2,256,256]{2,1,0:T(8,128)(2,1)S(1)}, u32[]{:S(2)}, u32[]{:S(2)}) collective-permute-start(bf16[2,256,256]{2,1,0:T(8,128)(2,1)S(1)} %get-tuple-element.68), channel_id=1, source_target_pairs={{0,64},{64,0},{1,65},{65,1},{2,66},{66,2},{3,67},{67,3},{4,68},{68... | collective-permute-start | bytes 786440 | tf_op jit(solution)/shard_map/ppermute | solution.py:396

commit v3 on v2

--- a/solution.py
+++ b/solution.py
@@ -35,11 +35,12 @@
     return np.concatenate([cos, sin], axis=0)
 
 
-def place(slots, slot):
-    if len(slots) == 2:
-        return slots[0][0, slot], slots[1][0, slot]
-    value = slots[0][slot]
-    return value & 2047, value >> 11
+def place(strip, slot):
+    lane = iota((1, 128), 1)
+    values = strip[W // 4 :].astype(F32)[0:1]
+    row = jnp.sum(jnp.where(lane == slot * 4, values, jnp.where(lane == slot * 4 + 1, values * W, 0.0)))
+    col = jnp.sum(jnp.where(lane == slot * 4 + 2, values, 0.0))
+    return row.astype(jnp.int32), col.astype(jnp.int32)
 
 
 def span(row, height):
@@ -57,8 +58,8 @@
     a = (iota((W, 1), 0) - shift) & (W - 1)
     b = (iota((1, W), 1) - shift) & (W - 1)
     k = jnp.abs(a - b)
-    out = jnp.where(k == 0, taps[0], 0.0)
-    for distance in range(1, 5):
+    out = jnp.zeros((W, W), F32)
+    for distance in range(5):
         out = jnp.where(k == distance, taps[distance], out)
     return out.astype(BF)
 
@@ -80,16 +81,6 @@
     else:
         hit = iota((1, W), 1) == ((iota((W, 1), 0) - shift) & (W - 1))
     return jnp.where(hit, 1.0, 0.0).astype(BF)
-
-
-def rotate_probe(probe, from_row, to_col):
-    re, im = probe[0], probe[1]
-    hr, hi = re.astype(BF), im.astype(BF)
-    lr, li = (re - hr.astype(F32)).astype(BF), (im - hi.astype(F32)).astype(BF)
-    x = dot(from_row, jnp.concatenate([hr, hi, lr, li], axis=1)).astype(BF)
-    y = jnp.concatenate([x[:, i * W : (i + 1) * W] for i in range(4)], axis=0)
-    z = dot(y, to_col)
-    return z[0:W] + z[2 * W : 3 * W], z[W : 2 * W] + z[3 * W :]
 
 
 def forward(w0, w1, psi0, t_row, t_col):
@@ -139,58 +130,84 @@
     return {(s, i): part for s, i, part in out}
 
 
-def edges(pos_row, pos_col, tile, records, strip_keep, strip_send, keep, buf, buf_send, sems):
-    mine = lax.axis_index("depth")
-    work = []
-    for k, (slot, target, width) in enumerate(((mine, buf, W), (1 - mine, buf_send, 128))):
-        base, offset = span(pos_row[0, slot], tile.shape[2])
-        source = tile.at[0, :, pl.ds(base, SPAN), pl.ds(W - width, width)]
-        copy = pltpu.make_async_copy(source, target, sems.at[k])
+def edges(
+    pos_row, pos_col, chirp_taps, tile, records, strip_keep, strip_send, keep,
+    rows, cols, taps, record, buf, side_buf, packed, packed_send, window, sems,
+):
+    mine = lax.axis_index("depth")
+    height = tile.shape[2]
+    pairs = [(pos_row, rows), (pos_col, cols), (chirp_taps, taps), (records.at[0, 1 - mine], record)]
+    pairs += [(tile.at[0, i, :, pl.ds(W - 128, 128)], side_buf.at[i]) for i in range(2)]
+    copies = [pltpu.make_async_copy(source, target, sems.at[k]) for k, (source, target) in enumerate(pairs)]
+    for copy in copies:
         copy.start()
-        work.append((copy, offset))
-    record_copies = []
-    for half in range(2):
-        source = records.at[0, 1 - mine, :, pl.ds(half * 128, 128)]
-        target = strip_send.at[pl.ds(W // 4 + half * W, W), :]
-        record_copies.append(pltpu.make_async_copy(source, target, sems.at[2 + half]))
-        record_copies[-1].start()
+    last = []
+
+    def put(source, target):
+        last.append(pltpu.make_async_copy(source, target, sems.at[len(pairs) + 1 + len(last)]))
+        last[-1].start()
+
+    copies[0].wait()
+    base, offset = span(rows[0, mine], height)
+    base_send, offset_send = span(rows[0, 1 - mine], height)
+    whole = pltpu.make_async_copy(tile.at[0, :, pl.ds(base, SPAN), :], buf, sems.at[len(pairs)])
+    whole.start()
+    copies[1].wait()
+    copies[2].wait()
     lane = iota((STEP, 128), 1)
     numbers = jnp.zeros((STEP, 128), jnp.int32)
     for slot in range(2):
-        row, col = pos_row[0, slot], pos_col[0, slot]
+        row, col = rows[0, slot], cols[0, slot]
         for k, part in enumerate((row & (W - 1), row >> 8, col)):
             numbers = jnp.where(lane == slot * 4 + k, part, numbers)
-    strip_keep[W // 4 :] = numbers.astype(F32).astype(BF)
-    (copy, offset), (copy_send, offset_send) = work
-    copy.wait()
-    window = [fold(buf[i], offset) for i in range(2)]
-    keep[0], keep[1] = window[0].astype(BF), window[1].astype(BF)
-    strip_keep[: W // 4] = pack([part[:, W - 128 :] for part in window], [128 - LS] * 2, LS)
-    copy_send.wait()
-    strip_send[: W // 4] = pack([fold(buf_send[i], offset_send) for i in range(2)], [128 - LS] * 2, LS)
-    for copy in record_copies:
+    numbers = numbers.astype(F32)
+    for k in range(5):
+        numbers = jnp.where(lane == 8 + k, taps[k], numbers)
+    packed[W // 4 :] = numbers.astype(BF)
+    copies[3].wait()
+    put(record, strip_send.at[W // 8 :])
+    copies[4].wait()
+    copies[5].wait()
+    strip = pack([fold(side_buf[i, pl.ds(base_send, SPAN), :], offset_send) for i in range(2)], [128 - LS] * 2, LS)
+    packed_send[...] = jnp.concatenate([strip[: W // 8], strip[W // 8 :]], axis=1)
+    put(packed_send, strip_send.at[: W // 8])
+    packed[: W // 4] = pack([fold(side_buf[i, pl.ds(base, SPAN), :], offset) for i in range(2)], [128 - LS] * 2, LS)
+    put(packed, strip_keep)
+    whole.wait()
+    for i in range(2):
+        window[i] = fold(buf[i], offset).astype(BF)
+    put(window, keep)
+    for copy in last:
         copy.wait()
 
 
-def receive(strip, slots):
-    lane = iota((8, 128), 1)
-    values = strip[W // 4 :].astype(F32)[:8]
-    for slot in range(2):
-        weight = jnp.zeros((8, 128), F32)
-        for k, factor in enumerate((1, W, 2048)):
-            weight = jnp.where(lane == slot * 4 + k, factor / 8.0, weight)
-        slots[slot] = jnp.sum(values * weight).astype(jnp.int32)
-
-
-def settle(height, slots, taps, probe, psi0, t_row, t_col):
-    row, col0 = place(slots, lax.axis_index("depth"))
+def settle(taps, probe, offset, col0, psi0, t_row, t_col):
+    t_row[...], t_col[...] = taps_table(taps, offset), taps_table(taps, col0)
+    for i in range(2):
+        psi0[i] = pltpu.roll(pltpu.roll(probe[i], offset, 0), col0, 1)
+
+
+def settle_own(height, pos_row, pos_col, chirp_taps, probe, psi0, t_row, t_col, rows, cols, taps, sems):
+    mine = lax.axis_index("depth")
+    pairs = [(pos_row, rows), (pos_col, cols), (chirp_taps, taps)]
+    copies = [pltpu.make_async_copy(source, target, sems.at[k]) for k, (source, target) in enumerate(pairs)]
+    for copy in copies:
+        copy.start()
+    for copy in copies:
+        copy.wait()
+    _, offset = span(rows[0, mine], height)
+    settle(taps, probe, offset, cols[0, mine], psi0, t_row, t_col)
+
+
+def settle_left(height, strip, probe, psi0, t_row, t_col):
+    row, col0 = place(strip, lax.axis_index("depth"))
     _, offset = span(row, height)
-    t_row[...], t_col[...] = taps_table(taps, offset), taps_table(taps, col0)
-    psi0[0], psi0[1] = rotate_probe(probe, one_hot(offset, False), one_hot(col0, True))
-
-
-def tables(height, slots, dft, t_row, t_col, f_to, f_right, f_back, f_last):
-    row, col0 = place(slots, lax.axis_index("depth"))
+    numbers = strip[W // 4 :].astype(F32)[0:1]
+    settle([numbers[:, 8 + k : 9 + k] for k in range(5)], probe, offset, col0, psi0, t_row, t_col)
+
+
+def tables(height, strip, dft, t_row, t_col, f_to, f_right, f_back, f_last):
+    row, col0 = place(strip, lax.axis_index("depth"))
     _, offset = span(row, height)
     tall = dft[...]
     wide = jnp.concatenate([tall[:W], tall[W:]], axis=1)
@@ -218,9 +235,9 @@
             exit_ref[(2 * i + half) * W : (2 * i + half + 1) * W] = part[:, half * 128 : (half + 1) * 128]
 
 
-def left_forward(slots, counts, keep, other, psi0, t_row, t_col, exit_ref, w_ref, psi1_ref):
-    mine = lax.axis_index("depth")
-    row, col0 = place(slots, mine)
+def left_forward(strip, live, keep, other, psi0, t_row, t_col, exit_ref, w_ref, psi1_ref):
+    mine = lax.axis_index("depth")
+    row, col0 = place(strip, mine)
     base, offset = span(row, other.shape[2])
     column = iota((1, W), 1)
     inside = column >= col0
@@ -234,19 +251,20 @@
     psi1_ref[0], psi1_ref[1] = psi1
     put_exit(exit_ref, psi2, inside & (column < EDGE))
     number, lane = iota((STEP, 128), 0), iota((STEP, 128), 1)
-    live = jnp.where(mine < counts[0], 1.0, 0.0)
     marks = jnp.where(lane + jnp.where(number == 2, 128, 0) >= col0, 1.0, 0.0)
-    exit_ref[4 * W :] = jnp.where(number == 0, live, marks).astype(BF)
+    exit_ref[4 * W :] = jnp.where(number == 0, live[...], marks).astype(BF)
 
 
 def right_forward(
-    slots, tile, other, strip_a, strip_b, psi0, t_row, t_col, exit_ref, w_ref, psi1_ref
+    tile, other, strip_a, strip_b, psi0, t_row, t_col, exit_ref, w_ref, psi1_ref
 ):
     mine = lax.axis_index("depth")
-    row, col0 = place(slots, mine)
+    row, col0 = place(strip_a, mine)
     base, offset = span(row, tile.shape[2])
     lane, column = iota((1, 128), 1), iota((1, W), 1)
-    strips = pair(strip_a[: W // 4].astype(F32), strip_b[: W // 4].astype(F32), mine)
+    across = strip_b[: W // 8]
+    across = jnp.concatenate([across[:, :128], across[:, 128:]], axis=0)
+    strips = pair(strip_a[: W // 4].astype(F32), across.astype(F32), mine)
     w = windows_of(tile, other, mine, base, offset)
     for s in range(2):
         lefts = unpack(strips[s], [128 - LS] * 2, LS)
@@ -278,7 +296,7 @@
     x = dot(jnp.concatenate([x[:W], x[W:]], axis=1), f_right[...])
     fr, fi = x[:, :W], x[:, W:]
     if side == 1:
-        record = jnp.concatenate([record[W // 4 : W // 4 + W], record[W // 4 + W :]], axis=1)
+        record = record[W // 8 :]
     misfit = (fr * fr + fi * fi - record[...].astype(F32)) * live
     x = dot(f_back[...], jnp.concatenate([(misfit * fr).astype(BF), (misfit * fi).astype(BF)], axis=0)).astype(BF)
     x = dot(jnp.concatenate([x[:W], x[W:]], axis=1), f_last[...])
@@ -340,7 +358,6 @@
         copy.wait()
 
 
-SMEM = pl.BlockSpec(memory_space=pltpu.SMEM)
 VMEM = pl.BlockSpec(memory_space=pltpu.VMEM)
 HBM = pl.BlockSpec(memory_space=pltpu.HBM)
 
@@ -373,7 +390,7 @@
 
 FIELD, WAVE = ((2, W, W), BF), ((2, W, W), F32)
 BAND, QUAD = ((W, W), BF), ((2 * W, 2 * W), BF)
-MARKED, LOADED, SLOTS = ((W // 4 + STEP, 128), BF), ((W // 4 + 2 * W, 128), BF), ((2,), jnp.int32)
+MARKED, LOADED = ((W // 4 + STEP, 128), BF), ((W // 8 + W, W), BF)
 EXIT_L, EXIT_R = ((4 * W + STEP, 128), BF), ((4 * W + W * 4 * RS // 128, 128), BF)
 
 
@@ -395,21 +412,14 @@
     def to_other(x):
         return lax.ppermute(x, "depth", [(0, 1), (1, 0)])
 
-    def own(kernel):
-        return lambda pos_row, pos_col, *refs: kernel((pos_row, pos_col), *refs)
-
-    def left(kernel):
-        return lambda slots, *refs: kernel((slots,), *refs)
-
     def table_kernel(*refs):
         tables(height, *refs)
 
-    def settle_own(*refs):
-        settle(height, *refs)
-
-    def settle_left(strip, taps, probe, slots, *refs):
-        receive(strip, slots)
-        settle(height, (slots,), taps, probe, *refs)
+    def settle_own_kernel(*refs):
+        settle_own(height, *refs)
+
+    def settle_left_kernel(*refs):
+        settle_left(height, *refs)
 
     def terms(side, *args, after=(), token=False):
         def kernel(*refs):
@@ -422,37 +432,40 @@
     dft = jnp.asarray(dft_tables(), BF)
     other_tile = to_other(transmission)
     record = lax.dynamic_index_in_dim(records[0], my_depth, 0, keepdims=False)
+    scratch = [pltpu.SMEM((1, 2), jnp.int32)] * 2 + [pltpu.SMEM((5,), F32)]
+    for shape in ((W, W), (2, SPAN, W), (2, height, 128), MARKED[0], (W // 8, W), (2, W, W)):
+        scratch.append(pltpu.VMEM(shape, BF))
     strip_keep, strip_send, keep = call(
-        edges, "edges", [SMEM, SMEM, HBM, HBM], [MARKED, LOADED, FIELD],
-        [pos_row, pos_col, transmission, records],
-        [pltpu.VMEM((2, SPAN, W), BF), pltpu.VMEM((2, SPAN, 128), BF), pltpu.SemaphoreType.DMA((4,))], vmem=56,
+        edges, "edges", [HBM] * 5, [MARKED, LOADED, FIELD],
+        [pos_row, pos_col, chirp_taps, transmission, records],
+        scratch + [pltpu.SemaphoreType.DMA((11,))], out_specs=[HBM] * 3, vmem=56,
     )
     strip_a = to_right(strip_keep)
     strip_b = to_right_other(strip_send)
+    live = jnp.broadcast_to((my_depth < counts[0]).astype(F32), (STEP, 128))
     settled = call(
-        own(settle_own), "settle", [SMEM, SMEM, SMEM, VMEM], [WAVE, BAND, BAND],
-        [pos_row, pos_col, chirp_taps, probe_field],
+        settle_own_kernel, "settle", [HBM] * 3 + [VMEM], [WAVE, BAND, BAND],
+        [pos_row, pos_col, chirp_taps, probe_field], scratch[:3] + [pltpu.SemaphoreType.DMA((3,))],
     )
     exit_l, w1, psi1, done = call(
-        own(left_forward), "left_forward", [SMEM] * 3 + [VMEM] * 5, [EXIT_L, FIELD, FIELD],
-        [pos_row, pos_col, counts, keep, other_tile, *settled], token=True,
+        left_forward, "left_forward", [VMEM] * 7, [EXIT_L, FIELD, FIELD],
+        [strip_keep, live, keep, other_tile, *settled], token=True,
     )
     exit_l_left = to_right(exit_l)
-    slots_left, *settled_left = call(
-        settle_left, "settle_left", [VMEM, SMEM, VMEM], [SLOTS, WAVE, BAND, BAND],
-        [strip_a, chirp_taps, probe_field], out_specs=[SMEM] + [VMEM] * 3, after=[done],
+    settled_left = call(
+        settle_left_kernel, "settle_left", [VMEM] * 2, [WAVE, BAND, BAND], [strip_a, probe_field], after=[done]
     )
     exit_r_left, w_left, psi1_left, done = call(
-        left(right_forward), "right_forward", [SMEM] + [VMEM] * 7, [EXIT_R, FIELD, FIELD],
-        [slots_left, transmission, other_tile, strip_a, strip_b, *settled_left], token=True,
+        right_forward, "right_forward", [VMEM] * 7, [EXIT_R, FIELD, FIELD],
+        [transmission, other_tile, strip_a, strip_b, *settled_left], token=True,
     )
     exit_r = to_left(exit_r_left)
     *left_tables, done = call(
-        left(table_kernel), "tables_left", [SMEM] + [VMEM] * 3, [QUAD] * 4, [slots_left, dft, *settled_left[1:]],
+        table_kernel, "tables_left", [VMEM] * 4, [QUAD] * 4, [strip_a, dft, *settled_left[1:]],
         after=[done], token=True,
     )
     *own_tables, done = call(
-        own(table_kernel), "tables", [SMEM] * 2 + [VMEM] * 3, [QUAD] * 4, [pos_row, pos_col, dft, *settled[1:]],
+        table_kernel, "tables", [VMEM] * 4, [QUAD] * 4, [strip_keep, dft, *settled[1:]],
         after=[done], token=True,
     )
     r_keep, r_send, done = terms(
@@ -462,12 +475,9 @@
     l_keep, l_send = terms(0, exit_l, exit_r, record, *settled, *own_tables, psi1, w1, after=[done])
     l_recv = to_other(l_send)
 
-    def assemble_kernel(pos_row, pos_col, slots, *refs):
-        assemble((pos_row, pos_col), (slots,), *refs)
-
     return call(
-        assemble_kernel, "assemble", [SMEM] * 3 + [VMEM] * 4, [(transmission.shape, BF)],
-        [pos_row, pos_col, slots_left, l_keep, l_recv, r_keep, r_recv],
+        assemble, "assemble", [VMEM] * 6, [(transmission.shape, BF)],
+        [strip_keep, strip_a, l_keep, l_recv, r_keep, r_recv],
         [pltpu.VMEM((2, height, W), BF), pltpu.SemaphoreType.DMA((2, 4))], out_specs=[HBM],
     )[0]
 

time: 33.5 us -> 32.3 us (0.964)
  Pallas kernels: 17 us -> 13.6 us
  waiting for transfers between devices: 6.19 us -> 8.49 us
    pallas_call x10, Pallas kernels: 17 us -> 13.6 us  [call(): pl.pallas_call(body, name=name, out_shape=[jax.ShapeDtypeStruct(shape, ki...]
    ppermute x2, waiting for transfers between devices: 3.03 us -> 4.07 us  [to_right(): return lax.ppermute(x, 'tile', [(i, (i + 1) % tiles) for i in range(tiles)])]
    ppermute x1, waiting for transfers between devices: 1.99 us -> 2.66 us  [to_right_other(): return lax.ppermute(x, ('depth', 'tile'), pairs)]
    ppermute x1, waiting for transfers between devices: 0.01 us -> 0.59 us  [to_left(): return lax.ppermute(x, 'tile', [(i, (i - 1) % tiles) for i in range(tiles)])]
    ppermute x3, starting transfers between devices: 3.61 us -> 3.08 us  [to_other(): return lax.ppermute(x, 'depth', [(0, 1), (1, 0)])]
    ppermute x1, starting transfers between devices: 1.75 us -> 2.09 us  [to_left(): return lax.ppermute(x, 'tile', [(i, (i - 1) % tiles) for i in range(tiles)])]
  transfers between devices with their start and end apart: 7 -> 7, of which waited for: 4 -> 5; matrix products, arithmetic and copies ran while one was open for 0% -> 0% of each run, Pallas kernels for 45% -> 38%
where the time goes in v3:
time: 32.3 us; the launch traced here: 32.1 us
  Pallas kernels  13.6 us (42%)
  starting transfers between devices  9.07 us (28%)
  waiting for transfers between devices  8.49 us (26%)
  between operations  0.85 us (3%)
    pallas_call x10, Pallas kernels, call(): pl.pallas_call(body, name=name, out_shape=[jax.ShapeDtypeStruct(shape, ki...  13.6 us
    ppermute x2, waiting for transfers between devices, to_right(): return lax.ppermute(x, 'tile', [(i, (i + 1) % tiles) for i in range(tiles)])  4.07 us
    ppermute x3, starting transfers between devices, to_other(): return lax.ppermute(x, 'depth', [(0, 1), (1, 0)])  3.08 us
    ppermute x1, waiting for transfers between devices, to_right_other(): return lax.ppermute(x, ('depth', 'tile'), pairs)  2.66 us
    ppermute x2, starting transfers between devices, to_right(): return lax.ppermute(x, 'tile', [(i, (i + 1) % tiles) for i in range(tiles)])  2.36 us
    ppermute x1, starting transfers between devices, to_left(): return lax.ppermute(x, 'tile', [(i, (i - 1) % tiles) for i in range(tiles)])  2.09 us
    ppermute x1, starting transfers between devices, to_right_other(): return lax.ppermute(x, ('depth', 'tile'), pairs)  1.54 us
    ppermute x3, waiting for transfers between devices, to_other(): return lax.ppermute(x, 'depth', [(0, 1), (1, 0)])  1.16 us
  transfers between devices with their start and end apart: 7, of which 5 were waited for; matrix products, arithmetic and copies ran while one was open for 0% of the time, Pallas kernels for 38%

profile of v3, /device:TPU:1, one launch (start us, length us, event | category | flops | bytes accessed | tf_op | source)
XLA Modules:
  0.0 32.1 jit_solution(1613852529124281540)
XLA Ops:
  0.0 0.0 copy-start.3
  0.0 0.0 copy-start.4
  0.0 0.0 copy-start.5
  0.0 0.0 copy-start.1
  0.0 1.5 %collective-permute-start.1 = (bf16[1,2,2048,256]{3,2,1,0:T(8,128)(2,1)}, bf16[1,2,2048,256]{3,2,1,0:T(8,128)(2,1)S(1)}, u32[]{:S(2)}, u32[]{:S(2)}) collective-permute-start(bf16[1,2,2048,256]{3,2,1,0:T(8,128)(2,1)} %refs_0_.5), channel_id=1, source_target_pairs={{0,64},{64,0},{1,65},{65,1},{2,66},{66,2},{3,67},{67,3},{4,68},{68... | collective-permute-start | bytes 6291464 | tf_op jit(solution)/shard_map/ppermute | solution.py:413
  1.5 2.5 %edges.1 = (bf16[80,128]{1,0:T(8,128)(2,1)}, bf16[288,256]{1,0:T(8,128)(2,1)}, bf16[2,256,256]{2,1,0:T(8,128)(2,1)}) custom-call(s32[1,2]{1,0:T(1,128)} %refs_0_.4, s32[1,2]{1,0:T(1,128)} %refs_1_.6, f32[5]{0:T(128)} %refs_2_.3, bf16[1,2,2048,256]{3,2,1,0:T(8,128)(2,1)} %refs_0_.5, bf16[1,2,256,256]{3,2,1,0:T(8,128)(2,1)} %refs_4_.1), custom_call_target="tpu_custom_call" | custom-call | flops 1000000000 | bytes 430080 | tf_op jit(solution)/shard_map/edges/pallas_call | solution.py:379
  4.0 0.0 copy-start.8
  4.1 0.0 copy-start.2
  4.1 0.0 copy-start.7
  4.1 1.4 %collective-permute-start = (bf16[80,128]{1,0:T(8,128)(2,1)}, bf16[80,128]{1,0:T(8,128)(2,1)S(1)}, u32[]{:S(2)}, u32[]{:S(2)}) collective-permute-start(bf16[80,128]{1,0:T(8,128)(2,1)} %get-tuple-element.37.refs_0_), channel_id=1, source_target_pairs={{0,1},{1,2},{2,3},{3,4},{4,5},{5,6},{6,7},{7,8},{8,9},{9,10},{10,1... | collective-permute-start | bytes 61448 | tf_op jit(solution)/shard_map/ppermute | solution.py:403
  5.5 1.5 %collective-permute-start.2 = (bf16[288,256]{1,0:T(8,128)(2,1)}, bf16[288,256]{1,0:T(8,128)(2,1)S(1)}, u32[]{:S(2)}, u32[]{:S(2)}) collective-permute-start(bf16[288,256]{1,0:T(8,128)(2,1)} %get-tuple-element.43), channel_id=1, source_target_pairs={{0,65},{1,66},{2,67},{3,68},{4,69},{5,70},{6,71},{7,72},{8,73},{9,... | collective-permute-start | bytes 442376 | tf_op jit(solution)/shard_map/ppermute | solution.py:410
  7.7 0.0 copy-done.3
  7.7 0.0 copy-done.4
  7.7 0.0 copy-done.5
  7.7 0.0 copy-done.1
  7.7 1.1 %settle.1 = (f32[2,256,256]{2,1,0:T(8,128)S(1)}, bf16[256,256]{1,0:T(8,128)(2,1)S(1)}, bf16[256,256]{1,0:T(8,128)(2,1)S(1)}) custom-call(s32[1,2]{1,0:T(1,128)S(1)} %copy-done.3, s32[1,2]{1,0:T(1,128)S(1)} %copy-done.4, f32[5]{0:T(128)S(1)} %copy-done.5, f32[2,256,256]{2,1,0:T(8,128)S(1)} %copy-done.1), custom_call_target="tpu_custom_call" | custom-call | flops 1000000000 | bytes 1310720 | tf_op jit(solution)/shard_map/settle/pallas_call | solution.py:379
  8.8 0.0 copy-done.8
  8.8 0.0 collective-permute-done.1.refs_3_.refs_1_
  8.8 0.0 copy-done.2
  8.8 0.0 copy-done.7
  8.9 0.9 %left_forward.1 = (bf16[1040,128]{1,0:T(8,128)(2,1)S(1)}, bf16[2,256,256]{2,1,0:T(8,128)(2,1)S(1)}, bf16[2,256,256]{2,1,0:T(8,128)(2,1)S(1)}, f32[8,128]{1,0:T(8,128)S(1)}) custom-call(bf16[80,128]{1,0:T(8,128)(2,1)S(1)} %copy-done.2, f32[16,128]{1,0:T(8,128)S(1)} %broadcast_in_dim.3.refs_1_, bf16[2,256,256]{2,1,0:T(8,128)(2,1)S(1)} %copy-done.7, ...), custom_call_target="tpu_custom_call" | custom-call | flops 1000000000 | bytes 3969024 | tf_op jit(solution)/shard_map/left_forward/pallas_call | solution.py:379
  9.7 0.0 copy-start
  9.8 1.0 %collective-permute-start.4 = (bf16[1040,128]{1,0:T(8,128)(2,1)S(1)}, bf16[1040,128]{1,0:T(8,128)(2,1)S(1)}, u32[]{:S(2)}, u32[]{:S(2)}) collective-permute-start(bf16[1040,128]{1,0:T(8,128)(2,1)S(1)} %get-tuple-element.42.refs_0_), channel_id=1, source_target_pairs={{0,1},{1,2},{2,3},{3,4},{4,5},{5,6},{6,7},{7,8},{8,9},{9,10},{10,1... | collective-permute-start | bytes 798728 | tf_op jit(solution)/shard_map/ppermute | solution.py:403
  10.7 3.3 %collective-permute-done.refs_0_.refs_2_.refs_1_ = bf16[80,128]{1,0:T(8,128)(2,1)S(1)} collective-permute-done((bf16[80,128]{1,0:T(8,128)(2,1)}, bf16[80,128]{1,0:T(8,128)(2,1)S(1)}, u32[]{:S(2)}, u32[]{:S(2)}) %collective-permute-start) | collective-permute-done | bytes 20512 | tf_op jit(solution)/shard_map/ppermute | solution.py:403
  14.0 0.7 %settle_left.1 = (f32[2,256,256]{2,1,0:T(8,128)S(1)}, bf16[256,256]{1,0:T(8,128)(2,1)S(1)}, bf16[256,256]{1,0:T(8,128)(2,1)S(1)}) custom-call(bf16[80,128]{1,0:T(8,128)(2,1)S(1)} %collective-permute-done.refs_0_.refs_2_.refs_1_, f32[2,256,256]{2,1,0:T(8,128)S(1)} %copy-done.1, f32[8,128]{1,0:T(8,128)S(1)} %get-tuple-element.44.refs_2_), custom_call_target="tpu_custom_call" | custom-call | flops 1000000000 | bytes 1331200 | tf_op jit(solution)/shard_map/settle_left/pallas_call | solution.py:379
  14.8 2.7 %collective-permute-done.2.refs_3_.refs_2_ = bf16[288,256]{1,0:T(8,128)(2,1)S(1)} collective-permute-done((bf16[288,256]{1,0:T(8,128)(2,1)}, bf16[288,256]{1,0:T(8,128)(2,1)S(1)}, u32[]{:S(2)}, u32[]{:S(2)}) %collective-permute-start.2) | collective-permute-done | bytes 147488 | tf_op jit(solution)/shard_map/ppermute | solution.py:410
  17.4 0.0 copy-done
  17.4 0.0 copy-start.6
  17.4 0.9 %right_forward.1 = (bf16[1056,128]{1,0:T(8,128)(2,1)S(1)}, bf16[2,256,256]{2,1,0:T(8,128)(2,1)S(1)}, bf16[2,256,256]{2,1,0:T(8,128)(2,1)S(1)}, f32[8,128]{1,0:T(8,128)S(1)}) custom-call(bf16[1,2,2048,256]{3,2,1,0:T(8,128)(2,1)S(1)} %copy-done, bf16[1,2,2048,256]{3,2,1,0:T(8,128)(2,1)S(1)} %collective-permute-done.1.refs_3_.refs_1_, ...), custom_call_target="tpu_custom_call" | custom-call | flops 1000000000 | bytes 5947392 | tf_op jit(solution)/shard_map/right_forward/pallas_call | solution.py:379
  18.3 2.1 %collective-permute-start.3 = (bf16[1056,128]{1,0:T(8,128)(2,1)S(1)}, bf16[1056,128]{1,0:T(8,128)(2,1)S(1)}, u32[]{:S(2)}, u32[]{:S(2)}) collective-permute-start(bf16[1056,128]{1,0:T(8,128)(2,1)S(1)} %get-tuple-element.48.refs_1_), channel_id=1, source_target_pairs={{0,63},{1,0},{2,1},{3,2},{4,3},{5,4},{6,5},{7,6},{8,7},{9,8},{10,9... | collective-permute-start | bytes 811016 | tf_op jit(solution)/shard_map/ppermute | solution.py:406
  20.4 0.0 copy-done.6
  20.4 1.0 %tables_left.1 = (bf16[512,512]{1,0:T(8,128)(2,1)S(1)}, bf16[512,512]{1,0:T(8,128)(2,1)S(1)}, bf16[512,512]{1,0:T(8,128)(2,1)S(1)}, bf16[512,512]{1,0:T(8,128)(2,1)S(1)}, f32[8,128]{1,0:T(8,128)S(1)}) custom-call(bf16[80,128]{1,0:T(8,128)(2,1)S(1)} %collective-permute-done.refs_0_.refs_2_.refs_1_, bf16[512,256]{1,0:T(8,128)(2,1)S(1)} %copy-done.6, ...), custom_call_target="tpu_custom_call" | custom-call | flops 1000000000 | bytes 2646016 | tf_op jit(solution)/shard_map/tables_left/pallas_call | solution.py:379
  21.4 1.0 %tables.1 = (bf16[512,512]{1,0:T(8,128)(2,1)S(1)}, bf16[512,512]{1,0:T(8,128)(2,1)S(1)}, bf16[512,512]{1,0:T(8,128)(2,1)S(1)}, bf16[512,512]{1,0:T(8,128)(2,1)S(1)}, f32[8,128]{1,0:T(8,128)S(1)}) custom-call(bf16[80,128]{1,0:T(8,128)(2,1)S(1)} %copy-done.2, bf16[512,256]{1,0:T(8,128)(2,1)S(1)} %copy-done.6, ...), custom_call_target="tpu_custom_call" | custom-call | flops 1000000000 | bytes 2646016 | tf_op jit(solution)/shard_map/tables/pallas_call | solution.py:379
  22.4 0.8 %collective-permute-done.4.refs_0_ = bf16[1040,128]{1,0:T(8,128)(2,1)S(1)} collective-permute-done((bf16[1040,128]{1,0:T(8,128)(2,1)S(1)}, bf16[1040,128]{1,0:T(8,128)(2,1)S(1)}, u32[]{:S(2)}, u32[]{:S(2)}) %collective-permute-start.4) | collective-permute-done | bytes 266272 | tf_op jit(solution)/shard_map/ppermute | solution.py:403
  23.2 2.0 %far_field_1.1 = (bf16[2,256,256]{2,1,0:T(8,128)(2,1)S(1)}, bf16[2,256,256]{2,1,0:T(8,128)(2,1)S(1)}, f32[8,128]{1,0:T(8,128)S(1)}) custom-call(bf16[1040,128]{1,0:T(8,128)(2,1)S(1)} %collective-permute-done.4.refs_0_, bf16[1056,128]{1,0:T(8,128)(2,1)S(1)} %get-tuple-element.48.refs_1_, bf16[288,256]{1,0:T(8,128)(2,1)S(1)} %collective-permute-done.2.refs_3_.refs_2_, ...), custom_call_target="tpu_custom_call" | custom-call | flops 1000000000 | bytes 4620288 | tf_op jit(solution)/shard_map/far_field_1/pallas_call | solution.py:379
  25.2 0.9 %collective-permute-start.6 = (bf16[2,256,256]{2,1,0:T(8,128)(2,1)S(1)}, bf16[2,256,256]{2,1,0:T(8,128)(2,1)S(1)}, u32[]{:S(2)}, u32[]{:S(2)}) collective-permute-start(bf16[2,256,256]{2,1,0:T(8,128)(2,1)S(1)} %get-tuple-element.68), channel_id=1, source_target_pairs={{0,64},{64,0},{1,65},{65,1},{2,66},{66,2},{3,67},{67,3},{4,68},{68... | collective-permute-start | bytes 786440 | tf_op jit(solution)/shard_map/ppermute | solution.py:413
  26.1 0.6 %collective-permute-done.3.refs_1_ = bf16[1056,128]{1,0:T(8,128)(2,1)S(1)} collective-permute-done((bf16[1056,128]{1,0:T(8,128)(2,1)S(1)}, bf16[1056,128]{1,0:T(8,128)(2,1)S(1)}, u32[]{:S(2)}, u32[]{:S(2)}) %collective-permute-start.3) | collective-permute-done | bytes 270368 | tf_op jit(solution)/shard_map/ppermute | solution.py:406
  26.7 2.0 %far_field_0.1 = (bf16[2,256,256]{2,1,0:T(8,128)(2,1)S(1)}, bf16[2,256,256]{2,1,0:T(8,128)(2,1)S(1)}) custom-call(bf16[1040,128]{1,0:T(8,128)(2,1)S(1)} %get-tuple-element.42.refs_0_, bf16[1056,128]{1,0:T(8,128)(2,1)S(1)} %collective-permute-done.3.refs_1_, bf16[256,256]{1,0:T(8,128)(2,1)S(1)} %dynamic-slice_bitcast_fusion.refs_2_, ...), custom_call_target="tpu_custom_call" | custom-call | flops 1000000000 | bytes 4599808 | tf_op jit(solution)/shard_map/far_field_0/pallas_call | solution.py:379
  28.7 0.7 %collective-permute-start.5 = (bf16[2,256,256]{2,1,0:T(8,128)(2,1)S(1)}, bf16[2,256,256]{2,1,0:T(8,128)(2,1)S(1)}, u32[]{:S(2)}, u32[]{:S(2)}) collective-permute-start(bf16[2,256,256]{2,1,0:T(8,128)(2,1)S(1)} %get-tuple-element.66), channel_id=1, source_target_pairs={{0,64},{64,0},{1,65},{65,1},{2,66},{66,2},{3,67},{67,3},{4,68},{68... | collective-permute-start | bytes 786440 | tf_op jit(solution)/shard_map/ppermute | solution.py:413
  29.4 0.0 collective-permute-done.6.refs_5_
  29.4 1.2 %collective-permute-done.5.refs_3_ = bf16[2,256,256]{2,1,0:T(8,128)(2,1)S(1)} collective-permute-done((bf16[2,256,256]{2,1,0:T(8,128)(2,1)S(1)}, bf16[2,256,256]{2,1,0:T(8,128)(2,1)S(1)}, u32[]{:S(2)}, u32[]{:S(2)}) %collective-permute-start.5) | collective-permute-done | bytes 262176 | tf_op jit(solution)/shard_map/ppermute | solution.py:413
  30.5 1.6 %assemble.1 = bf16[1,2,2048,256]{3,2,1,0:T(8,128)(2,1)} custom-call(bf16[80,128]{1,0:T(8,128)(2,1)S(1)} %copy-done.2, bf16[80,128]{1,0:T(8,128)(2,1)S(1)} %collective-permute-done.refs_0_.refs_2_.refs_1_, bf16[2,256,256]{2,1,0:T(8,128)(2,1)S(1)} %get-tuple-element.65.refs_2_, bf16[2,256,256]{2,1,0:T(8,128)(2,1)S(1)} %collective-permute-done.5.refs_3_, ...), custom_call_target="tpu_custom_call" | custom-call | flops 1000000000 | bytes 3186688 | tf_op jit(solution)/shard_map/assemble/pallas_call | solution.py:379
  (2 shorter events, 0.0 us)
Async XLA Ops:
  0.0 7.7 %copy-start.3 = (s32[1,2]{1,0:T(1,128)S(1)}, s32[1,2]{1,0:T(1,128)}, u32[]{:S(2)}) copy-start(s32[1,2]{1,0:T(1,128)} %refs_0_.4) | copy-start | bytes 28
  0.0 7.7 %copy-start.4 = (s32[1,2]{1,0:T(1,128)S(1)}, s32[1,2]{1,0:T(1,128)}, u32[]{:S(2)}) copy-start(s32[1,2]{1,0:T(1,128)} %refs_1_.6) | copy-start | bytes 28
  0.0 7.7 %copy-start.5 = (f32[5]{0:T(128)S(1)}, f32[5]{0:T(128)}, u32[]{:S(2)}) copy-start(f32[5]{0:T(128)} %refs_2_.3) | copy-start | bytes 64
  0.0 7.7 %copy-start.1 = (f32[2,256,256]{2,1,0:T(8,128)S(1)}, f32[2,256,256]{2,1,0:T(8,128)}, u32[]{:S(2)}) copy-start(f32[2,256,256]{2,1,0:T(8,128)} %refs_1_.7) | copy-start | bytes 1572868
  0.0 8.8 %collective-permute-start.1 = (bf16[1,2,2048,256]{3,2,1,0:T(8,128)(2,1)}, bf16[1,2,2048,256]{3,2,1,0:T(8,128)(2,1)S(1)}, u32[]{:S(2)}, u32[]{:S(2)}) collective-permute-start(bf16[1,2,2048,256]{3,2,1,0:T(8,128)(2,1)} %refs_0_.5), channel_id=1, source_target_pairs={{0,64},{64,0},{1,65},{65,1},{2,66},{66,2},{3,67},{67,3},{4,68},{68... | collective-permute-start | bytes 6291464 | tf_op jit(solution)/shard_map/ppermute | solution.py:413
  4.0 4.7 %copy-start.8 = (bf16[1,2,256,256]{3,2,1,0:T(8,128)(2,1)S(1)}, bf16[1,2,256,256]{3,2,1,0:T(8,128)(2,1)}, u32[]{:S(2)}) copy-start(bf16[1,2,256,256]{3,2,1,0:T(8,128)(2,1)} %refs_4_.1) | copy-start | bytes 786436
  4.1 4.8 %copy-start.2 = (bf16[80,128]{1,0:T(8,128)(2,1)S(1)}, bf16[80,128]{1,0:T(8,128)(2,1)}, u32[]{:S(2)}) copy-start(bf16[80,128]{1,0:T(8,128)(2,1)} %get-tuple-element.37.refs_0_) | copy-start | bytes 61444
  4.1 4.8 %copy-start.7 = (bf16[2,256,256]{2,1,0:T(8,128)(2,1)S(1)}, bf16[2,256,256]{2,1,0:T(8,128)(2,1)}, u32[]{:S(2)}) copy-start(bf16[2,256,256]{2,1,0:T(8,128)(2,1)} %get-tuple-element.38.refs_2_) | copy-start | bytes 786436
  4.1 10.0 %collective-permute-start = (bf16[80,128]{1,0:T(8,128)(2,1)}, bf16[80,128]{1,0:T(8,128)(2,1)S(1)}, u32[]{:S(2)}, u32[]{:S(2)}) collective-permute-start(bf16[80,128]{1,0:T(8,128)(2,1)} %get-tuple-element.37.refs_0_), channel_id=1, source_target_pairs={{0,1},{1,2},{2,3},{3,4},{4,5},{5,6},{6,7},{7,8},{8,9},{9,10},{10,1... | collective-permute-start | bytes 61448 | tf_op jit(solution)/shard_map/ppermute | solution.py:403
  5.5 12.0 %collective-permute-start.2 = (bf16[288,256]{1,0:T(8,128)(2,1)}, bf16[288,256]{1,0:T(8,128)(2,1)S(1)}, u32[]{:S(2)}, u32[]{:S(2)}) collective-permute-start(bf16[288,256]{1,0:T(8,128)(2,1)} %get-tuple-element.43), channel_id=1, source_target_pairs={{0,65},{1,66},{2,67},{3,68},{4,69},{5,70},{6,71},{7,72},{8,73},{9,... | collective-permute-start | bytes 442376 | tf_op jit(solution)/shard_map/ppermute | solution.py:410
  9.7 7.7 %copy-start = (bf16[1,2,2048,256]{3,2,1,0:T(8,128)(2,1)S(1)}, bf16[1,2,2048,256]{3,2,1,0:T(8,128)(2,1)}, u32[]{:S(2)}) copy-start(bf16[1,2,2048,256]{3,2,1,0:T(8,128)(2,1)} %refs_0_.5) | copy-start | bytes 6291460
  9.8 13.5 %collective-permute-start.4 = (bf16[1040,128]{1,0:T(8,128)(2,1)S(1)}, bf16[1040,128]{1,0:T(8,128)(2,1)S(1)}, u32[]{:S(2)}, u32[]{:S(2)}) collective-permute-start(bf16[1040,128]{1,0:T(8,128)(2,1)S(1)} %get-tuple-element.42.refs_0_), channel_id=1, source_target_pairs={{0,1},{1,2},{2,3},{3,4},{4,5},{5,6},{6,7},{7,8},{8,9},{9,10},{10,1... | collective-permute-start | bytes 798728 | tf_op jit(solution)/shard_map/ppermute | solution.py:403
  17.4 3.0 %copy-start.6 = (bf16[512,256]{1,0:T(8,128)(2,1)S(1)}, bf16[512,256]{1,0:T(8,128)(2,1)}, u32[]{:S(2)}) copy-start(bf16[512,256]{1,0:T(8,128)(2,1)} %constant.15.clone.refs_1_) | copy-start | bytes 786436
  18.3 8.4 %collective-permute-start.3 = (bf16[1056,128]{1,0:T(8,128)(2,1)S(1)}, bf16[1056,128]{1,0:T(8,128)(2,1)S(1)}, u32[]{:S(2)}, u32[]{:S(2)}) collective-permute-start(bf16[1056,128]{1,0:T(8,128)(2,1)S(1)} %get-tuple-element.48.refs_1_), channel_id=1, source_target_pairs={{0,63},{1,0},{2,1},{3,2},{4,3},{5,4},{6,5},{7,6},{8,7},{9,8},{10,9... | collective-permute-start | bytes 811016 | tf_op jit(solution)/shard_map/ppermute | solution.py:406
  25.2 4.2 %collective-permute-start.6 = (bf16[2,256,256]{2,1,0:T(8,128)(2,1)S(1)}, bf16[2,256,256]{2,1,0:T(8,128)(2,1)S(1)}, u32[]{:S(2)}, u32[]{:S(2)}) collective-permute-start(bf16[2,256,256]{2,1,0:T(8,128)(2,1)S(1)} %get-tuple-element.68), channel_id=1, source_target_pairs={{0,64},{64,0},{1,65},{65,1},{2,66},{66,2},{3,67},{67,3},{4,68},{68... | collective-permute-start | bytes 786440 | tf_op jit(solution)/shard_map/ppermute | solution.py:413
  28.7 1.8 %collective-permute-start.5 = (bf16[2,256,256]{2,1,0:T(8,128)(2,1)S(1)}, bf16[2,256,256]{2,1,0:T(8,128)(2,1)S(1)}, u32[]{:S(2)}, u32[]{:S(2)}) collective-permute-start(bf16[2,256,256]{2,1,0:T(8,128)(2,1)S(1)} %get-tuple-element.66), channel_id=1, source_target_pairs={{0,64},{64,0},{1,65},{65,1},{2,66},{66,2},{3,67},{67,3},{4,68},{68... | collective-permute-start | bytes 786440 | tf_op jit(solution)/shard_map/ppermute | solution.py:413

commit v4 on v3

--- a/solution.py
+++ b/solution.py
@@ -13,6 +13,7 @@
 SPAN = W + STEP
 LS = 16
 RS = 4
+EARLY = 48
 EDGE = W - 8
 BF = jnp.bfloat16
 F32 = jnp.float32
@@ -136,7 +137,7 @@
 ):
     mine = lax.axis_index("depth")
     height = tile.shape[2]
-    pairs = [(pos_row, rows), (pos_col, cols), (chirp_taps, taps), (records.at[0, 1 - mine], record)]
+    pairs = [(pos_row, rows), (pos_col, cols), (chirp_taps, taps), (records.at[0, 1 - mine, EARLY:], record)]
     pairs += [(tile.at[0, i, :, pl.ds(W - 128, 128)], side_buf.at[i]) for i in range(2)]
     copies = [pltpu.make_async_copy(source, target, sems.at[k]) for k, (source, target) in enumerate(pairs)]
     for copy in copies:
@@ -235,7 +236,7 @@
             exit_ref[(2 * i + half) * W : (2 * i + half + 1) * W] = part[:, half * 128 : (half + 1) * 128]
 
 
-def left_forward(strip, live, keep, other, psi0, t_row, t_col, exit_ref, w_ref, psi1_ref):
+def left_forward(strip, live, record, keep, other, psi0, t_row, t_col, exit_ref, w_ref, psi1_ref):
     mine = lax.axis_index("depth")
     row, col0 = place(strip, mine)
     base, offset = span(row, other.shape[2])
@@ -252,7 +253,10 @@
     put_exit(exit_ref, psi2, inside & (column < EDGE))
     number, lane = iota((STEP, 128), 0), iota((STEP, 128), 1)
     marks = jnp.where(lane + jnp.where(number == 2, 128, 0) >= col0, 1.0, 0.0)
-    exit_ref[4 * W :] = jnp.where(number == 0, live[...], marks).astype(BF)
+    exit_ref[4 * W : 4 * W + STEP] = jnp.where(number == 0, live[...], marks).astype(BF)
+    for half in range(2):
+        start = 4 * W + STEP + half * EARLY
+        exit_ref[start : start + EARLY] = record[:EARLY, half * 128 : (half + 1) * 128]
 
 
 def right_forward(
@@ -285,7 +289,7 @@
     side, exit_l, exit_r, record, psi0, t_row, t_col, f_to, f_right, f_back, f_last, psi1, w1, keep, send
 ):
     mine = lax.axis_index("depth")
-    notes = exit_l[4 * W :].astype(F32)
+    notes = exit_l[4 * W : 4 * W + STEP].astype(F32)
     live = notes[0:1, 0:1]
     of_left = jnp.concatenate([notes[1:2], notes[2:3]], axis=1)
     region = of_left if side == 0 else 1.0 - of_left
@@ -296,7 +300,9 @@
     x = dot(jnp.concatenate([x[:W], x[W:]], axis=1), f_right[...])
     fr, fi = x[:, :W], x[:, W:]
     if side == 1:
-        record = record[W // 8 :]
+        early = exit_l[4 * W + STEP :]
+        early = jnp.concatenate([early[:EARLY], early[EARLY:]], axis=1)
+        record = jnp.concatenate([early, record[W // 8 :]], axis=0)
     misfit = (fr * fr + fi * fi - record[...].astype(F32)) * live
     x = dot(f_back[...], jnp.concatenate([(misfit * fr).astype(BF), (misfit * fi).astype(BF)], axis=0)).astype(BF)
     x = dot(jnp.concatenate([x[:W], x[W:]], axis=1), f_last[...])
@@ -324,16 +330,22 @@
         keep[i], send[i] = first.astype(BF), second.astype(BF)
 
 
-def assemble(own, left, l_keep, l_recv, r_keep, r_recv, out, buf, sems):
+def add_part(buf, i, base, offset, term):
+    mask = iota((STEP, 1), 0) >= offset
+    top = term[i, 0:STEP].astype(F32)
+    rows = pl.ds(base, STEP)
+    buf[i, rows, :] = buf[i, rows, :] + jnp.where(mask, top, 0.0).astype(BF)
+    rows = pl.ds(base + STEP, W - STEP) if isinstance(base, int) else pl.ds(pl.multiple_of(base + STEP, STEP), W - STEP)
+    buf[i, rows, :] = buf[i, rows, :] + term[i, STEP:W]
+    rows = pl.ds(base + W, STEP) if isinstance(base, int) else pl.ds(pl.multiple_of(base + W, STEP), STEP)
+    buf[i, rows, :] = buf[i, rows, :] + jnp.where(mask, 0.0, top).astype(BF)
+
+
+def lay_out(own, left, l_keep, r_keep, r_recv, out, buf, sems):
     height = out.shape[2]
     mine = lax.axis_index("depth")
     work = []
-    for where, slot, term in (
-        (left, mine, r_keep),
-        (left, 1 - mine, r_recv),
-        (own, mine, l_keep),
-        (own, 1 - mine, l_recv),
-    ):
+    for where, slot, term in ((left, mine, r_keep), (left, 1 - mine, r_recv), (own, mine, l_keep)):
         row, _ = place(where, slot)
         base, offset = span(row, height)
         work.append((base, offset, term))
@@ -341,14 +353,7 @@
     for i in range(2):
         buf[i] = jnp.zeros((height, W), BF)
         for base, offset, term in work:
-            mask = iota((STEP, 1), 0) >= offset
-            top = term[i, 0:STEP].astype(F32)
-            rows = pl.ds(base, STEP)
-            buf[i, rows, :] = buf[i, rows, :] + jnp.where(mask, top, 0.0).astype(BF)
-            rows = pl.ds(pl.multiple_of(base + STEP, STEP), W - STEP)
-            buf[i, rows, :] = buf[i, rows, :] + term[i, STEP:W]
-            rows = pl.ds(pl.multiple_of(base + W, STEP), STEP)
-            buf[i, rows, :] = buf[i, rows, :] + jnp.where(mask, 0.0, top).astype(BF)
+            add_part(buf, i, base, offset, term)
         for k in range(4):
             rows = pl.ds(k * (height // 4), height // 4)
             copy = pltpu.make_async_copy(buf.at[i, rows, :], out.at[0, i, rows, :], sems.at[i, k])
@@ -358,11 +363,24 @@
         copy.wait()
 
 
+def finish(own, l_recv, laid, before, out, buf, sem):
+    del before
+    row, _ = place(own, 1 - lax.axis_index("depth"))
+    base, offset = span(row, out.shape[2])
+    rows = pl.ds(base, SPAN)
+    for i in range(2):
+        buf[i] = laid[i, rows, :]
+        add_part(buf, i, 0, offset, l_recv)
+    copy = pltpu.make_async_copy(buf, out.at[0, :, rows, :], sem)
+    copy.start()
+    copy.wait()
+
+
 VMEM = pl.BlockSpec(memory_space=pltpu.VMEM)
 HBM = pl.BlockSpec(memory_space=pltpu.HBM)
 
 
-def call(kernel, name, specs, outs, args, scratch=(), out_specs=None, vmem=40, after=(), token=False):
+def call(kernel, name, specs, outs, args, scratch=(), out_specs=None, vmem=40, after=(), token=False, aliases=None):
     count, extra, made = len(args), len(after), len(outs)
 
     def body(*refs):
@@ -383,6 +401,7 @@
         in_specs=list(specs) + [VMEM] * extra,
         out_specs=out_specs,
         scratch_shapes=list(scratch),
+        input_output_aliases=aliases or {},
         compiler_params=pltpu.CompilerParams(vmem_limit_bytes=vmem * 1024 * 1024),
         cost_estimate=pl.CostEstimate(flops=10**9, bytes_accessed=moved, transcendentals=0),
     )(*args, *after)
@@ -390,8 +409,8 @@
 
 FIELD, WAVE = ((2, W, W), BF), ((2, W, W), F32)
 BAND, QUAD = ((W, W), BF), ((2 * W, 2 * W), BF)
-MARKED, LOADED = ((W // 4 + STEP, 128), BF), ((W // 8 + W, W), BF)
-EXIT_L, EXIT_R = ((4 * W + STEP, 128), BF), ((4 * W + W * 4 * RS // 128, 128), BF)
+MARKED, LOADED = ((W // 4 + STEP, 128), BF), ((W // 8 + W - EARLY, W), BF)
+EXIT_L, EXIT_R = ((4 * W + STEP + 2 * EARLY, 128), BF), ((4 * W + W * 4 * RS // 128, 128), BF)
 
 
 def on_device(transmission, chirp_taps, probe_field, records, pos_row, pos_col, counts):
@@ -433,7 +452,7 @@
     other_tile = to_other(transmission)
     record = lax.dynamic_index_in_dim(records[0], my_depth, 0, keepdims=False)
     scratch = [pltpu.SMEM((1, 2), jnp.int32)] * 2 + [pltpu.SMEM((5,), F32)]
-    for shape in ((W, W), (2, SPAN, W), (2, height, 128), MARKED[0], (W // 8, W), (2, W, W)):
+    for shape in ((W - EARLY, W), (2, SPAN, W), (2, height, 128), MARKED[0], (W // 8, W), (2, W, W)):
         scratch.append(pltpu.VMEM(shape, BF))
     strip_keep, strip_send, keep = call(
         edges, "edges", [HBM] * 5, [MARKED, LOADED, FIELD],
@@ -448,8 +467,8 @@
         [pos_row, pos_col, chirp_taps, probe_field], scratch[:3] + [pltpu.SemaphoreType.DMA((3,))],
     )
     exit_l, w1, psi1, done = call(
-        left_forward, "left_forward", [VMEM] * 7, [EXIT_L, FIELD, FIELD],
-        [strip_keep, live, keep, other_tile, *settled], token=True,
+        left_forward, "left_forward", [VMEM] * 8, [EXIT_L, FIELD, FIELD],
+        [strip_keep, live, record, keep, other_tile, *settled], token=True,
     )
     exit_l_left = to_right(exit_l)
     settled_left = call(
@@ -475,10 +494,13 @@
     l_keep, l_send = terms(0, exit_l, exit_r, record, *settled, *own_tables, psi1, w1, after=[done])
     l_recv = to_other(l_send)
 
+    laid_out, laid = call(
+        lay_out, "lay_out", [VMEM] * 5, [(transmission.shape, BF), ((2, height, W), BF)],
+        [strip_keep, strip_a, l_keep, r_keep, r_recv], [pltpu.SemaphoreType.DMA((2, 4))], out_specs=[HBM, VMEM],
+    )
     return call(
-        assemble, "assemble", [VMEM] * 6, [(transmission.shape, BF)],
-        [strip_keep, strip_a, l_keep, l_recv, r_keep, r_recv],
-        [pltpu.VMEM((2, height, W), BF), pltpu.SemaphoreType.DMA((2, 4))], out_specs=[HBM],
+        finish, "finish", [VMEM] * 3 + [HBM], [(transmission.shape, BF)], [strip_keep, l_recv, laid, laid_out],
+        [pltpu.VMEM((2, SPAN, W), BF), pltpu.SemaphoreType.DMA], out_specs=[HBM], aliases={3: 0},
     )[0]
 
 

time: 32.3 us -> 31.5 us (0.975)
  waiting for transfers between devices: 8.49 us -> 7.54 us
  Pallas kernels: 13.6 us -> 14.5 us
  starting transfers between devices: 9.07 us -> 8.33 us
    ppermute x2, waiting for transfers between devices: 4.07 us -> 5.39 us  [to_right(): return lax.ppermute(x, 'tile', [(i, (i + 1) % tiles) for i in range(tiles)])]
    ppermute x3, waiting for transfers between devices: 1.16 us -> 0.01 us  [to_other(): return lax.ppermute(x, 'depth', [(0, 1), (1, 0)])]
    pallas_call x10 -> x11, Pallas kernels: 13.6 us -> 14.5 us  [call(): pl.pallas_call(body, name=name, out_shape=[jax.ShapeDtypeStruct(shape, ki...]
    ppermute x1, waiting for transfers between devices: 0.59 us -> 0.01 us  [to_left(): return lax.ppermute(x, 'tile', [(i, (i - 1) % tiles) for i in range(tiles)])]
    ppermute x1, waiting for transfers between devices: 2.66 us -> 2.14 us  [to_right_other(): return lax.ppermute(x, ('depth', 'tile'), pairs)]
    ppermute x3, starting transfers between devices: 3.08 us -> 2.63 us  [to_other(): return lax.ppermute(x, 'depth', [(0, 1), (1, 0)])]
  transfers between devices with their start and end apart: 7 -> 7, of which waited for: 5 -> 3; matrix products, arithmetic and copies ran while one was open for 0% -> 0% of each run, Pallas kernels for 38% -> 44%
where the time goes in v4:
time: 31.5 us; the launch traced here: 31.3 us
  Pallas kernels  14.5 us (46%)
  starting transfers between devices  8.33 us (26%)
  waiting for transfers between devices  7.54 us (24%)
  between operations  0.87 us (3%)
    pallas_call x11, Pallas kernels, call(): pl.pallas_call(body, name=name, out_shape=[jax.ShapeDtypeStruct(shape, ki...  14.5 us
    ppermute x2, waiting for transfers between devices, to_right(): return lax.ppermute(x, 'tile', [(i, (i + 1) % tiles) for i in range(tiles)])  5.39 us
    ppermute x3, starting transfers between devices, to_other(): return lax.ppermute(x, 'depth', [(0, 1), (1, 0)])  2.63 us
    ppermute x2, starting transfers between devices, to_right(): return lax.ppermute(x, 'tile', [(i, (i + 1) % tiles) for i in range(tiles)])  2.37 us
    ppermute x1, waiting for transfers between devices, to_right_other(): return lax.ppermute(x, ('depth', 'tile'), pairs)  2.14 us
    ppermute x1, starting transfers between devices, to_left(): return lax.ppermute(x, 'tile', [(i, (i - 1) % tiles) for i in range(tiles)])  1.79 us
    ppermute x1, starting transfers between devices, to_right_other(): return lax.ppermute(x, ('depth', 'tile'), pairs)  1.54 us
  transfers between devices with their start and end apart: 7, of which 3 were waited for; matrix products, arithmetic and copies ran while one was open for 0% of the time, Pallas kernels for 44%

profile of v4, /device:TPU:1, one launch (start us, length us, event | category | flops | bytes accessed | tf_op | source)
XLA Modules:
  0.0 31.3 jit_solution(383764711420369784)
XLA Ops:
  0.0 0.0 copy-start.3
  0.0 0.0 copy-start.4
  0.0 0.0 copy-start.5
  0.0 0.0 copy-start.2
  0.0 1.5 %collective-permute-start = (bf16[1,2,2048,256]{3,2,1,0:T(8,128)(2,1)}, bf16[1,2,2048,256]{3,2,1,0:T(8,128)(2,1)S(1)}, u32[]{:S(2)}, u32[]{:S(2)}) collective-permute-start(bf16[1,2,2048,256]{3,2,1,0:T(8,128)(2,1)} %refs_0_.5), channel_id=1, source_target_pairs={{0,64},{64,0},{1,65},{65,1},{2,66},{66,2},{3,67},{67,3},{4,68},{68... | collective-permute-start | bytes 6291464 | tf_op jit(solution)/shard_map/ppermute | solution.py:432
  1.5 2.5 %edges.1 = (bf16[80,128]{1,0:T(8,128)(2,1)}, bf16[240,256]{1,0:T(8,128)(2,1)}, bf16[2,256,256]{2,1,0:T(8,128)(2,1)}) custom-call(s32[1,2]{1,0:T(1,128)} %refs_0_.4, s32[1,2]{1,0:T(1,128)} %refs_1_.6, f32[5]{0:T(128)} %refs_2_.3, bf16[1,2,2048,256]{3,2,1,0:T(8,128)(2,1)} %refs_0_.5, bf16[1,2,256,256]{3,2,1,0:T(8,128)(2,1)} %refs_4_.1), custom_call_target="tpu_custom_call" | custom-call | flops 1000000000 | bytes 405504 | tf_op jit(solution)/shard_map/edges/pallas_call | solution.py:397
  4.0 0.0 copy-start.8
  4.1 0.0 copy-start.1
  4.1 0.0 copy-start.7
  4.1 1.4 %collective-permute-start.1 = (bf16[80,128]{1,0:T(8,128)(2,1)}, bf16[80,128]{1,0:T(8,128)(2,1)S(1)}, u32[]{:S(2)}, u32[]{:S(2)}) collective-permute-start(bf16[80,128]{1,0:T(8,128)(2,1)} %get-tuple-element.39.refs_0_), channel_id=1, source_target_pairs={{0,1},{1,2},{2,3},{3,4},{4,5},{5,6},{6,7},{7,8},{8,9},{9,10},{10,1... | collective-permute-start | bytes 61448 | tf_op jit(solution)/shard_map/ppermute | solution.py:422
  5.5 1.5 %collective-permute-start.2 = (bf16[240,256]{1,0:T(8,128)(2,1)}, bf16[240,256]{1,0:T(8,128)(2,1)S(1)}, u32[]{:S(2)}, u32[]{:S(2)}) collective-permute-start(bf16[240,256]{1,0:T(8,128)(2,1)} %get-tuple-element.45), channel_id=1, source_target_pairs={{0,65},{1,66},{2,67},{3,68},{4,69},{5,70},{6,71},{7,72},{8,73},{9,... | collective-permute-start | bytes 368648 | tf_op jit(solution)/shard_map/ppermute | solution.py:429
  7.7 0.0 copy-done.3
  7.7 0.0 copy-done.4
  7.7 0.0 copy-done.5
  7.7 0.0 copy-done.2
  7.7 1.1 %settle.1 = (f32[2,256,256]{2,1,0:T(8,128)S(1)}, bf16[256,256]{1,0:T(8,128)(2,1)S(1)}, bf16[256,256]{1,0:T(8,128)(2,1)S(1)}) custom-call(s32[1,2]{1,0:T(1,128)S(1)} %copy-done.3, s32[1,2]{1,0:T(1,128)S(1)} %copy-done.4, f32[5]{0:T(128)S(1)} %copy-done.5, f32[2,256,256]{2,1,0:T(8,128)S(1)} %copy-done.2), custom_call_target="tpu_custom_call" | custom-call | flops 1000000000 | bytes 1310720 | tf_op jit(solution)/shard_map/settle/pallas_call | solution.py:397
  8.8 0.0 copy-done.8
  8.8 0.0 collective-permute-done.refs_4_.refs_1_
  8.8 0.0 copy-done.1
  8.8 0.0 copy-done.7
  8.9 0.9 %left_forward.1 = (bf16[1136,128]{1,0:T(8,128)(2,1)S(1)}, bf16[2,256,256]{2,1,0:T(8,128)(2,1)S(1)}, bf16[2,256,256]{2,1,0:T(8,128)(2,1)S(1)}, f32[8,128]{1,0:T(8,128)S(1)}) custom-call(bf16[80,128]{1,0:T(8,128)(2,1)S(1)} %copy-done.1, f32[16,128]{1,0:T(8,128)S(1)} %broadcast_in_dim.3.refs_1_, bf16[256,256]{1,0:T(8,128)(2,1)S(1)} %dynamic-slice_bitcast_fusion.refs_2_, ...), custom_call_target="tpu_custom_call" | custom-call | flops 1000000000 | bytes 4124672 | tf_op jit(solution)/shard_map/left_forward/pallas_call | solution.py:397
  9.7 0.0 copy-start
  9.7 1.0 %collective-permute-start.4 = (bf16[1136,128]{1,0:T(8,128)(2,1)S(1)}, bf16[1136,128]{1,0:T(8,128)(2,1)S(1)}, u32[]{:S(2)}, u32[]{:S(2)}) collective-permute-start(bf16[1136,128]{1,0:T(8,128)(2,1)S(1)} %get-tuple-element.44.refs_0_), channel_id=1, source_target_pairs={{0,1},{1,2},{2,3},{3,4},{4,5},{5,6},{6,7},{7,8},{8,9},{9,10},{10,1... | collective-permute-start | bytes 872456 | tf_op jit(solution)/shard_map/ppermute | solution.py:422
  10.7 3.3 %collective-permute-done.1.refs_0_.refs_2_.refs_1_ = bf16[80,128]{1,0:T(8,128)(2,1)S(1)} collective-permute-done((bf16[80,128]{1,0:T(8,128)(2,1)}, bf16[80,128]{1,0:T(8,128)(2,1)S(1)}, u32[]{:S(2)}, u32[]{:S(2)}) %collective-permute-start.1) | collective-permute-done | bytes 20512 | tf_op jit(solution)/shard_map/ppermute | solution.py:422
  14.0 0.7 %settle_left.1 = (f32[2,256,256]{2,1,0:T(8,128)S(1)}, bf16[256,256]{1,0:T(8,128)(2,1)S(1)}, bf16[256,256]{1,0:T(8,128)(2,1)S(1)}) custom-call(bf16[80,128]{1,0:T(8,128)(2,1)S(1)} %collective-permute-done.1.refs_0_.refs_2_.refs_1_, f32[2,256,256]{2,1,0:T(8,128)S(1)} %copy-done.2, f32[8,128]{1,0:T(8,128)S(1)} %get-tuple-element.46.refs_2_), custom_call_target="tpu_custom_call" | custom-call | flops 1000000000 | bytes 1331200 | tf_op jit(solution)/shard_map/settle_left/pallas_call | solution.py:397
  14.7 2.1 %collective-permute-done.2.refs_3_.refs_2_ = bf16[240,256]{1,0:T(8,128)(2,1)S(1)} collective-permute-done((bf16[240,256]{1,0:T(8,128)(2,1)}, bf16[240,256]{1,0:T(8,128)(2,1)S(1)}, u32[]{:S(2)}, u32[]{:S(2)}) %collective-permute-start.2) | collective-permute-done | bytes 122912 | tf_op jit(solution)/shard_map/ppermute | solution.py:429
  16.9 0.0 copy-done
  16.9 0.0 copy-start.6
  16.9 0.9 %right_forward.1 = (bf16[1056,128]{1,0:T(8,128)(2,1)S(1)}, bf16[2,256,256]{2,1,0:T(8,128)(2,1)S(1)}, bf16[2,256,256]{2,1,0:T(8,128)(2,1)S(1)}, f32[8,128]{1,0:T(8,128)S(1)}) custom-call(bf16[1,2,2048,256]{3,2,1,0:T(8,128)(2,1)S(1)} %copy-done, bf16[1,2,2048,256]{3,2,1,0:T(8,128)(2,1)S(1)} %collective-permute-done.refs_4_.refs_1_, ...), custom_call_target="tpu_custom_call" | custom-call | flops 1000000000 | bytes 5922816 | tf_op jit(solution)/shard_map/right_forward/pallas_call | solution.py:397
  17.8 1.8 %collective-permute-start.3 = (bf16[1056,128]{1,0:T(8,128)(2,1)S(1)}, bf16[1056,128]{1,0:T(8,128)(2,1)S(1)}, u32[]{:S(2)}, u32[]{:S(2)}) collective-permute-start(bf16[1056,128]{1,0:T(8,128)(2,1)S(1)} %get-tuple-element.50.refs_1_), channel_id=1, source_target_pairs={{0,63},{1,0},{2,1},{3,2},{4,3},{5,4},{6,5},{7,6},{8,7},{9,8},{10,9... | collective-permute-start | bytes 811016 | tf_op jit(solution)/shard_map/ppermute | solution.py:425
  19.6 0.0 copy-done.6
  19.6 1.0 %tables_left.1 = (bf16[512,512]{1,0:T(8,128)(2,1)S(1)}, bf16[512,512]{1,0:T(8,128)(2,1)S(1)}, bf16[512,512]{1,0:T(8,128)(2,1)S(1)}, bf16[512,512]{1,0:T(8,128)(2,1)S(1)}, f32[8,128]{1,0:T(8,128)S(1)}) custom-call(bf16[80,128]{1,0:T(8,128)(2,1)S(1)} %collective-permute-done.1.refs_0_.refs_2_.refs_1_, bf16[512,256]{1,0:T(8,128)(2,1)S(1)} %copy-done.6, ...), custom_call_target="tpu_custom_call" | custom-call | flops 1000000000 | bytes 2646016 | tf_op jit(solution)/shard_map/tables_left/pallas_call | solution.py:397
  20.6 1.0 %tables.1 = (bf16[512,512]{1,0:T(8,128)(2,1)S(1)}, bf16[512,512]{1,0:T(8,128)(2,1)S(1)}, bf16[512,512]{1,0:T(8,128)(2,1)S(1)}, bf16[512,512]{1,0:T(8,128)(2,1)S(1)}, f32[8,128]{1,0:T(8,128)S(1)}) custom-call(bf16[80,128]{1,0:T(8,128)(2,1)S(1)} %copy-done.1, bf16[512,256]{1,0:T(8,128)(2,1)S(1)} %copy-done.6, ...), custom_call_target="tpu_custom_call" | custom-call | flops 1000000000 | bytes 2646016 | tf_op jit(solution)/shard_map/tables/pallas_call | solution.py:397
  21.6 2.1 %collective-permute-done.4.refs_0_ = bf16[1136,128]{1,0:T(8,128)(2,1)S(1)} collective-permute-done((bf16[1136,128]{1,0:T(8,128)(2,1)S(1)}, bf16[1136,128]{1,0:T(8,128)(2,1)S(1)}, u32[]{:S(2)}, u32[]{:S(2)}) %collective-permute-start.4) | collective-permute-done | bytes 290848 | tf_op jit(solution)/shard_map/ppermute | solution.py:422
  23.7 2.0 %far_field_1.1 = (bf16[2,256,256]{2,1,0:T(8,128)(2,1)S(1)}, bf16[2,256,256]{2,1,0:T(8,128)(2,1)S(1)}, f32[8,128]{1,0:T(8,128)S(1)}) custom-call(bf16[1136,128]{1,0:T(8,128)(2,1)S(1)} %collective-permute-done.4.refs_0_, bf16[1056,128]{1,0:T(8,128)(2,1)S(1)} %get-tuple-element.50.refs_1_, bf16[240,256]{1,0:T(8,128)(2,1)S(1)} %collective-permute-done.2.refs_3_.refs_2_, ...), custom_call_target="tpu_custom_call" | custom-call | flops 1000000000 | bytes 4620288 | tf_op jit(solution)/shard_map/far_field_1/pallas_call | solution.py:397
  25.7 0.9 %collective-permute-start.6 = (bf16[2,256,256]{2,1,0:T(8,128)(2,1)S(1)}, bf16[2,256,256]{2,1,0:T(8,128)(2,1)S(1)}, u32[]{:S(2)}, u32[]{:S(2)}) collective-permute-start(bf16[2,256,256]{2,1,0:T(8,128)(2,1)S(1)} %get-tuple-element.70), channel_id=1, source_target_pairs={{0,64},{64,0},{1,65},{65,1},{2,66},{66,2},{3,67},{67,3},{4,68},{68... | collective-permute-start | bytes 786440 | tf_op jit(solution)/shard_map/ppermute | solution.py:432
  26.6 0.0 collective-permute-done.3.refs_1_
  26.6 2.0 %far_field_0.1 = (bf16[2,256,256]{2,1,0:T(8,128)(2,1)S(1)}, bf16[2,256,256]{2,1,0:T(8,128)(2,1)S(1)}) custom-call(bf16[1136,128]{1,0:T(8,128)(2,1)S(1)} %get-tuple-element.44.refs_0_, bf16[1056,128]{1,0:T(8,128)(2,1)S(1)} %collective-permute-done.3.refs_1_, bf16[256,256]{1,0:T(8,128)(2,1)S(1)} %dynamic-slice_bitcast_fusion.refs_2_, ...), custom_call_target="tpu_custom_call" | custom-call | flops 1000000000 | bytes 4624384 | tf_op jit(solution)/shard_map/far_field_0/pallas_call | solution.py:397
  28.6 0.2 collective-permute-start.5
  28.9 0.0 collective-permute-done.6.refs_4_
  28.9 1.6 %lay_out.1 = (bf16[1,2,2048,256]{3,2,1,0:T(8,128)(2,1)}, bf16[2,2048,256]{2,1,0:T(8,128)(2,1)S(1)}) custom-call(bf16[80,128]{1,0:T(8,128)(2,1)S(1)} %copy-done.1, bf16[80,128]{1,0:T(8,128)(2,1)S(1)} %collective-permute-done.1.refs_0_.refs_2_.refs_1_, bf16[2,256,256]{2,1,0:T(8,128)(2,1)S(1)} %get-tuple-element.68.refs_2_, ...), custom_call_target="tpu_custom_call" | custom-call | flops 1000000000 | bytes 5021696 | tf_op jit(solution)/shard_map/lay_out/pallas_call | solution.py:397
  30.4 0.0 collective-permute-done.5.refs_1_
  30.4 0.9 %finish.1 = bf16[1,2,2048,256]{3,2,1,0:T(8,128)(2,1)} custom-call(bf16[80,128]{1,0:T(8,128)(2,1)S(1)} %copy-done.1, bf16[2,256,256]{2,1,0:T(8,128)(2,1)S(1)} %collective-permute-done.5.refs_1_, bf16[2,2048,256]{2,1,0:T(8,128)(2,1)S(1)} %get-tuple-element.71.refs_2_, bf16[1,2,2048,256]{3,2,1,0:T(8,128)(2,1)} %get-tuple-element.72.refs_3_), custom_call_target="tpu_custom_call", output_to_operand_aliasing={{}: (3, {})} | custom-call | flops 1000000000 | bytes 4476928 | tf_op jit(solution)/shard_map/finish/pallas_call | solution.py:397
  (2 shorter events, 0.0 us)
Async XLA Ops:
  0.0 7.7 %copy-start.3 = (s32[1,2]{1,0:T(1,128)S(1)}, s32[1,2]{1,0:T(1,128)}, u32[]{:S(2)}) copy-start(s32[1,2]{1,0:T(1,128)} %refs_0_.4) | copy-start | bytes 28
  0.0 7.7 %copy-start.4 = (s32[1,2]{1,0:T(1,128)S(1)}, s32[1,2]{1,0:T(1,128)}, u32[]{:S(2)}) copy-start(s32[1,2]{1,0:T(1,128)} %refs_1_.6) | copy-start | bytes 28
  0.0 7.7 %copy-start.5 = (f32[5]{0:T(128)S(1)}, f32[5]{0:T(128)}, u32[]{:S(2)}) copy-start(f32[5]{0:T(128)} %refs_2_.3) | copy-start | bytes 64
  0.0 7.7 %copy-start.2 = (f32[2,256,256]{2,1,0:T(8,128)S(1)}, f32[2,256,256]{2,1,0:T(8,128)}, u32[]{:S(2)}) copy-start(f32[2,256,256]{2,1,0:T(8,128)} %refs_1_.7) | copy-start | bytes 1572868
  0.0 8.8 %collective-permute-start = (bf16[1,2,2048,256]{3,2,1,0:T(8,128)(2,1)}, bf16[1,2,2048,256]{3,2,1,0:T(8,128)(2,1)S(1)}, u32[]{:S(2)}, u32[]{:S(2)}) collective-permute-start(bf16[1,2,2048,256]{3,2,1,0:T(8,128)(2,1)} %refs_0_.5), channel_id=1, source_target_pairs={{0,64},{64,0},{1,65},{65,1},{2,66},{66,2},{3,67},{67,3},{4,68},{68... | collective-permute-start | bytes 6291464 | tf_op jit(solution)/shard_map/ppermute | solution.py:432
  4.0 4.7 %copy-start.8 = (bf16[1,2,256,256]{3,2,1,0:T(8,128)(2,1)S(1)}, bf16[1,2,256,256]{3,2,1,0:T(8,128)(2,1)}, u32[]{:S(2)}) copy-start(bf16[1,2,256,256]{3,2,1,0:T(8,128)(2,1)} %refs_4_.1) | copy-start | bytes 786436
  4.1 4.8 %copy-start.1 = (bf16[80,128]{1,0:T(8,128)(2,1)S(1)}, bf16[80,128]{1,0:T(8,128)(2,1)}, u32[]{:S(2)}) copy-start(bf16[80,128]{1,0:T(8,128)(2,1)} %get-tuple-element.39.refs_0_) | copy-start | bytes 61444
  4.1 4.8 %copy-start.7 = (bf16[2,256,256]{2,1,0:T(8,128)(2,1)S(1)}, bf16[2,256,256]{2,1,0:T(8,128)(2,1)}, u32[]{:S(2)}) copy-start(bf16[2,256,256]{2,1,0:T(8,128)(2,1)} %get-tuple-element.40.refs_3_) | copy-start | bytes 786436
  4.1 10.0 %collective-permute-start.1 = (bf16[80,128]{1,0:T(8,128)(2,1)}, bf16[80,128]{1,0:T(8,128)(2,1)S(1)}, u32[]{:S(2)}, u32[]{:S(2)}) collective-permute-start(bf16[80,128]{1,0:T(8,128)(2,1)} %get-tuple-element.39.refs_0_), channel_id=1, source_target_pairs={{0,1},{1,2},{2,3},{3,4},{4,5},{5,6},{6,7},{7,8},{8,9},{9,10},{10,1... | collective-permute-start | bytes 61448 | tf_op jit(solution)/shard_map/ppermute | solution.py:422
  5.5 11.4 %collective-permute-start.2 = (bf16[240,256]{1,0:T(8,128)(2,1)}, bf16[240,256]{1,0:T(8,128)(2,1)S(1)}, u32[]{:S(2)}, u32[]{:S(2)}) collective-permute-start(bf16[240,256]{1,0:T(8,128)(2,1)} %get-tuple-element.45), channel_id=1, source_target_pairs={{0,65},{1,66},{2,67},{3,68},{4,69},{5,70},{6,71},{7,72},{8,73},{9,... | collective-permute-start | bytes 368648 | tf_op jit(solution)/shard_map/ppermute | solution.py:429
  9.7 7.2 %copy-start = (bf16[1,2,2048,256]{3,2,1,0:T(8,128)(2,1)S(1)}, bf16[1,2,2048,256]{3,2,1,0:T(8,128)(2,1)}, u32[]{:S(2)}) copy-start(bf16[1,2,2048,256]{3,2,1,0:T(8,128)(2,1)} %refs_0_.5) | copy-start | bytes 6291460
  9.7 14.0 %collective-permute-start.4 = (bf16[1136,128]{1,0:T(8,128)(2,1)S(1)}, bf16[1136,128]{1,0:T(8,128)(2,1)S(1)}, u32[]{:S(2)}, u32[]{:S(2)}) collective-permute-start(bf16[1136,128]{1,0:T(8,128)(2,1)S(1)} %get-tuple-element.44.refs_0_), channel_id=1, source_target_pairs={{0,1},{1,2},{2,3},{3,4},{4,5},{5,6},{6,7},{7,8},{8,9},{9,10},{10,1... | collective-permute-start | bytes 872456 | tf_op jit(solution)/shard_map/ppermute | solution.py:422
  16.9 2.7 %copy-start.6 = (bf16[512,256]{1,0:T(8,128)(2,1)S(1)}, bf16[512,256]{1,0:T(8,128)(2,1)}, u32[]{:S(2)}) copy-start(bf16[512,256]{1,0:T(8,128)(2,1)} %constant.15.clone.refs_1_) | copy-start | bytes 786436
  17.8 8.8 %collective-permute-start.3 = (bf16[1056,128]{1,0:T(8,128)(2,1)S(1)}, bf16[1056,128]{1,0:T(8,128)(2,1)S(1)}, u32[]{:S(2)}, u32[]{:S(2)}) collective-permute-start(bf16[1056,128]{1,0:T(8,128)(2,1)S(1)} %get-tuple-element.50.refs_1_), channel_id=1, source_target_pairs={{0,63},{1,0},{2,1},{3,2},{4,3},{5,4},{6,5},{7,6},{8,7},{9,8},{10,9... | collective-permute-start | bytes 811016 | tf_op jit(solution)/shard_map/ppermute | solution.py:425
  25.7 3.2 %collective-permute-start.6 = (bf16[2,256,256]{2,1,0:T(8,128)(2,1)S(1)}, bf16[2,256,256]{2,1,0:T(8,128)(2,1)S(1)}, u32[]{:S(2)}, u32[]{:S(2)}) collective-permute-start(bf16[2,256,256]{2,1,0:T(8,128)(2,1)S(1)} %get-tuple-element.70), channel_id=1, source_target_pairs={{0,64},{64,0},{1,65},{65,1},{2,66},{66,2},{3,67},{67,3},{4,68},{68... | collective-permute-start | bytes 786440 | tf_op jit(solution)/shard_map/ppermute | solution.py:432
  28.6 1.8 %collective-permute-start.5 = (bf16[2,256,256]{2,1,0:T(8,128)(2,1)S(1)}, bf16[2,256,256]{2,1,0:T(8,128)(2,1)S(1)}, u32[]{:S(2)}, u32[]{:S(2)}) collective-permute-start(bf16[2,256,256]{2,1,0:T(8,128)(2,1)S(1)} %get-tuple-element.67), channel_id=1, source_target_pairs={{0,64},{64,0},{1,65},{65,1},{2,66},{66,2},{3,67},{67,3},{4,68},{68... | collective-permute-start | bytes 786440 | tf_op jit(solution)/shard_map/ppermute | solution.py:432

commit v5 on v4

--- a/solution.py
+++ b/solution.py
@@ -13,7 +13,7 @@
 SPAN = W + STEP
 LS = 16
 RS = 4
-EARLY = 48
+EARLY = 32
 EDGE = W - 8
 BF = jnp.bfloat16
 F32 = jnp.float32
@@ -132,8 +132,8 @@
 
 
 def edges(
-    pos_row, pos_col, chirp_taps, tile, records, strip_keep, strip_send, keep,
-    rows, cols, taps, record, buf, side_buf, packed, packed_send, window, sems,
+    pos_row, pos_col, chirp_taps, tile, records, strip_keep, strip_send,
+    rows, cols, taps, record, side_buf, packed, packed_send, sems,
 ):
     mine = lax.axis_index("depth")
     height = tile.shape[2]
@@ -145,14 +145,12 @@
     last = []
 
     def put(source, target):
-        last.append(pltpu.make_async_copy(source, target, sems.at[len(pairs) + 1 + len(last)]))
+        last.append(pltpu.make_async_copy(source, target, sems.at[len(pairs) + len(last)]))
         last[-1].start()
 
     copies[0].wait()
     base, offset = span(rows[0, mine], height)
     base_send, offset_send = span(rows[0, 1 - mine], height)
-    whole = pltpu.make_async_copy(tile.at[0, :, pl.ds(base, SPAN), :], buf, sems.at[len(pairs)])
-    whole.start()
     copies[1].wait()
     copies[2].wait()
     lane = iota((STEP, 128), 1)
@@ -174,10 +172,6 @@
     put(packed_send, strip_send.at[: W // 8])
     packed[: W // 4] = pack([fold(side_buf[i, pl.ds(base, SPAN), :], offset) for i in range(2)], [128 - LS] * 2, LS)
     put(packed, strip_keep)
-    whole.wait()
-    for i in range(2):
-        window[i] = fold(buf[i], offset).astype(BF)
-    put(window, keep)
     for copy in last:
         copy.wait()
 
@@ -188,16 +182,22 @@
         psi0[i] = pltpu.roll(pltpu.roll(probe[i], offset, 0), col0, 1)
 
 
-def settle_own(height, pos_row, pos_col, chirp_taps, probe, psi0, t_row, t_col, rows, cols, taps, sems):
+def settle_own(pos_row, pos_col, chirp_taps, tile, probe, keep, psi0, t_row, t_col, rows, cols, taps, buf, sems):
     mine = lax.axis_index("depth")
     pairs = [(pos_row, rows), (pos_col, cols), (chirp_taps, taps)]
     copies = [pltpu.make_async_copy(source, target, sems.at[k]) for k, (source, target) in enumerate(pairs)]
     for copy in copies:
         copy.start()
-    for copy in copies:
-        copy.wait()
-    _, offset = span(rows[0, mine], height)
+    copies[0].wait()
+    base, offset = span(rows[0, mine], tile.shape[2])
+    whole = pltpu.make_async_copy(tile.at[0, :, pl.ds(base, SPAN), :], buf, sems.at[3])
+    whole.start()
+    copies[1].wait()
+    copies[2].wait()
     settle(taps, probe, offset, cols[0, mine], psi0, t_row, t_col)
+    whole.wait()
+    for i in range(2):
+        keep[i] = fold(buf[i], offset).astype(BF)
 
 
 def settle_left(height, strip, probe, psi0, t_row, t_col):
@@ -434,9 +434,6 @@
     def table_kernel(*refs):
         tables(height, *refs)
 
-    def settle_own_kernel(*refs):
-        settle_own(height, *refs)
-
     def settle_left_kernel(*refs):
         settle_left(height, *refs)
 
@@ -451,20 +448,20 @@
     dft = jnp.asarray(dft_tables(), BF)
     other_tile = to_other(transmission)
     record = lax.dynamic_index_in_dim(records[0], my_depth, 0, keepdims=False)
-    scratch = [pltpu.SMEM((1, 2), jnp.int32)] * 2 + [pltpu.SMEM((5,), F32)]
-    for shape in ((W - EARLY, W), (2, SPAN, W), (2, height, 128), MARKED[0], (W // 8, W), (2, W, W)):
-        scratch.append(pltpu.VMEM(shape, BF))
-    strip_keep, strip_send, keep = call(
-        edges, "edges", [HBM] * 5, [MARKED, LOADED, FIELD],
-        [pos_row, pos_col, chirp_taps, transmission, records],
-        scratch + [pltpu.SemaphoreType.DMA((11,))], out_specs=[HBM] * 3, vmem=56,
+    scalars = [pltpu.SMEM((1, 2), jnp.int32)] * 2 + [pltpu.SMEM((5,), F32)]
+    shapes = (W - EARLY, W), (2, height, 128), MARKED[0], (W // 8, W)
+    strip_keep, strip_send = call(
+        edges, "edges", [HBM] * 5, [MARKED, LOADED], [pos_row, pos_col, chirp_taps, transmission, records],
+        scalars + [pltpu.VMEM(shape, BF) for shape in shapes] + [pltpu.SemaphoreType.DMA((9,))],
+        out_specs=[HBM] * 2, vmem=56,
     )
     strip_a = to_right(strip_keep)
     strip_b = to_right_other(strip_send)
     live = jnp.broadcast_to((my_depth < counts[0]).astype(F32), (STEP, 128))
-    settled = call(
-        settle_own_kernel, "settle", [HBM] * 3 + [VMEM], [WAVE, BAND, BAND],
-        [pos_row, pos_col, chirp_taps, probe_field], scratch[:3] + [pltpu.SemaphoreType.DMA((3,))],
+    keep, *settled = call(
+        settle_own, "settle", [HBM] * 4 + [VMEM], [FIELD, WAVE, BAND, BAND],
+        [pos_row, pos_col, chirp_taps, transmission, probe_field],
+        scalars + [pltpu.VMEM((2, SPAN, W), BF), pltpu.SemaphoreType.DMA((4,))], vmem=51,
     )
     exit_l, w1, psi1, done = call(
         left_forward, "left_forward", [VMEM] * 8, [EXIT_L, FIELD, FIELD],

time: 31.5 us -> 31.3 us (level)
  no operation moved by 1% of the time
where the time goes in v5:
time: 31.3 us; the launch traced here: 31.2 us
  Pallas kernels  14.7 us (47%)
  starting transfers between devices  8.08 us (26%)
  waiting for transfers between devices  7.52 us (24%)
  between operations  0.85 us (3%)
    pallas_call x11, Pallas kernels, call(): pl.pallas_call(body, name=name, out_shape=[jax.ShapeDtypeStruct(shape, ki...  14.7 us
    ppermute x2, waiting for transfers between devices, to_right(): return lax.ppermute(x, 'tile', [(i, (i + 1) % tiles) for i in range(tiles)])  5.18 us
    ppermute x3, starting transfers between devices, to_other(): return lax.ppermute(x, 'depth', [(0, 1), (1, 0)])  2.71 us
    ppermute x2, starting transfers between devices, to_right(): return lax.ppermute(x, 'tile', [(i, (i + 1) % tiles) for i in range(tiles)])  2.38 us
    ppermute x1, waiting for transfers between devices, to_right_other(): return lax.ppermute(x, ('depth', 'tile'), pairs)  2.33 us
    ppermute x1, starting transfers between devices, to_left(): return lax.ppermute(x, 'tile', [(i, (i - 1) % tiles) for i in range(tiles)])  1.54 us
    ppermute x1, starting transfers between devices, to_right_other(): return lax.ppermute(x, ('depth', 'tile'), pairs)  1.46 us
  transfers between devices with their start and end apart: 7, of which 3 were waited for; matrix products, arithmetic and copies ran while one was open for 0% of the time, Pallas kernels for 44%

profile of v5, /device:TPU:1, one launch (start us, length us, event | category | flops | bytes accessed | tf_op | source)
XLA Modules:
  0.0 31.2 jit_solution(11750737526129002014)
XLA Ops:
  0.0 0.0 copy-start.3
  0.0 0.0 copy-start.4
  0.0 0.0 copy-start.5
  0.0 0.0 copy-start.2
  0.0 1.5 %collective-permute-start = (bf16[1,2,2048,256]{3,2,1,0:T(8,128)(2,1)}, bf16[1,2,2048,256]{3,2,1,0:T(8,128)(2,1)S(1)}, u32[]{:S(2)}, u32[]{:S(2)}) collective-permute-start(bf16[1,2,2048,256]{3,2,1,0:T(8,128)(2,1)} %refs_0_.5), channel_id=1, source_target_pairs={{0,64},{64,0},{1,65},{65,1},{2,66},{66,2},{3,67},{67,3},{4,68},{68... | collective-permute-start | bytes 6291464 | tf_op jit(solution)/shard_map/ppermute | solution.py:432
  1.5 2.2 %edges.1 = (bf16[80,128]{1,0:T(8,128)(2,1)}, bf16[256,256]{1,0:T(8,128)(2,1)}) custom-call(s32[1,2]{1,0:T(1,128)} %refs_0_.4, s32[1,2]{1,0:T(1,128)} %refs_1_.6, f32[5]{0:T(128)} %refs_2_.3, bf16[1,2,2048,256]{3,2,1,0:T(8,128)(2,1)} %refs_0_.5, bf16[1,2,256,256]{3,2,1,0:T(8,128)(2,1)} %refs_4_.2), custom_call_target="tpu_custom_call" | custom-call | flops 1000000000 | bytes 151552 | tf_op jit(solution)/shard_map/edges/pallas_call | solution.py:397
  3.7 0.0 copy-start.7
  3.7 0.0 copy-start.1
  3.7 1.4 %collective-permute-start.1 = (bf16[80,128]{1,0:T(8,128)(2,1)}, bf16[80,128]{1,0:T(8,128)(2,1)S(1)}, u32[]{:S(2)}, u32[]{:S(2)}) collective-permute-start(bf16[80,128]{1,0:T(8,128)(2,1)} %get-tuple-element.39.refs_0_), channel_id=1, source_target_pairs={{0,1},{1,2},{2,3},{3,4},{4,5},{5,6},{6,7},{7,8},{8,9},{9,10},{10,1... | collective-permute-start | bytes 61448 | tf_op jit(solution)/shard_map/ppermute | solution.py:422
  5.1 1.5 %collective-permute-start.2 = (bf16[256,256]{1,0:T(8,128)(2,1)}, bf16[256,256]{1,0:T(8,128)(2,1)S(1)}, u32[]{:S(2)}, u32[]{:S(2)}) collective-permute-start(bf16[256,256]{1,0:T(8,128)(2,1)} %get-tuple-element.45), channel_id=1, source_target_pairs={{0,65},{1,66},{2,67},{3,68},{4,69},{5,70},{6,71},{7,72},{8,73},{9,... | collective-permute-start | bytes 393224 | tf_op jit(solution)/shard_map/ppermute | solution.py:429
  7.2 0.0 copy-done.3
  7.2 0.0 copy-done.4
  7.3 0.0 copy-done.5
  7.3 0.0 copy-done.2
  7.3 1.6 %settle.1 = (bf16[2,256,256]{2,1,0:T(8,128)(2,1)S(1)}, f32[2,256,256]{2,1,0:T(8,128)S(1)}, bf16[256,256]{1,0:T(8,128)(2,1)S(1)}, bf16[256,256]{1,0:T(8,128)(2,1)S(1)}) custom-call(s32[1,2]{1,0:T(1,128)S(1)} %copy-done.3, s32[1,2]{1,0:T(1,128)S(1)} %copy-done.4, f32[5]{0:T(128)S(1)} %copy-done.5, bf16[1,2,2048,256]{3,2,1,0:T(8,128)(2,1)} %refs_0_.5, ...), custom_call_target="tpu_custom_call" | custom-call | flops 1000000000 | bytes 1572864 | tf_op jit(solution)/shard_map/settle/pallas_call | solution.py:397
  8.8 0.0 copy-done.7
  8.9 0.0 collective-permute-done.refs_4_.refs_1_
  8.9 0.0 copy-done.1
  8.9 0.9 %left_forward.1 = (bf16[1104,128]{1,0:T(8,128)(2,1)S(1)}, bf16[2,256,256]{2,1,0:T(8,128)(2,1)S(1)}, bf16[2,256,256]{2,1,0:T(8,128)(2,1)S(1)}, f32[8,128]{1,0:T(8,128)S(1)}) custom-call(bf16[80,128]{1,0:T(8,128)(2,1)S(1)} %copy-done.1, f32[16,128]{1,0:T(8,128)S(1)} %broadcast_in_dim.3.refs_1_, bf16[256,256]{1,0:T(8,128)(2,1)S(1)} %dynamic-slice_bitcast_fusion.refs_2_, ...), custom_call_target="tpu_custom_call" | custom-call | flops 1000000000 | bytes 4116480 | tf_op jit(solution)/shard_map/left_forward/pallas_call | solution.py:397
  9.8 0.0 copy-start
  9.8 1.0 %collective-permute-start.4 = (bf16[1104,128]{1,0:T(8,128)(2,1)S(1)}, bf16[1104,128]{1,0:T(8,128)(2,1)S(1)}, u32[]{:S(2)}, u32[]{:S(2)}) collective-permute-start(bf16[1104,128]{1,0:T(8,128)(2,1)S(1)} %get-tuple-element.44.refs_0_), channel_id=1, source_target_pairs={{0,1},{1,2},{2,3},{3,4},{4,5},{5,6},{6,7},{7,8},{8,9},{9,10},{10,1... | collective-permute-start | bytes 847880 | tf_op jit(solution)/shard_map/ppermute | solution.py:422
  10.8 2.9 %collective-permute-done.1.refs_0_.refs_2_.refs_1_ = bf16[80,128]{1,0:T(8,128)(2,1)S(1)} collective-permute-done((bf16[80,128]{1,0:T(8,128)(2,1)}, bf16[80,128]{1,0:T(8,128)(2,1)S(1)}, u32[]{:S(2)}, u32[]{:S(2)}) %collective-permute-start.1) | collective-permute-done | bytes 20512 | tf_op jit(solution)/shard_map/ppermute | solution.py:422
  13.7 0.7 %settle_left.1 = (f32[2,256,256]{2,1,0:T(8,128)S(1)}, bf16[256,256]{1,0:T(8,128)(2,1)S(1)}, bf16[256,256]{1,0:T(8,128)(2,1)S(1)}) custom-call(bf16[80,128]{1,0:T(8,128)(2,1)S(1)} %collective-permute-done.1.refs_0_.refs_2_.refs_1_, f32[2,256,256]{2,1,0:T(8,128)S(1)} %copy-done.2, f32[8,128]{1,0:T(8,128)S(1)} %get-tuple-element.46.refs_2_), custom_call_target="tpu_custom_call" | custom-call | flops 1000000000 | bytes 1331200 | tf_op jit(solution)/shard_map/settle_left/pallas_call | solution.py:397
  14.4 2.3 %collective-permute-done.2.refs_3_.refs_2_ = bf16[256,256]{1,0:T(8,128)(2,1)S(1)} collective-permute-done((bf16[256,256]{1,0:T(8,128)(2,1)}, bf16[256,256]{1,0:T(8,128)(2,1)S(1)}, u32[]{:S(2)}, u32[]{:S(2)}) %collective-permute-start.2) | collective-permute-done | bytes 131104 | tf_op jit(solution)/shard_map/ppermute | solution.py:429
  16.7 0.0 copy-done
  16.7 0.0 copy-start.6
  16.7 0.9 %right_forward.1 = (bf16[1056,128]{1,0:T(8,128)(2,1)S(1)}, bf16[2,256,256]{2,1,0:T(8,128)(2,1)S(1)}, bf16[2,256,256]{2,1,0:T(8,128)(2,1)S(1)}, f32[8,128]{1,0:T(8,128)S(1)}) custom-call(bf16[1,2,2048,256]{3,2,1,0:T(8,128)(2,1)S(1)} %copy-done, bf16[1,2,2048,256]{3,2,1,0:T(8,128)(2,1)S(1)} %collective-permute-done.refs_4_.refs_1_, ...), custom_call_target="tpu_custom_call" | custom-call | flops 1000000000 | bytes 5931008 | tf_op jit(solution)/shard_map/right_forward/pallas_call | solution.py:397
  17.6 1.5 %collective-permute-start.3 = (bf16[1056,128]{1,0:T(8,128)(2,1)S(1)}, bf16[1056,128]{1,0:T(8,128)(2,1)S(1)}, u32[]{:S(2)}, u32[]{:S(2)}) collective-permute-start(bf16[1056,128]{1,0:T(8,128)(2,1)S(1)} %get-tuple-element.50.refs_1_), channel_id=1, source_target_pairs={{0,63},{1,0},{2,1},{3,2},{4,3},{5,4},{6,5},{7,6},{8,7},{9,8},{10,9... | collective-permute-start | bytes 811016 | tf_op jit(solution)/shard_map/ppermute | solution.py:425
  19.2 0.0 copy-done.6
  19.2 1.0 %tables_left.1 = (bf16[512,512]{1,0:T(8,128)(2,1)S(1)}, bf16[512,512]{1,0:T(8,128)(2,1)S(1)}, bf16[512,512]{1,0:T(8,128)(2,1)S(1)}, bf16[512,512]{1,0:T(8,128)(2,1)S(1)}, f32[8,128]{1,0:T(8,128)S(1)}) custom-call(bf16[80,128]{1,0:T(8,128)(2,1)S(1)} %collective-permute-done.1.refs_0_.refs_2_.refs_1_, bf16[512,256]{1,0:T(8,128)(2,1)S(1)} %copy-done.6, ...), custom_call_target="tpu_custom_call" | custom-call | flops 1000000000 | bytes 2646016 | tf_op jit(solution)/shard_map/tables_left/pallas_call | solution.py:397
  20.2 1.0 %tables.1 = (bf16[512,512]{1,0:T(8,128)(2,1)S(1)}, bf16[512,512]{1,0:T(8,128)(2,1)S(1)}, bf16[512,512]{1,0:T(8,128)(2,1)S(1)}, bf16[512,512]{1,0:T(8,128)(2,1)S(1)}, f32[8,128]{1,0:T(8,128)S(1)}) custom-call(bf16[80,128]{1,0:T(8,128)(2,1)S(1)} %copy-done.1, bf16[512,256]{1,0:T(8,128)(2,1)S(1)} %copy-done.6, ...), custom_call_target="tpu_custom_call" | custom-call | flops 1000000000 | bytes 2646016 | tf_op jit(solution)/shard_map/tables/pallas_call | solution.py:397
  21.2 2.3 %collective-permute-done.4.refs_0_ = bf16[1104,128]{1,0:T(8,128)(2,1)S(1)} collective-permute-done((bf16[1104,128]{1,0:T(8,128)(2,1)S(1)}, bf16[1104,128]{1,0:T(8,128)(2,1)S(1)}, u32[]{:S(2)}, u32[]{:S(2)}) %collective-permute-start.4) | collective-permute-done | bytes 282656 | tf_op jit(solution)/shard_map/ppermute | solution.py:422
  23.5 2.0 %far_field_1.1 = (bf16[2,256,256]{2,1,0:T(8,128)(2,1)S(1)}, bf16[2,256,256]{2,1,0:T(8,128)(2,1)S(1)}, f32[8,128]{1,0:T(8,128)S(1)}) custom-call(bf16[1104,128]{1,0:T(8,128)(2,1)S(1)} %collective-permute-done.4.refs_0_, bf16[1056,128]{1,0:T(8,128)(2,1)S(1)} %get-tuple-element.50.refs_1_, bf16[256,256]{1,0:T(8,128)(2,1)S(1)} %collective-permute-done.2.refs_3_.refs_2_, ...), custom_call_target="tpu_custom_call" | custom-call | flops 1000000000 | bytes 4620288 | tf_op jit(solution)/shard_map/far_field_1/pallas_call | solution.py:397
  25.5 1.0 %collective-permute-start.6 = (bf16[2,256,256]{2,1,0:T(8,128)(2,1)S(1)}, bf16[2,256,256]{2,1,0:T(8,128)(2,1)S(1)}, u32[]{:S(2)}, u32[]{:S(2)}) collective-permute-start(bf16[2,256,256]{2,1,0:T(8,128)(2,1)S(1)} %get-tuple-element.70), channel_id=1, source_target_pairs={{0,64},{64,0},{1,65},{65,1},{2,66},{66,2},{3,67},{67,3},{4,68},{68... | collective-permute-start | bytes 786440 | tf_op jit(solution)/shard_map/ppermute | solution.py:432
  26.5 0.0 collective-permute-done.3.refs_1_
  26.5 2.0 %far_field_0.1 = (bf16[2,256,256]{2,1,0:T(8,128)(2,1)S(1)}, bf16[2,256,256]{2,1,0:T(8,128)(2,1)S(1)}) custom-call(bf16[1104,128]{1,0:T(8,128)(2,1)S(1)} %get-tuple-element.44.refs_0_, bf16[1056,128]{1,0:T(8,128)(2,1)S(1)} %collective-permute-done.3.refs_1_, bf16[256,256]{1,0:T(8,128)(2,1)S(1)} %dynamic-slice_bitcast_fusion.refs_2_, ...), custom_call_target="tpu_custom_call" | custom-call | flops 1000000000 | bytes 4616192 | tf_op jit(solution)/shard_map/far_field_0/pallas_call | solution.py:397
  28.5 0.2 collective-permute-start.5
  28.7 0.0 collective-permute-done.6.refs_4_
  28.7 1.6 %lay_out.1 = (bf16[1,2,2048,256]{3,2,1,0:T(8,128)(2,1)}, bf16[2,2048,256]{2,1,0:T(8,128)(2,1)S(1)}) custom-call(bf16[80,128]{1,0:T(8,128)(2,1)S(1)} %copy-done.1, bf16[80,128]{1,0:T(8,128)(2,1)S(1)} %collective-permute-done.1.refs_0_.refs_2_.refs_1_, bf16[2,256,256]{2,1,0:T(8,128)(2,1)S(1)} %get-tuple-element.68.refs_2_, ...), custom_call_target="tpu_custom_call" | custom-call | flops 1000000000 | bytes 5021696 | tf_op jit(solution)/shard_map/lay_out/pallas_call | solution.py:397
  30.3 0.0 collective-permute-done.5.refs_1_
  30.3 0.9 %finish.1 = bf16[1,2,2048,256]{3,2,1,0:T(8,128)(2,1)} custom-call(bf16[80,128]{1,0:T(8,128)(2,1)S(1)} %copy-done.1, bf16[2,256,256]{2,1,0:T(8,128)(2,1)S(1)} %collective-permute-done.5.refs_1_, bf16[2,2048,256]{2,1,0:T(8,128)(2,1)S(1)} %get-tuple-element.71.refs_2_, bf16[1,2,2048,256]{3,2,1,0:T(8,128)(2,1)} %get-tuple-element.72.refs_3_), custom_call_target="tpu_custom_call", output_to_operand_aliasing={{}: (3, {})} | custom-call | flops 1000000000 | bytes 4476928 | tf_op jit(solution)/shard_map/finish/pallas_call | solution.py:397
  (2 shorter events, 0.0 us)
Async XLA Ops:
  0.0 7.2 %copy-start.3 = (s32[1,2]{1,0:T(1,128)S(1)}, s32[1,2]{1,0:T(1,128)}, u32[]{:S(2)}) copy-start(s32[1,2]{1,0:T(1,128)} %refs_0_.4) | copy-start | bytes 28
  0.0 7.2 %copy-start.4 = (s32[1,2]{1,0:T(1,128)S(1)}, s32[1,2]{1,0:T(1,128)}, u32[]{:S(2)}) copy-start(s32[1,2]{1,0:T(1,128)} %refs_1_.6) | copy-start | bytes 28
  0.0 7.3 %copy-start.5 = (f32[5]{0:T(128)S(1)}, f32[5]{0:T(128)}, u32[]{:S(2)}) copy-start(f32[5]{0:T(128)} %refs_2_.3) | copy-start | bytes 64
  0.0 7.3 %copy-start.2 = (f32[2,256,256]{2,1,0:T(8,128)S(1)}, f32[2,256,256]{2,1,0:T(8,128)}, u32[]{:S(2)}) copy-start(f32[2,256,256]{2,1,0:T(8,128)} %refs_1_.7) | copy-start | bytes 1572868
  0.0 8.9 %collective-permute-start = (bf16[1,2,2048,256]{3,2,1,0:T(8,128)(2,1)}, bf16[1,2,2048,256]{3,2,1,0:T(8,128)(2,1)S(1)}, u32[]{:S(2)}, u32[]{:S(2)}) collective-permute-start(bf16[1,2,2048,256]{3,2,1,0:T(8,128)(2,1)} %refs_0_.5), channel_id=1, source_target_pairs={{0,64},{64,0},{1,65},{65,1},{2,66},{66,2},{3,67},{67,3},{4,68},{68... | collective-permute-start | bytes 6291464 | tf_op jit(solution)/shard_map/ppermute | solution.py:432
  3.7 5.1 %copy-start.7 = (bf16[1,2,256,256]{3,2,1,0:T(8,128)(2,1)S(1)}, bf16[1,2,256,256]{3,2,1,0:T(8,128)(2,1)}, u32[]{:S(2)}) copy-start(bf16[1,2,256,256]{3,2,1,0:T(8,128)(2,1)} %refs_4_.2) | copy-start | bytes 786436
  3.7 5.2 %copy-start.1 = (bf16[80,128]{1,0:T(8,128)(2,1)S(1)}, bf16[80,128]{1,0:T(8,128)(2,1)}, u32[]{:S(2)}) copy-start(bf16[80,128]{1,0:T(8,128)(2,1)} %get-tuple-element.39.refs_0_) | copy-start | bytes 61444
  3.7 10.0 %collective-permute-start.1 = (bf16[80,128]{1,0:T(8,128)(2,1)}, bf16[80,128]{1,0:T(8,128)(2,1)S(1)}, u32[]{:S(2)}, u32[]{:S(2)}) collective-permute-start(bf16[80,128]{1,0:T(8,128)(2,1)} %get-tuple-element.39.refs_0_), channel_id=1, source_target_pairs={{0,1},{1,2},{2,3},{3,4},{4,5},{5,6},{6,7},{7,8},{8,9},{9,10},{10,1... | collective-permute-start | bytes 61448 | tf_op jit(solution)/shard_map/ppermute | solution.py:422
  5.1 11.6 %collective-permute-start.2 = (bf16[256,256]{1,0:T(8,128)(2,1)}, bf16[256,256]{1,0:T(8,128)(2,1)S(1)}, u32[]{:S(2)}, u32[]{:S(2)}) collective-permute-start(bf16[256,256]{1,0:T(8,128)(2,1)} %get-tuple-element.45), channel_id=1, source_target_pairs={{0,65},{1,66},{2,67},{3,68},{4,69},{5,70},{6,71},{7,72},{8,73},{9,... | collective-permute-start | bytes 393224 | tf_op jit(solution)/shard_map/ppermute | solution.py:429
  9.8 6.9 %copy-start = (bf16[1,2,2048,256]{3,2,1,0:T(8,128)(2,1)S(1)}, bf16[1,2,2048,256]{3,2,1,0:T(8,128)(2,1)}, u32[]{:S(2)}) copy-start(bf16[1,2,2048,256]{3,2,1,0:T(8,128)(2,1)} %refs_0_.5) | copy-start | bytes 6291460
  9.8 13.7 %collective-permute-start.4 = (bf16[1104,128]{1,0:T(8,128)(2,1)S(1)}, bf16[1104,128]{1,0:T(8,128)(2,1)S(1)}, u32[]{:S(2)}, u32[]{:S(2)}) collective-permute-start(bf16[1104,128]{1,0:T(8,128)(2,1)S(1)} %get-tuple-element.44.refs_0_), channel_id=1, source_target_pairs={{0,1},{1,2},{2,3},{3,4},{4,5},{5,6},{6,7},{7,8},{8,9},{9,10},{10,1... | collective-permute-start | bytes 847880 | tf_op jit(solution)/shard_map/ppermute | solution.py:422
  16.7 2.5 %copy-start.6 = (bf16[512,256]{1,0:T(8,128)(2,1)S(1)}, bf16[512,256]{1,0:T(8,128)(2,1)}, u32[]{:S(2)}) copy-start(bf16[512,256]{1,0:T(8,128)(2,1)} %constant.15.clone.refs_1_) | copy-start | bytes 786436
  17.6 8.9 %collective-permute-start.3 = (bf16[1056,128]{1,0:T(8,128)(2,1)S(1)}, bf16[1056,128]{1,0:T(8,128)(2,1)S(1)}, u32[]{:S(2)}, u32[]{:S(2)}) collective-permute-start(bf16[1056,128]{1,0:T(8,128)(2,1)S(1)} %get-tuple-element.50.refs_1_), channel_id=1, source_target_pairs={{0,63},{1,0},{2,1},{3,2},{4,3},{5,4},{6,5},{7,6},{8,7},{9,8},{10,9... | collective-permute-start | bytes 811016 | tf_op jit(solution)/shard_map/ppermute | solution.py:425
  25.5 3.2 %collective-permute-start.6 = (bf16[2,256,256]{2,1,0:T(8,128)(2,1)S(1)}, bf16[2,256,256]{2,1,0:T(8,128)(2,1)S(1)}, u32[]{:S(2)}, u32[]{:S(2)}) collective-permute-start(bf16[2,256,256]{2,1,0:T(8,128)(2,1)S(1)} %get-tuple-element.70), channel_id=1, source_target_pairs={{0,64},{64,0},{1,65},{65,1},{2,66},{66,2},{3,67},{67,3},{4,68},{68... | collective-permute-start | bytes 786440 | tf_op jit(solution)/shard_map/ppermute | solution.py:432
  28.5 1.8 %collective-permute-start.5 = (bf16[2,256,256]{2,1,0:T(8,128)(2,1)S(1)}, bf16[2,256,256]{2,1,0:T(8,128)(2,1)S(1)}, u32[]{:S(2)}, u32[]{:S(2)}) collective-permute-start(bf16[2,256,256]{2,1,0:T(8,128)(2,1)S(1)} %get-tuple-element.67), channel_id=1, source_target_pairs={{0,64},{64,0},{1,65},{65,1},{2,66},{66,2},{3,67},{67,3},{4,68},{68... | collective-permute-start | bytes 786440 | tf_op jit(solution)/shard_map/ppermute | solution.py:432

commit v6 on v5

--- a/solution.py
+++ b/solution.py
@@ -354,11 +354,9 @@
         buf[i] = jnp.zeros((height, W), BF)
         for base, offset, term in work:
             add_part(buf, i, base, offset, term)
-        for k in range(4):
-            rows = pl.ds(k * (height // 4), height // 4)
-            copy = pltpu.make_async_copy(buf.at[i, rows, :], out.at[0, i, rows, :], sems.at[i, k])
-            copy.start()
-            copies.append(copy)
+        copy = pltpu.make_async_copy(buf.at[i], out.at[0, i], sems.at[i])
+        copy.start()
+        copies.append(copy)
     for copy in copies:
         copy.wait()
 
@@ -493,7 +491,7 @@
 
     laid_out, laid = call(
         lay_out, "lay_out", [VMEM] * 5, [(transmission.shape, BF), ((2, height, W), BF)],
-        [strip_keep, strip_a, l_keep, r_keep, r_recv], [pltpu.SemaphoreType.DMA((2, 4))], out_specs=[HBM, VMEM],
+        [strip_keep, strip_a, l_keep, r_keep, r_recv], [pltpu.SemaphoreType.DMA((2,))], out_specs=[HBM, VMEM],
     )
     return call(
         finish, "finish", [VMEM] * 3 + [HBM], [(transmission.shape, BF)], [strip_keep, l_recv, laid, laid_out],

time: 31.3 us -> 31.3 us (level)
  no operation moved by 1% of the time
where the time goes in v6:
time: 31.3 us; the launch traced here: 31.1 us
  Pallas kernels  14.6 us (47%)
  starting transfers between devices  8.08 us (26%)
  waiting for transfers between devices  7.52 us (24%)
  between operations  0.85 us (3%)
    pallas_call x11, Pallas kernels, call(): pl.pallas_call(body, name=name, out_shape=[jax.ShapeDtypeStruct(shape, ki...  14.6 us
    ppermute x2, waiting for transfers between devices, to_right(): return lax.ppermute(x, 'tile', [(i, (i + 1) % tiles) for i in range(tiles)])  5.18 us
    ppermute x3, starting transfers between devices, to_other(): return lax.ppermute(x, 'depth', [(0, 1), (1, 0)])  2.7 us
    ppermute x2, starting transfers between devices, to_right(): return lax.ppermute(x, 'tile', [(i, (i + 1) % tiles) for i in range(tiles)])  2.38 us
    ppermute x1, waiting for transfers between devices, to_right_other(): return lax.ppermute(x, ('depth', 'tile'), pairs)  2.33 us
    ppermute x1, starting transfers between devices, to_left(): return lax.ppermute(x, 'tile', [(i, (i - 1) % tiles) for i in range(tiles)])  1.54 us
    ppermute x1, starting transfers between devices, to_right_other(): return lax.ppermute(x, ('depth', 'tile'), pairs)  1.46 us
  transfers between devices with their start and end apart: 7, of which 3 were waited for; matrix products, arithmetic and copies ran while one was open for 0% of the time, Pallas kernels for 44%

profile of v6, /device:TPU:1, one launch (start us, length us, event | category | flops | bytes accessed | tf_op | source)
XLA Modules:
  0.0 31.1 jit_solution(625081370201732766)
XLA Ops:
  0.0 0.0 copy-start.3
  0.0 0.0 copy-start.4
  0.0 0.0 copy-start.5
  0.0 0.0 copy-start.2
  0.0 1.5 %collective-permute-start = (bf16[1,2,2048,256]{3,2,1,0:T(8,128)(2,1)}, bf16[1,2,2048,256]{3,2,1,0:T(8,128)(2,1)S(1)}, u32[]{:S(2)}, u32[]{:S(2)}) collective-permute-start(bf16[1,2,2048,256]{3,2,1,0:T(8,128)(2,1)} %refs_0_.5), channel_id=1, source_target_pairs={{0,64},{64,0},{1,65},{65,1},{2,66},{66,2},{3,67},{67,3},{4,68},{68... | collective-permute-start | bytes 6291464 | tf_op jit(solution)/shard_map/ppermute | solution.py:430
  1.5 2.2 %edges.1 = (bf16[80,128]{1,0:T(8,128)(2,1)}, bf16[256,256]{1,0:T(8,128)(2,1)}) custom-call(s32[1,2]{1,0:T(1,128)} %refs_0_.4, s32[1,2]{1,0:T(1,128)} %refs_1_.6, f32[5]{0:T(128)} %refs_2_.3, bf16[1,2,2048,256]{3,2,1,0:T(8,128)(2,1)} %refs_0_.5, bf16[1,2,256,256]{3,2,1,0:T(8,128)(2,1)} %refs_4_.2), custom_call_target="tpu_custom_call" | custom-call | flops 1000000000 | bytes 151552 | tf_op jit(solution)/shard_map/edges/pallas_call | solution.py:395
  3.7 0.0 copy-start.7
  3.7 0.0 copy-start.1
  3.7 1.4 %collective-permute-start.1 = (bf16[80,128]{1,0:T(8,128)(2,1)}, bf16[80,128]{1,0:T(8,128)(2,1)S(1)}, u32[]{:S(2)}, u32[]{:S(2)}) collective-permute-start(bf16[80,128]{1,0:T(8,128)(2,1)} %get-tuple-element.39.refs_0_), channel_id=1, source_target_pairs={{0,1},{1,2},{2,3},{3,4},{4,5},{5,6},{6,7},{7,8},{8,9},{9,10},{10,1... | collective-permute-start | bytes 61448 | tf_op jit(solution)/shard_map/ppermute | solution.py:420
  5.1 1.5 %collective-permute-start.2 = (bf16[256,256]{1,0:T(8,128)(2,1)}, bf16[256,256]{1,0:T(8,128)(2,1)S(1)}, u32[]{:S(2)}, u32[]{:S(2)}) collective-permute-start(bf16[256,256]{1,0:T(8,128)(2,1)} %get-tuple-element.45), channel_id=1, source_target_pairs={{0,65},{1,66},{2,67},{3,68},{4,69},{5,70},{6,71},{7,72},{8,73},{9,... | collective-permute-start | bytes 393224 | tf_op jit(solution)/shard_map/ppermute | solution.py:427
  7.2 0.0 copy-done.3
  7.2 0.0 copy-done.4
  7.3 0.0 copy-done.5
  7.3 0.0 copy-done.2
  7.3 1.6 %settle.1 = (bf16[2,256,256]{2,1,0:T(8,128)(2,1)S(1)}, f32[2,256,256]{2,1,0:T(8,128)S(1)}, bf16[256,256]{1,0:T(8,128)(2,1)S(1)}, bf16[256,256]{1,0:T(8,128)(2,1)S(1)}) custom-call(s32[1,2]{1,0:T(1,128)S(1)} %copy-done.3, s32[1,2]{1,0:T(1,128)S(1)} %copy-done.4, f32[5]{0:T(128)S(1)} %copy-done.5, bf16[1,2,2048,256]{3,2,1,0:T(8,128)(2,1)} %refs_0_.5, ...), custom_call_target="tpu_custom_call" | custom-call | flops 1000000000 | bytes 1572864 | tf_op jit(solution)/shard_map/settle/pallas_call | solution.py:395
  8.8 0.0 copy-done.7
  8.9 0.0 collective-permute-done.refs_4_.refs_1_
  8.9 0.0 copy-done.1
  8.9 0.9 %left_forward.1 = (bf16[1104,128]{1,0:T(8,128)(2,1)S(1)}, bf16[2,256,256]{2,1,0:T(8,128)(2,1)S(1)}, bf16[2,256,256]{2,1,0:T(8,128)(2,1)S(1)}, f32[8,128]{1,0:T(8,128)S(1)}) custom-call(bf16[80,128]{1,0:T(8,128)(2,1)S(1)} %copy-done.1, f32[16,128]{1,0:T(8,128)S(1)} %broadcast_in_dim.3.refs_1_, bf16[256,256]{1,0:T(8,128)(2,1)S(1)} %dynamic-slice_bitcast_fusion.refs_2_, ...), custom_call_target="tpu_custom_call" | custom-call | flops 1000000000 | bytes 4116480 | tf_op jit(solution)/shard_map/left_forward/pallas_call | solution.py:395
  9.8 0.0 copy-start
  9.8 1.0 %collective-permute-start.4 = (bf16[1104,128]{1,0:T(8,128)(2,1)S(1)}, bf16[1104,128]{1,0:T(8,128)(2,1)S(1)}, u32[]{:S(2)}, u32[]{:S(2)}) collective-permute-start(bf16[1104,128]{1,0:T(8,128)(2,1)S(1)} %get-tuple-element.44.refs_0_), channel_id=1, source_target_pairs={{0,1},{1,2},{2,3},{3,4},{4,5},{5,6},{6,7},{7,8},{8,9},{9,10},{10,1... | collective-permute-start | bytes 847880 | tf_op jit(solution)/shard_map/ppermute | solution.py:420
  10.8 2.9 %collective-permute-done.1.refs_0_.refs_2_.refs_1_ = bf16[80,128]{1,0:T(8,128)(2,1)S(1)} collective-permute-done((bf16[80,128]{1,0:T(8,128)(2,1)}, bf16[80,128]{1,0:T(8,128)(2,1)S(1)}, u32[]{:S(2)}, u32[]{:S(2)}) %collective-permute-start.1) | collective-permute-done | bytes 20512 | tf_op jit(solution)/shard_map/ppermute | solution.py:420
  13.7 0.7 %settle_left.1 = (f32[2,256,256]{2,1,0:T(8,128)S(1)}, bf16[256,256]{1,0:T(8,128)(2,1)S(1)}, bf16[256,256]{1,0:T(8,128)(2,1)S(1)}) custom-call(bf16[80,128]{1,0:T(8,128)(2,1)S(1)} %collective-permute-done.1.refs_0_.refs_2_.refs_1_, f32[2,256,256]{2,1,0:T(8,128)S(1)} %copy-done.2, f32[8,128]{1,0:T(8,128)S(1)} %get-tuple-element.46.refs_2_), custom_call_target="tpu_custom_call" | custom-call | flops 1000000000 | bytes 1331200 | tf_op jit(solution)/shard_map/settle_left/pallas_call | solution.py:395
  14.4 2.3 %collective-permute-done.2.refs_3_.refs_2_ = bf16[256,256]{1,0:T(8,128)(2,1)S(1)} collective-permute-done((bf16[256,256]{1,0:T(8,128)(2,1)}, bf16[256,256]{1,0:T(8,128)(2,1)S(1)}, u32[]{:S(2)}, u32[]{:S(2)}) %collective-permute-start.2) | collective-permute-done | bytes 131104 | tf_op jit(solution)/shard_map/ppermute | solution.py:427
  16.7 0.0 copy-done
  16.7 0.0 copy-start.6
  16.7 0.9 %right_forward.1 = (bf16[1056,128]{1,0:T(8,128)(2,1)S(1)}, bf16[2,256,256]{2,1,0:T(8,128)(2,1)S(1)}, bf16[2,256,256]{2,1,0:T(8,128)(2,1)S(1)}, f32[8,128]{1,0:T(8,128)S(1)}) custom-call(bf16[1,2,2048,256]{3,2,1,0:T(8,128)(2,1)S(1)} %copy-done, bf16[1,2,2048,256]{3,2,1,0:T(8,128)(2,1)S(1)} %collective-permute-done.refs_4_.refs_1_, ...), custom_call_target="tpu_custom_call" | custom-call | flops 1000000000 | bytes 5931008 | tf_op jit(solution)/shard_map/right_forward/pallas_call | solution.py:395
  17.6 1.5 %collective-permute-start.3 = (bf16[1056,128]{1,0:T(8,128)(2,1)S(1)}, bf16[1056,128]{1,0:T(8,128)(2,1)S(1)}, u32[]{:S(2)}, u32[]{:S(2)}) collective-permute-start(bf16[1056,128]{1,0:T(8,128)(2,1)S(1)} %get-tuple-element.50.refs_1_), channel_id=1, source_target_pairs={{0,63},{1,0},{2,1},{3,2},{4,3},{5,4},{6,5},{7,6},{8,7},{9,8},{10,9... | collective-permute-start | bytes 811016 | tf_op jit(solution)/shard_map/ppermute | solution.py:423
  19.2 0.0 copy-done.6
  19.2 1.0 %tables_left.1 = (bf16[512,512]{1,0:T(8,128)(2,1)S(1)}, bf16[512,512]{1,0:T(8,128)(2,1)S(1)}, bf16[512,512]{1,0:T(8,128)(2,1)S(1)}, bf16[512,512]{1,0:T(8,128)(2,1)S(1)}, f32[8,128]{1,0:T(8,128)S(1)}) custom-call(bf16[80,128]{1,0:T(8,128)(2,1)S(1)} %collective-permute-done.1.refs_0_.refs_2_.refs_1_, bf16[512,256]{1,0:T(8,128)(2,1)S(1)} %copy-done.6, ...), custom_call_target="tpu_custom_call" | custom-call | flops 1000000000 | bytes 2646016 | tf_op jit(solution)/shard_map/tables_left/pallas_call | solution.py:395
  20.2 1.0 %tables.1 = (bf16[512,512]{1,0:T(8,128)(2,1)S(1)}, bf16[512,512]{1,0:T(8,128)(2,1)S(1)}, bf16[512,512]{1,0:T(8,128)(2,1)S(1)}, bf16[512,512]{1,0:T(8,128)(2,1)S(1)}, f32[8,128]{1,0:T(8,128)S(1)}) custom-call(bf16[80,128]{1,0:T(8,128)(2,1)S(1)} %copy-done.1, bf16[512,256]{1,0:T(8,128)(2,1)S(1)} %copy-done.6, ...), custom_call_target="tpu_custom_call" | custom-call | flops 1000000000 | bytes 2646016 | tf_op jit(solution)/shard_map/tables/pallas_call | solution.py:395
  21.2 2.3 %collective-permute-done.4.refs_0_ = bf16[1104,128]{1,0:T(8,128)(2,1)S(1)} collective-permute-done((bf16[1104,128]{1,0:T(8,128)(2,1)S(1)}, bf16[1104,128]{1,0:T(8,128)(2,1)S(1)}, u32[]{:S(2)}, u32[]{:S(2)}) %collective-permute-start.4) | collective-permute-done | bytes 282656 | tf_op jit(solution)/shard_map/ppermute | solution.py:420
  23.5 2.0 %far_field_1.1 = (bf16[2,256,256]{2,1,0:T(8,128)(2,1)S(1)}, bf16[2,256,256]{2,1,0:T(8,128)(2,1)S(1)}, f32[8,128]{1,0:T(8,128)S(1)}) custom-call(bf16[1104,128]{1,0:T(8,128)(2,1)S(1)} %collective-permute-done.4.refs_0_, bf16[1056,128]{1,0:T(8,128)(2,1)S(1)} %get-tuple-element.50.refs_1_, bf16[256,256]{1,0:T(8,128)(2,1)S(1)} %collective-permute-done.2.refs_3_.refs_2_, ...), custom_call_target="tpu_custom_call" | custom-call | flops 1000000000 | bytes 4620288 | tf_op jit(solution)/shard_map/far_field_1/pallas_call | solution.py:395
  25.5 1.0 %collective-permute-start.6 = (bf16[2,256,256]{2,1,0:T(8,128)(2,1)S(1)}, bf16[2,256,256]{2,1,0:T(8,128)(2,1)S(1)}, u32[]{:S(2)}, u32[]{:S(2)}) collective-permute-start(bf16[2,256,256]{2,1,0:T(8,128)(2,1)S(1)} %get-tuple-element.70), channel_id=1, source_target_pairs={{0,64},{64,0},{1,65},{65,1},{2,66},{66,2},{3,67},{67,3},{4,68},{68... | collective-permute-start | bytes 786440 | tf_op jit(solution)/shard_map/ppermute | solution.py:430
  26.5 0.0 collective-permute-done.3.refs_1_
  26.5 2.0 %far_field_0.1 = (bf16[2,256,256]{2,1,0:T(8,128)(2,1)S(1)}, bf16[2,256,256]{2,1,0:T(8,128)(2,1)S(1)}) custom-call(bf16[1104,128]{1,0:T(8,128)(2,1)S(1)} %get-tuple-element.44.refs_0_, bf16[1056,128]{1,0:T(8,128)(2,1)S(1)} %collective-permute-done.3.refs_1_, bf16[256,256]{1,0:T(8,128)(2,1)S(1)} %dynamic-slice_bitcast_fusion.refs_2_, ...), custom_call_target="tpu_custom_call" | custom-call | flops 1000000000 | bytes 4616192 | tf_op jit(solution)/shard_map/far_field_0/pallas_call | solution.py:395
  28.5 0.2 collective-permute-start.5
  28.7 0.0 collective-permute-done.6.refs_4_
  28.7 1.5 %lay_out.1 = (bf16[1,2,2048,256]{3,2,1,0:T(8,128)(2,1)}, bf16[2,2048,256]{2,1,0:T(8,128)(2,1)S(1)}) custom-call(bf16[80,128]{1,0:T(8,128)(2,1)S(1)} %copy-done.1, bf16[80,128]{1,0:T(8,128)(2,1)S(1)} %collective-permute-done.1.refs_0_.refs_2_.refs_1_, bf16[2,256,256]{2,1,0:T(8,128)(2,1)S(1)} %get-tuple-element.68.refs_2_, ...), custom_call_target="tpu_custom_call" | custom-call | flops 1000000000 | bytes 5021696 | tf_op jit(solution)/shard_map/lay_out/pallas_call | solution.py:395
  30.2 0.0 collective-permute-done.5.refs_1_
  30.2 0.9 %finish.1 = bf16[1,2,2048,256]{3,2,1,0:T(8,128)(2,1)} custom-call(bf16[80,128]{1,0:T(8,128)(2,1)S(1)} %copy-done.1, bf16[2,256,256]{2,1,0:T(8,128)(2,1)S(1)} %collective-permute-done.5.refs_1_, bf16[2,2048,256]{2,1,0:T(8,128)(2,1)S(1)} %get-tuple-element.71.refs_2_, bf16[1,2,2048,256]{3,2,1,0:T(8,128)(2,1)} %get-tuple-element.72.refs_3_), custom_call_target="tpu_custom_call", output_to_operand_aliasing={{}: (3, {})} | custom-call | flops 1000000000 | bytes 4476928 | tf_op jit(solution)/shard_map/finish/pallas_call | solution.py:395
  (2 shorter events, 0.0 us)
Async XLA Ops:
  0.0 7.2 %copy-start.3 = (s32[1,2]{1,0:T(1,128)S(1)}, s32[1,2]{1,0:T(1,128)}, u32[]{:S(2)}) copy-start(s32[1,2]{1,0:T(1,128)} %refs_0_.4) | copy-start | bytes 28
  0.0 7.2 %copy-start.4 = (s32[1,2]{1,0:T(1,128)S(1)}, s32[1,2]{1,0:T(1,128)}, u32[]{:S(2)}) copy-start(s32[1,2]{1,0:T(1,128)} %refs_1_.6) | copy-start | bytes 28
  0.0 7.3 %copy-start.5 = (f32[5]{0:T(128)S(1)}, f32[5]{0:T(128)}, u32[]{:S(2)}) copy-start(f32[5]{0:T(128)} %refs_2_.3) | copy-start | bytes 64
  0.0 7.3 %copy-start.2 = (f32[2,256,256]{2,1,0:T(8,128)S(1)}, f32[2,256,256]{2,1,0:T(8,128)}, u32[]{:S(2)}) copy-start(f32[2,256,256]{2,1,0:T(8,128)} %refs_1_.7) | copy-start | bytes 1572868
  0.0 8.9 %collective-permute-start = (bf16[1,2,2048,256]{3,2,1,0:T(8,128)(2,1)}, bf16[1,2,2048,256]{3,2,1,0:T(8,128)(2,1)S(1)}, u32[]{:S(2)}, u32[]{:S(2)}) collective-permute-start(bf16[1,2,2048,256]{3,2,1,0:T(8,128)(2,1)} %refs_0_.5), channel_id=1, source_target_pairs={{0,64},{64,0},{1,65},{65,1},{2,66},{66,2},{3,67},{67,3},{4,68},{68... | collective-permute-start | bytes 6291464 | tf_op jit(solution)/shard_map/ppermute | solution.py:430
  3.7 5.1 %copy-start.7 = (bf16[1,2,256,256]{3,2,1,0:T(8,128)(2,1)S(1)}, bf16[1,2,256,256]{3,2,1,0:T(8,128)(2,1)}, u32[]{:S(2)}) copy-start(bf16[1,2,256,256]{3,2,1,0:T(8,128)(2,1)} %refs_4_.2) | copy-start | bytes 786436
  3.7 5.2 %copy-start.1 = (bf16[80,128]{1,0:T(8,128)(2,1)S(1)}, bf16[80,128]{1,0:T(8,128)(2,1)}, u32[]{:S(2)}) copy-start(bf16[80,128]{1,0:T(8,128)(2,1)} %get-tuple-element.39.refs_0_) | copy-start | bytes 61444
  3.7 10.0 %collective-permute-start.1 = (bf16[80,128]{1,0:T(8,128)(2,1)}, bf16[80,128]{1,0:T(8,128)(2,1)S(1)}, u32[]{:S(2)}, u32[]{:S(2)}) collective-permute-start(bf16[80,128]{1,0:T(8,128)(2,1)} %get-tuple-element.39.refs_0_), channel_id=1, source_target_pairs={{0,1},{1,2},{2,3},{3,4},{4,5},{5,6},{6,7},{7,8},{8,9},{9,10},{10,1... | collective-permute-start | bytes 61448 | tf_op jit(solution)/shard_map/ppermute | solution.py:420
  5.1 11.6 %collective-permute-start.2 = (bf16[256,256]{1,0:T(8,128)(2,1)}, bf16[256,256]{1,0:T(8,128)(2,1)S(1)}, u32[]{:S(2)}, u32[]{:S(2)}) collective-permute-start(bf16[256,256]{1,0:T(8,128)(2,1)} %get-tuple-element.45), channel_id=1, source_target_pairs={{0,65},{1,66},{2,67},{3,68},{4,69},{5,70},{6,71},{7,72},{8,73},{9,... | collective-permute-start | bytes 393224 | tf_op jit(solution)/shard_map/ppermute | solution.py:427
  9.8 6.9 %copy-start = (bf16[1,2,2048,256]{3,2,1,0:T(8,128)(2,1)S(1)}, bf16[1,2,2048,256]{3,2,1,0:T(8,128)(2,1)}, u32[]{:S(2)}) copy-start(bf16[1,2,2048,256]{3,2,1,0:T(8,128)(2,1)} %refs_0_.5) | copy-start | bytes 6291460
  9.8 13.7 %collective-permute-start.4 = (bf16[1104,128]{1,0:T(8,128)(2,1)S(1)}, bf16[1104,128]{1,0:T(8,128)(2,1)S(1)}, u32[]{:S(2)}, u32[]{:S(2)}) collective-permute-start(bf16[1104,128]{1,0:T(8,128)(2,1)S(1)} %get-tuple-element.44.refs_0_), channel_id=1, source_target_pairs={{0,1},{1,2},{2,3},{3,4},{4,5},{5,6},{6,7},{7,8},{8,9},{9,10},{10,1... | collective-permute-start | bytes 847880 | tf_op jit(solution)/shard_map/ppermute | solution.py:420
  16.7 2.5 %copy-start.6 = (bf16[512,256]{1,0:T(8,128)(2,1)S(1)}, bf16[512,256]{1,0:T(8,128)(2,1)}, u32[]{:S(2)}) copy-start(bf16[512,256]{1,0:T(8,128)(2,1)} %constant.15.clone.refs_1_) | copy-start | bytes 786436
  17.6 8.9 %collective-permute-start.3 = (bf16[1056,128]{1,0:T(8,128)(2,1)S(1)}, bf16[1056,128]{1,0:T(8,128)(2,1)S(1)}, u32[]{:S(2)}, u32[]{:S(2)}) collective-permute-start(bf16[1056,128]{1,0:T(8,128)(2,1)S(1)} %get-tuple-element.50.refs_1_), channel_id=1, source_target_pairs={{0,63},{1,0},{2,1},{3,2},{4,3},{5,4},{6,5},{7,6},{8,7},{9,8},{10,9... | collective-permute-start | bytes 811016 | tf_op jit(solution)/shard_map/ppermute | solution.py:423
  25.5 3.2 %collective-permute-start.6 = (bf16[2,256,256]{2,1,0:T(8,128)(2,1)S(1)}, bf16[2,256,256]{2,1,0:T(8,128)(2,1)S(1)}, u32[]{:S(2)}, u32[]{:S(2)}) collective-permute-start(bf16[2,256,256]{2,1,0:T(8,128)(2,1)S(1)} %get-tuple-element.70), channel_id=1, source_target_pairs={{0,64},{64,0},{1,65},{65,1},{2,66},{66,2},{3,67},{67,3},{4,68},{68... | collective-permute-start | bytes 786440 | tf_op jit(solution)/shard_map/ppermute | solution.py:430
  28.5 1.7 %collective-permute-start.5 = (bf16[2,256,256]{2,1,0:T(8,128)(2,1)S(1)}, bf16[2,256,256]{2,1,0:T(8,128)(2,1)S(1)}, u32[]{:S(2)}, u32[]{:S(2)}) collective-permute-start(bf16[2,256,256]{2,1,0:T(8,128)(2,1)S(1)} %get-tuple-element.67), channel_id=1, source_target_pairs={{0,64},{64,0},{1,65},{65,1},{2,66},{66,2},{3,67},{67,3},{4,68},{68... | collective-permute-start | bytes 786440 | tf_op jit(solution)/shard_map/ppermute | solution.py:430

commit v7 on v6

--- a/solution.py
+++ b/solution.py
@@ -13,7 +13,7 @@
 SPAN = W + STEP
 LS = 16
 RS = 4
-EARLY = 32
+EARLY = 48
 EDGE = W - 8
 BF = jnp.bfloat16
 F32 = jnp.float32

time: 31.3 us -> 31.4 us (level)
    ppermute x2, waiting for transfers between devices: 5.18 us -> 5.54 us  [to_right(): return lax.ppermute(x, 'tile', [(i, (i + 1) % tiles) for i in range(tiles)])]
where the time goes in v7:
time: 31.4 us; the launch traced here: 31.2 us
  Pallas kernels  14.6 us (46%)
  starting transfers between devices  7.99 us (25%)
  waiting for transfers between devices  7.71 us (25%)
  between operations  0.85 us (3%)
    pallas_call x11, Pallas kernels, call(): pl.pallas_call(body, name=name, out_shape=[jax.ShapeDtypeStruct(shape, ki...  14.6 us
    ppermute x2, waiting for transfers between devices, to_right(): return lax.ppermute(x, 'tile', [(i, (i + 1) % tiles) for i in range(tiles)])  5.54 us
    ppermute x3, starting transfers between devices, to_other(): return lax.ppermute(x, 'depth', [(0, 1), (1, 0)])  2.63 us
    ppermute x2, starting transfers between devices, to_right(): return lax.ppermute(x, 'tile', [(i, (i + 1) % tiles) for i in range(tiles)])  2.38 us
    ppermute x1, waiting for transfers between devices, to_right_other(): return lax.ppermute(x, ('depth', 'tile'), pairs)  2.16 us
    ppermute x1, starting transfers between devices, to_left(): return lax.ppermute(x, 'tile', [(i, (i - 1) % tiles) for i in range(tiles)])  1.52 us
    ppermute x1, starting transfers between devices, to_right_other(): return lax.ppermute(x, ('depth', 'tile'), pairs)  1.46 us
  transfers between devices with their start and end apart: 7, of which 3 were waited for; matrix products, arithmetic and copies ran while one was open for 0% of the time, Pallas kernels for 44%

profile of v7, /device:TPU:1, one launch (start us, length us, event | category | flops | bytes accessed | tf_op | source)
XLA Modules:
  0.0 31.2 jit_solution(7391750689105137058)
XLA Ops:
  0.0 0.0 copy-start.3
  0.0 0.0 copy-start.4
  0.0 0.0 copy-start.5
  0.0 0.0 copy-start.2
  0.0 1.5 %collective-permute-start = (bf16[1,2,2048,256]{3,2,1,0:T(8,128)(2,1)}, bf16[1,2,2048,256]{3,2,1,0:T(8,128)(2,1)S(1)}, u32[]{:S(2)}, u32[]{:S(2)}) collective-permute-start(bf16[1,2,2048,256]{3,2,1,0:T(8,128)(2,1)} %refs_0_.5), channel_id=1, source_target_pairs={{0,64},{64,0},{1,65},{65,1},{2,66},{66,2},{3,67},{67,3},{4,68},{68... | collective-permute-start | bytes 6291464 | tf_op jit(solution)/shard_map/ppermute | solution.py:430
  1.5 2.2 %edges.1 = (bf16[80,128]{1,0:T(8,128)(2,1)}, bf16[240,256]{1,0:T(8,128)(2,1)}) custom-call(s32[1,2]{1,0:T(1,128)} %refs_0_.4, s32[1,2]{1,0:T(1,128)} %refs_1_.6, f32[5]{0:T(128)} %refs_2_.3, bf16[1,2,2048,256]{3,2,1,0:T(8,128)(2,1)} %refs_0_.5, bf16[1,2,256,256]{3,2,1,0:T(8,128)(2,1)} %refs_4_.2), custom_call_target="tpu_custom_call" | custom-call | flops 1000000000 | bytes 143360 | tf_op jit(solution)/shard_map/edges/pallas_call | solution.py:395
  3.7 0.0 copy-start.7
  3.7 0.0 copy-start.1
  3.7 1.4 %collective-permute-start.1 = (bf16[80,128]{1,0:T(8,128)(2,1)}, bf16[80,128]{1,0:T(8,128)(2,1)S(1)}, u32[]{:S(2)}, u32[]{:S(2)}) collective-permute-start(bf16[80,128]{1,0:T(8,128)(2,1)} %get-tuple-element.39.refs_0_), channel_id=1, source_target_pairs={{0,1},{1,2},{2,3},{3,4},{4,5},{5,6},{6,7},{7,8},{8,9},{9,10},{10,1... | collective-permute-start | bytes 61448 | tf_op jit(solution)/shard_map/ppermute | solution.py:420
  5.1 1.5 %collective-permute-start.2 = (bf16[240,256]{1,0:T(8,128)(2,1)}, bf16[240,256]{1,0:T(8,128)(2,1)S(1)}, u32[]{:S(2)}, u32[]{:S(2)}) collective-permute-start(bf16[240,256]{1,0:T(8,128)(2,1)} %get-tuple-element.45), channel_id=1, source_target_pairs={{0,65},{1,66},{2,67},{3,68},{4,69},{5,70},{6,71},{7,72},{8,73},{9,... | collective-permute-start | bytes 368648 | tf_op jit(solution)/shard_map/ppermute | solution.py:427
  7.2 0.0 copy-done.3
  7.2 0.0 copy-done.4
  7.3 0.0 copy-done.5
  7.3 0.0 copy-done.2
  7.3 1.6 %settle.1 = (bf16[2,256,256]{2,1,0:T(8,128)(2,1)S(1)}, f32[2,256,256]{2,1,0:T(8,128)S(1)}, bf16[256,256]{1,0:T(8,128)(2,1)S(1)}, bf16[256,256]{1,0:T(8,128)(2,1)S(1)}) custom-call(s32[1,2]{1,0:T(1,128)S(1)} %copy-done.3, s32[1,2]{1,0:T(1,128)S(1)} %copy-done.4, f32[5]{0:T(128)S(1)} %copy-done.5, bf16[1,2,2048,256]{3,2,1,0:T(8,128)(2,1)} %refs_0_.5, ...), custom_call_target="tpu_custom_call" | custom-call | flops 1000000000 | bytes 1572864 | tf_op jit(solution)/shard_map/settle/pallas_call | solution.py:395
  8.8 0.0 copy-done.7
  8.9 0.0 collective-permute-done.refs_4_.refs_1_
  8.9 0.0 copy-done.1
  8.9 0.9 %left_forward.1 = (bf16[1136,128]{1,0:T(8,128)(2,1)S(1)}, bf16[2,256,256]{2,1,0:T(8,128)(2,1)S(1)}, bf16[2,256,256]{2,1,0:T(8,128)(2,1)S(1)}, f32[8,128]{1,0:T(8,128)S(1)}) custom-call(bf16[80,128]{1,0:T(8,128)(2,1)S(1)} %copy-done.1, f32[16,128]{1,0:T(8,128)S(1)} %broadcast_in_dim.3.refs_1_, bf16[256,256]{1,0:T(8,128)(2,1)S(1)} %dynamic-slice_bitcast_fusion.refs_2_, ...), custom_call_target="tpu_custom_call" | custom-call | flops 1000000000 | bytes 4124672 | tf_op jit(solution)/shard_map/left_forward/pallas_call | solution.py:395
  9.8 0.0 copy-start
  9.8 1.0 %collective-permute-start.4 = (bf16[1136,128]{1,0:T(8,128)(2,1)S(1)}, bf16[1136,128]{1,0:T(8,128)(2,1)S(1)}, u32[]{:S(2)}, u32[]{:S(2)}) collective-permute-start(bf16[1136,128]{1,0:T(8,128)(2,1)S(1)} %get-tuple-element.44.refs_0_), channel_id=1, source_target_pairs={{0,1},{1,2},{2,3},{3,4},{4,5},{5,6},{6,7},{7,8},{8,9},{9,10},{10,1... | collective-permute-start | bytes 872456 | tf_op jit(solution)/shard_map/ppermute | solution.py:420
  10.8 2.9 %collective-permute-done.1.refs_0_.refs_2_.refs_1_ = bf16[80,128]{1,0:T(8,128)(2,1)S(1)} collective-permute-done((bf16[80,128]{1,0:T(8,128)(2,1)}, bf16[80,128]{1,0:T(8,128)(2,1)S(1)}, u32[]{:S(2)}, u32[]{:S(2)}) %collective-permute-start.1) | collective-permute-done | bytes 20512 | tf_op jit(solution)/shard_map/ppermute | solution.py:420
  13.7 0.7 %settle_left.1 = (f32[2,256,256]{2,1,0:T(8,128)S(1)}, bf16[256,256]{1,0:T(8,128)(2,1)S(1)}, bf16[256,256]{1,0:T(8,128)(2,1)S(1)}) custom-call(bf16[80,128]{1,0:T(8,128)(2,1)S(1)} %collective-permute-done.1.refs_0_.refs_2_.refs_1_, f32[2,256,256]{2,1,0:T(8,128)S(1)} %copy-done.2, f32[8,128]{1,0:T(8,128)S(1)} %get-tuple-element.46.refs_2_), custom_call_target="tpu_custom_call" | custom-call | flops 1000000000 | bytes 1331200 | tf_op jit(solution)/shard_map/settle_left/pallas_call | solution.py:395
  14.4 2.2 %collective-permute-done.2.refs_3_.refs_2_ = bf16[240,256]{1,0:T(8,128)(2,1)S(1)} collective-permute-done((bf16[240,256]{1,0:T(8,128)(2,1)}, bf16[240,256]{1,0:T(8,128)(2,1)S(1)}, u32[]{:S(2)}, u32[]{:S(2)}) %collective-permute-start.2) | collective-permute-done | bytes 122912 | tf_op jit(solution)/shard_map/ppermute | solution.py:427
  16.6 0.0 copy-done
  16.6 0.0 copy-start.6
  16.6 0.9 %right_forward.1 = (bf16[1056,128]{1,0:T(8,128)(2,1)S(1)}, bf16[2,256,256]{2,1,0:T(8,128)(2,1)S(1)}, bf16[2,256,256]{2,1,0:T(8,128)(2,1)S(1)}, f32[8,128]{1,0:T(8,128)S(1)}) custom-call(bf16[1,2,2048,256]{3,2,1,0:T(8,128)(2,1)S(1)} %copy-done, bf16[1,2,2048,256]{3,2,1,0:T(8,128)(2,1)S(1)} %collective-permute-done.refs_4_.refs_1_, ...), custom_call_target="tpu_custom_call" | custom-call | flops 1000000000 | bytes 5922816 | tf_op jit(solution)/shard_map/right_forward/pallas_call | solution.py:395
  17.5 1.5 %collective-permute-start.3 = (bf16[1056,128]{1,0:T(8,128)(2,1)S(1)}, bf16[1056,128]{1,0:T(8,128)(2,1)S(1)}, u32[]{:S(2)}, u32[]{:S(2)}) collective-permute-start(bf16[1056,128]{1,0:T(8,128)(2,1)S(1)} %get-tuple-element.50.refs_1_), channel_id=1, source_target_pairs={{0,63},{1,0},{2,1},{3,2},{4,3},{5,4},{6,5},{7,6},{8,7},{9,8},{10,9... | collective-permute-start | bytes 811016 | tf_op jit(solution)/shard_map/ppermute | solution.py:423
  19.0 0.0 copy-done.6
  19.0 1.0 %tables_left.1 = (bf16[512,512]{1,0:T(8,128)(2,1)S(1)}, bf16[512,512]{1,0:T(8,128)(2,1)S(1)}, bf16[512,512]{1,0:T(8,128)(2,1)S(1)}, bf16[512,512]{1,0:T(8,128)(2,1)S(1)}, f32[8,128]{1,0:T(8,128)S(1)}) custom-call(bf16[80,128]{1,0:T(8,128)(2,1)S(1)} %collective-permute-done.1.refs_0_.refs_2_.refs_1_, bf16[512,256]{1,0:T(8,128)(2,1)S(1)} %copy-done.6, ...), custom_call_target="tpu_custom_call" | custom-call | flops 1000000000 | bytes 2646016 | tf_op jit(solution)/shard_map/tables_left/pallas_call | solution.py:395
  20.0 1.0 %tables.1 = (bf16[512,512]{1,0:T(8,128)(2,1)S(1)}, bf16[512,512]{1,0:T(8,128)(2,1)S(1)}, bf16[512,512]{1,0:T(8,128)(2,1)S(1)}, bf16[512,512]{1,0:T(8,128)(2,1)S(1)}, f32[8,128]{1,0:T(8,128)S(1)}) custom-call(bf16[80,128]{1,0:T(8,128)(2,1)S(1)} %copy-done.1, bf16[512,256]{1,0:T(8,128)(2,1)S(1)} %copy-done.6, ...), custom_call_target="tpu_custom_call" | custom-call | flops 1000000000 | bytes 2646016 | tf_op jit(solution)/shard_map/tables/pallas_call | solution.py:395
  21.0 2.6 %collective-permute-done.4.refs_0_ = bf16[1136,128]{1,0:T(8,128)(2,1)S(1)} collective-permute-done((bf16[1136,128]{1,0:T(8,128)(2,1)S(1)}, bf16[1136,128]{1,0:T(8,128)(2,1)S(1)}, u32[]{:S(2)}, u32[]{:S(2)}) %collective-permute-start.4) | collective-permute-done | bytes 290848 | tf_op jit(solution)/shard_map/ppermute | solution.py:420
  23.7 2.0 %far_field_1.1 = (bf16[2,256,256]{2,1,0:T(8,128)(2,1)S(1)}, bf16[2,256,256]{2,1,0:T(8,128)(2,1)S(1)}, f32[8,128]{1,0:T(8,128)S(1)}) custom-call(bf16[1136,128]{1,0:T(8,128)(2,1)S(1)} %collective-permute-done.4.refs_0_, bf16[1056,128]{1,0:T(8,128)(2,1)S(1)} %get-tuple-element.50.refs_1_, bf16[240,256]{1,0:T(8,128)(2,1)S(1)} %collective-permute-done.2.refs_3_.refs_2_, ...), custom_call_target="tpu_custom_call" | custom-call | flops 1000000000 | bytes 4620288 | tf_op jit(solution)/shard_map/far_field_1/pallas_call | solution.py:395
  25.6 1.0 %collective-permute-start.6 = (bf16[2,256,256]{2,1,0:T(8,128)(2,1)S(1)}, bf16[2,256,256]{2,1,0:T(8,128)(2,1)S(1)}, u32[]{:S(2)}, u32[]{:S(2)}) collective-permute-start(bf16[2,256,256]{2,1,0:T(8,128)(2,1)S(1)} %get-tuple-element.70), channel_id=1, source_target_pairs={{0,64},{64,0},{1,65},{65,1},{2,66},{66,2},{3,67},{67,3},{4,68},{68... | collective-permute-start | bytes 786440 | tf_op jit(solution)/shard_map/ppermute | solution.py:430
  26.7 0.0 collective-permute-done.3.refs_1_
  26.7 2.0 %far_field_0.1 = (bf16[2,256,256]{2,1,0:T(8,128)(2,1)S(1)}, bf16[2,256,256]{2,1,0:T(8,128)(2,1)S(1)}) custom-call(bf16[1136,128]{1,0:T(8,128)(2,1)S(1)} %get-tuple-element.44.refs_0_, bf16[1056,128]{1,0:T(8,128)(2,1)S(1)} %collective-permute-done.3.refs_1_, bf16[256,256]{1,0:T(8,128)(2,1)S(1)} %dynamic-slice_bitcast_fusion.refs_2_, ...), custom_call_target="tpu_custom_call" | custom-call | flops 1000000000 | bytes 4624384 | tf_op jit(solution)/shard_map/far_field_0/pallas_call | solution.py:395
  28.7 0.1 collective-permute-start.5
  28.8 0.0 collective-permute-done.6.refs_4_
  28.8 1.5 %lay_out.1 = (bf16[1,2,2048,256]{3,2,1,0:T(8,128)(2,1)}, bf16[2,2048,256]{2,1,0:T(8,128)(2,1)S(1)}) custom-call(bf16[80,128]{1,0:T(8,128)(2,1)S(1)} %copy-done.1, bf16[80,128]{1,0:T(8,128)(2,1)S(1)} %collective-permute-done.1.refs_0_.refs_2_.refs_1_, bf16[2,256,256]{2,1,0:T(8,128)(2,1)S(1)} %get-tuple-element.68.refs_2_, ...), custom_call_target="tpu_custom_call" | custom-call | flops 1000000000 | bytes 5021696 | tf_op jit(solution)/shard_map/lay_out/pallas_call | solution.py:395
  30.3 0.0 collective-permute-done.5.refs_1_
  30.3 0.9 %finish.1 = bf16[1,2,2048,256]{3,2,1,0:T(8,128)(2,1)} custom-call(bf16[80,128]{1,0:T(8,128)(2,1)S(1)} %copy-done.1, bf16[2,256,256]{2,1,0:T(8,128)(2,1)S(1)} %collective-permute-done.5.refs_1_, bf16[2,2048,256]{2,1,0:T(8,128)(2,1)S(1)} %get-tuple-element.71.refs_2_, bf16[1,2,2048,256]{3,2,1,0:T(8,128)(2,1)} %get-tuple-element.72.refs_3_), custom_call_target="tpu_custom_call", output_to_operand_aliasing={{}: (3, {})} | custom-call | flops 1000000000 | bytes 4476928 | tf_op jit(solution)/shard_map/finish/pallas_call | solution.py:395
  (2 shorter events, 0.0 us)
Async XLA Ops:
  0.0 7.2 %copy-start.3 = (s32[1,2]{1,0:T(1,128)S(1)}, s32[1,2]{1,0:T(1,128)}, u32[]{:S(2)}) copy-start(s32[1,2]{1,0:T(1,128)} %refs_0_.4) | copy-start | bytes 28
  0.0 7.2 %copy-start.4 = (s32[1,2]{1,0:T(1,128)S(1)}, s32[1,2]{1,0:T(1,128)}, u32[]{:S(2)}) copy-start(s32[1,2]{1,0:T(1,128)} %refs_1_.6) | copy-start | bytes 28
  0.0 7.2 %copy-start.5 = (f32[5]{0:T(128)S(1)}, f32[5]{0:T(128)}, u32[]{:S(2)}) copy-start(f32[5]{0:T(128)} %refs_2_.3) | copy-start | bytes 64
  0.0 7.3 %copy-start.2 = (f32[2,256,256]{2,1,0:T(8,128)S(1)}, f32[2,256,256]{2,1,0:T(8,128)}, u32[]{:S(2)}) copy-start(f32[2,256,256]{2,1,0:T(8,128)} %refs_1_.7) | copy-start | bytes 1572868
  0.0 8.9 %collective-permute-start = (bf16[1,2,2048,256]{3,2,1,0:T(8,128)(2,1)}, bf16[1,2,2048,256]{3,2,1,0:T(8,128)(2,1)S(1)}, u32[]{:S(2)}, u32[]{:S(2)}) collective-permute-start(bf16[1,2,2048,256]{3,2,1,0:T(8,128)(2,1)} %refs_0_.5), channel_id=1, source_target_pairs={{0,64},{64,0},{1,65},{65,1},{2,66},{66,2},{3,67},{67,3},{4,68},{68... | collective-permute-start | bytes 6291464 | tf_op jit(solution)/shard_map/ppermute | solution.py:430
  3.7 5.1 %copy-start.7 = (bf16[1,2,256,256]{3,2,1,0:T(8,128)(2,1)S(1)}, bf16[1,2,256,256]{3,2,1,0:T(8,128)(2,1)}, u32[]{:S(2)}) copy-start(bf16[1,2,256,256]{3,2,1,0:T(8,128)(2,1)} %refs_4_.2) | copy-start | bytes 786436
  3.7 5.2 %copy-start.1 = (bf16[80,128]{1,0:T(8,128)(2,1)S(1)}, bf16[80,128]{1,0:T(8,128)(2,1)}, u32[]{:S(2)}) copy-start(bf16[80,128]{1,0:T(8,128)(2,1)} %get-tuple-element.39.refs_0_) | copy-start | bytes 61444
  3.7 10.0 %collective-permute-start.1 = (bf16[80,128]{1,0:T(8,128)(2,1)}, bf16[80,128]{1,0:T(8,128)(2,1)S(1)}, u32[]{:S(2)}, u32[]{:S(2)}) collective-permute-start(bf16[80,128]{1,0:T(8,128)(2,1)} %get-tuple-element.39.refs_0_), channel_id=1, source_target_pairs={{0,1},{1,2},{2,3},{3,4},{4,5},{5,6},{6,7},{7,8},{8,9},{9,10},{10,1... | collective-permute-start | bytes 61448 | tf_op jit(solution)/shard_map/ppermute | solution.py:420
  5.1 11.4 %collective-permute-start.2 = (bf16[240,256]{1,0:T(8,128)(2,1)}, bf16[240,256]{1,0:T(8,128)(2,1)S(1)}, u32[]{:S(2)}, u32[]{:S(2)}) collective-permute-start(bf16[240,256]{1,0:T(8,128)(2,1)} %get-tuple-element.45), channel_id=1, source_target_pairs={{0,65},{1,66},{2,67},{3,68},{4,69},{5,70},{6,71},{7,72},{8,73},{9,... | collective-permute-start | bytes 368648 | tf_op jit(solution)/shard_map/ppermute | solution.py:427
  9.8 6.8 %copy-start = (bf16[1,2,2048,256]{3,2,1,0:T(8,128)(2,1)S(1)}, bf16[1,2,2048,256]{3,2,1,0:T(8,128)(2,1)}, u32[]{:S(2)}) copy-start(bf16[1,2,2048,256]{3,2,1,0:T(8,128)(2,1)} %refs_0_.5) | copy-start | bytes 6291460
  9.8 13.9 %collective-permute-start.4 = (bf16[1136,128]{1,0:T(8,128)(2,1)S(1)}, bf16[1136,128]{1,0:T(8,128)(2,1)S(1)}, u32[]{:S(2)}, u32[]{:S(2)}) collective-permute-start(bf16[1136,128]{1,0:T(8,128)(2,1)S(1)} %get-tuple-element.44.refs_0_), channel_id=1, source_target_pairs={{0,1},{1,2},{2,3},{3,4},{4,5},{5,6},{6,7},{7,8},{8,9},{9,10},{10,1... | collective-permute-start | bytes 872456 | tf_op jit(solution)/shard_map/ppermute | solution.py:420
  16.6 2.4 %copy-start.6 = (bf16[512,256]{1,0:T(8,128)(2,1)S(1)}, bf16[512,256]{1,0:T(8,128)(2,1)}, u32[]{:S(2)}) copy-start(bf16[512,256]{1,0:T(8,128)(2,1)} %constant.15.clone.refs_1_) | copy-start | bytes 786436
  17.5 9.2 %collective-permute-start.3 = (bf16[1056,128]{1,0:T(8,128)(2,1)S(1)}, bf16[1056,128]{1,0:T(8,128)(2,1)S(1)}, u32[]{:S(2)}, u32[]{:S(2)}) collective-permute-start(bf16[1056,128]{1,0:T(8,128)(2,1)S(1)} %get-tuple-element.50.refs_1_), channel_id=1, source_target_pairs={{0,63},{1,0},{2,1},{3,2},{4,3},{5,4},{6,5},{7,6},{8,7},{9,8},{10,9... | collective-permute-start | bytes 811016 | tf_op jit(solution)/shard_map/ppermute | solution.py:423
  25.6 3.2 %collective-permute-start.6 = (bf16[2,256,256]{2,1,0:T(8,128)(2,1)S(1)}, bf16[2,256,256]{2,1,0:T(8,128)(2,1)S(1)}, u32[]{:S(2)}, u32[]{:S(2)}) collective-permute-start(bf16[2,256,256]{2,1,0:T(8,128)(2,1)S(1)} %get-tuple-element.70), channel_id=1, source_target_pairs={{0,64},{64,0},{1,65},{65,1},{2,66},{66,2},{3,67},{67,3},{4,68},{68... | collective-permute-start | bytes 786440 | tf_op jit(solution)/shard_map/ppermute | solution.py:430
  28.7 1.6 %collective-permute-start.5 = (bf16[2,256,256]{2,1,0:T(8,128)(2,1)S(1)}, bf16[2,256,256]{2,1,0:T(8,128)(2,1)S(1)}, u32[]{:S(2)}, u32[]{:S(2)}) collective-permute-start(bf16[2,256,256]{2,1,0:T(8,128)(2,1)S(1)} %get-tuple-element.67), channel_id=1, source_target_pairs={{0,64},{64,0},{1,65},{65,1},{2,66},{66,2},{3,67},{67,3},{4,68},{68... | collective-permute-start | bytes 786440 | tf_op jit(solution)/shard_map/ppermute | solution.py:430
